TPU v7x, 256 devices: a whole 4x4x8 slice. The times are simulated.
256 devices in a mesh: attn: 32 (over z, x), tp: 8 (over y, core).
Axes of the slice: x: 4, y: 4, z: 8, core: 2. Of those that a mesh axis runs over, the one named last changes fastest.
Arguments:
- hidden: bfloat16 [32, 2, 8192], P(None, None, 'attn'), may hold values from -40 to 40
- lengths: int32 [32], replicated, may hold values from 2048 to 4096, as said below
- slot_of: int32 [32], replicated, may hold values from 0 to 63, as said below
- kv_cache: bfloat16 [64, 2, 4096, 1024], P('attn', None, None, 'tp'), may hold values from -300 to 300
- attn_gain: float32 [8192], P('attn'), may hold values from 0.1 to 1.9
- w_query: bfloat16 [8192, 8192], P('attn', 'tp'), may hold values from -0.06629126 to 0.06629126
- key_matrix: bfloat16 [8192, 1024], P('attn', 'tp'), may hold values from -0.22097087 to 0.22097087
- value_matrix: bfloat16 [8192, 1024], P('attn', 'tp'), may hold values from -0.0625 to 0.0625
- w_attn_out: bfloat16 [8192, 8192], P('tp', 'attn'), may hold values from -0.1875 to 0.1875
- mamba_gain: float32 [8192], P('attn'), may hold values from 0.1 to 1.9
- w_mamba_in: bfloat16 [8192, 8, 4608], P('attn', 'tp'), may hold values from -0.0625 to 0.0625
- w_mamba_dt: bfloat16 [8192, 256], P('attn', 'tp'), may hold values from -0.0625 to 0.0625
- w_mamba_out: bfloat16 [16384, 8192], P('tp', 'attn'), may hold values from -0.046875 to 0.046875
- conv_weight: float32 [4, 8, 2560], P(None, 'tp'), may hold values from -3 to 3
- conv_bias: float32 [8, 2560], P('tp'), may hold values from -0.5 to 0.5
- conv_state: float32 [32, 3, 8, 2560], P('attn', None, 'tp'), may hold values from -6 to 6
- ssm_state: float32 [32, 256, 64, 256], P('attn', 'tp'), may hold values from -6 to 6
- a_log: float32 [256], P('tp'), may hold values from -3.9 to 0.7
- dt_bias: float32 [256], P('tp'), may hold values from -2 to 1
- skip_gain: float32 [256], P('tp'), may hold values from 0.25 to 12
- group_gain: float32 [8, 2048], P('tp'), may hold values from 0.1 to 1.9
- mlp_gain: float32 [8192], P('attn'), may hold values from 0.1 to 1.9
- w_up: bfloat16 [8192, 16384], P('attn', 'tp'), may hold values from -0.0625 to 0.0625
- w_down: bfloat16 [16384, 8192], P('tp', 'attn'), may hold values from -0.046875 to 0.046875
Outputs:
- result: bfloat16 [32, 2, 8192], P(None, None, 'attn')
Inputs may be any that keep to these rules, and one draw needn't show every extreme that they name: `lengths`: cache positions below a request's length hold its earlier tokens; some request has exactly 4096. Request r is in slot slot_of[r] of kv_cache, held by attention device slot_of[r] // 2; no two requests share a slot; some device holds 2 requests, some none.
All inputs are finite; a program needn't handle non-finite values.
Results may differ from a plain program's by a relative error of at most 0.027.
Values may be sent and summed in bfloat16 or wider, within the bound.
No kernel may reach another device: no remote copies, remote signals or barrier semaphores. Data moves between devices by JAX's collectives and lax.ppermute only.
A program may use at most 64 MiB of HBM per device.

v0:
```python
import jax
import jax.numpy as jnp
from jax import lax
from jax.sharding import PartitionSpec as P

HEAD_SIZE = 128


EPS = 1e-05
MASKED = -1e30
SQUARE_COLUMNS = 128


def shortened(x):

    def short(part):
        return part.astype(jnp.bfloat16) if part.dtype == jnp.float32 else part

    return jax.tree.map(short, x)


def local_squares(values):
    widened = values.astype(jnp.float32)
    return jnp.sum(widened * widened, axis=-1)


def scale_from(squares, layer_width):
    return lax.rsqrt(squares / layer_width + EPS)


def square_block(squares):
    return jnp.broadcast_to(squares[..., None], squares.shape + (SQUARE_COLUMNS,))


def gained(values, gain):
    return (values.astype(jnp.float32) * gain).astype(jnp.bfloat16)


def tp_sum(values):
    return lax.psum(values, "tp")


def attend(query, new_keys, new_values, cache, length):
    steps = query.shape[0]
    kv_local = new_keys.shape[1] // HEAD_SIZE
    group = query.shape[1] // new_keys.shape[1]
    capacity = cache.shape[1]
    queries = query.reshape(steps, kv_local, group, HEAD_SIZE)
    old_keys = cache[0].reshape(capacity, kv_local, HEAD_SIZE)
    old_values = cache[1].reshape(capacity, kv_local, HEAD_SIZE)
    fresh_keys = new_keys.reshape(steps, kv_local, HEAD_SIZE)
    fresh_values = new_values.reshape(steps, kv_local, HEAD_SIZE)
    factor = HEAD_SIZE ** (-0.5)
    old_scores = (
        jnp.einsum("sngd,cnd->sngc", queries, old_keys, preferred_element_type=jnp.float32) * factor
    )
    positions = jnp.arange(capacity, dtype=jnp.int32)
    old_scores = jnp.where(positions < length, old_scores, MASKED)
    fresh_scores = (
        jnp.einsum("sngd,tnd->sngt", queries, fresh_keys, preferred_element_type=jnp.float32)
        * factor
    )
    later = jnp.arange(steps)[:, None] >= jnp.arange(steps)[None, :]
    fresh_scores = jnp.where(later[:, None, None, :], fresh_scores, MASKED)
    highest = jnp.maximum(old_scores.max(axis=-1), fresh_scores.max(axis=-1))
    old_weights = jnp.exp(old_scores - highest[..., None])
    fresh_weights = jnp.exp(fresh_scores - highest[..., None])
    total = old_weights.sum(axis=-1) + fresh_weights.sum(axis=-1)
    mixed = jnp.einsum(
        "sngc,cnd->sngd",
        old_weights.astype(jnp.bfloat16),
        old_values,
        preferred_element_type=jnp.float32,
    )
    mixed = mixed + jnp.einsum(
        "sngt,tnd->sngd",
        fresh_weights.astype(jnp.bfloat16),
        fresh_values,
        preferred_element_type=jnp.float32,
    )
    return (mixed / total[..., None]).reshape(steps, -1).astype(jnp.bfloat16)


def mamba_core(
    main_part,
    dt_raw,
    conv_prev,
    state,
    conv_weight,
    conv_bias,
    a_log,
    dt_bias,
    skip_gain,
    group_gain,
):
    steps, groups, _ = main_part.shape
    inner = group_gain.shape[1]
    heads = a_log.shape[0]
    per_group = heads // groups
    head_dim = inner // per_group
    states = state.shape[-1]
    state = state.reshape(groups, per_group, head_dim, states)
    gate = main_part[:, :, :inner]
    conv_in = main_part[:, :, inner:]
    window = jnp.concatenate([conv_prev, conv_in], axis=0)
    taps = conv_weight.shape[0]
    rates = jnp.exp(a_log).reshape(groups, per_group)
    step_size = jax.nn.softplus(dt_raw + dt_bias)
    skips = skip_gain.reshape(groups, per_group)
    outputs = []
    for position in range(steps):
        summed = conv_bias
        for tap_index in range(taps):
            summed = summed + conv_weight[tap_index] * window[position + tap_index]
        conved = jax.nn.silu(summed)
        inputs_x = conved[:, :inner].reshape(groups, per_group, head_dim)
        b_in = conved[:, inner : inner + states]
        c_out = conved[:, inner + states :]
        delta = step_size[position].reshape(groups, per_group)
        decay = jnp.exp(-delta * rates)
        state = (
            state * decay[:, :, None, None]
            + (delta[:, :, None] * inputs_x)[..., None] * b_in[:, None, None, :]
        )
        readout = jnp.sum(state * c_out[:, None, None, :], axis=-1) + skips[:, :, None] * inputs_x
        gated = readout.reshape(groups, inner) * jax.nn.silu(gate[position])
        normed = (
            gated * lax.rsqrt(jnp.mean(gated * gated, axis=-1, keepdims=True) + EPS) * group_gain
        )
        outputs.append(normed.reshape(-1))
    return jnp.stack(outputs).astype(jnp.bfloat16)


def squared_relu(values):
    lifted = jnp.maximum(values, 0.0)
    return (lifted * lifted).astype(jnp.bfloat16)


def on_device(
    hidden,
    lengths,
    slot_of,
    kv_cache,
    attn_gain,
    w_query,
    key_matrix,
    value_matrix,
    w_attn_out,
    mamba_gain,
    w_mamba_in,
    w_mamba_dt,
    w_mamba_out,
    conv_weight,
    conv_bias,
    conv_state,
    ssm_state,
    a_log,
    dt_bias,
    skip_gain,
    group_gain,
    mlp_gain,
    w_up,
    w_down,
):
    requests, steps, local_width = hidden.shape
    devices = lax.axis_size("attn")
    layer_width = local_width * devices
    slots = kv_cache.shape[0]
    total_slots = slots * devices
    position_here = lax.axis_index("attn")
    slot_numbers = jnp.arange(total_slots, dtype=jnp.int32)
    placed = slot_numbers[:, None] == slot_of[None, :]
    own_slots = lax.dynamic_slice_in_dim(placed, position_here * slots, slots, 0)
    slot_length = jnp.sum(jnp.where(own_slots, lengths[None, :], 0), axis=1)
    query_cols = w_query.shape[1]
    key_cols = key_matrix.shape[1]
    squares_attn = local_squares(hidden)
    normed_attn = gained(hidden, attn_gain)
    flat_rows = normed_attn.reshape(requests * steps, local_width)
    query_part = jnp.dot(flat_rows, w_query, preferred_element_type=jnp.float32).reshape(
        requests, steps, -1
    )
    key_part = jnp.dot(flat_rows, key_matrix, preferred_element_type=jnp.float32).reshape(
        requests, steps, -1
    )
    value_part = jnp.dot(flat_rows, value_matrix, preferred_element_type=jnp.float32).reshape(
        requests, steps, -1
    )
    summed = lax.psum((query_part, key_part, value_part, squares_attn), "attn")
    scale_attn = scale_from(summed[3], layer_width)
    joined = jnp.concatenate(summed[:3], axis=2) * scale_attn[..., None]
    projected = jnp.einsum(
        "jr,rsc->jsc", own_slots.astype(jnp.float32), joined, precision=lax.Precision.HIGHEST
    )
    projected = projected.astype(jnp.bfloat16)
    query = projected[..., :query_cols]
    new_keys = projected[..., query_cols : query_cols + key_cols]
    new_values = projected[..., query_cols + key_cols :]
    slot_outputs = jax.vmap(attend)(query, new_keys, new_values, kv_cache, slot_length)
    shard_piece = lax.all_gather(slot_outputs, "attn", axis=0, tiled=True)
    row_count = shard_piece.shape[0]
    flat_piece = shard_piece.reshape(row_count * steps, -1)
    slot_result = jnp.dot(flat_piece, w_attn_out, preferred_element_type=jnp.float32).reshape(
        row_count, steps, local_width
    )
    request_result = jnp.einsum(
        "jr,jsd->rsd", placed.astype(jnp.float32), slot_result, precision=lax.Precision.HIGHEST
    )
    first = (hidden.astype(jnp.float32) + tp_sum(request_result)).astype(jnp.bfloat16)
    squares_mix = local_squares(first)
    normed_mix = gained(first, mamba_gain)
    groups_local = w_mamba_in.shape[1]
    main_cols = groups_local * w_mamba_in.shape[2]
    mix_cols = main_cols + w_mamba_dt.shape[1]
    w_main = w_mamba_in.reshape(local_width, main_cols)
    own_rows = conv_state.shape[0]
    block = normed_mix.reshape(requests * steps, local_width)
    main_term = jnp.dot(block, w_main, preferred_element_type=jnp.float32)
    step_term = jnp.dot(block, w_mamba_dt, preferred_element_type=jnp.float32)
    block_squares = square_block(squares_mix).reshape(requests * steps, SQUARE_COLUMNS)
    every_terms = lax.psum(
        jnp.concatenate([main_term, step_term, block_squares], axis=1)
        .reshape(requests, steps, -1)
        .astype(jnp.bfloat16),
        "attn",
    ).astype(jnp.float32)
    own_terms = lax.dynamic_slice_in_dim(every_terms, position_here * own_rows, own_rows, 0)
    own_scale_mix = scale_from(own_terms[..., mix_cols], layer_width)
    own_terms = own_terms[..., :mix_cols] * own_scale_mix[..., None]
    main_part = own_terms[..., :main_cols].reshape(own_rows, steps, groups_local, -1)
    dt_raw = own_terms[..., main_cols:]

    def one_request(one_main, one_dt, one_conv, one_state):
        return mamba_core(
            one_main,
            one_dt,
            one_conv,
            one_state,
            conv_weight,
            conv_bias,
            a_log,
            dt_bias,
            skip_gain,
            group_gain,
        )

    mixer = jax.vmap(one_request)(main_part, dt_raw, conv_state, ssm_state)
    shard_piece = lax.all_gather(shortened(mixer), "attn", axis=0, tiled=True)
    row_count = shard_piece.shape[0]
    flat_piece = shard_piece.reshape(row_count * steps, -1)
    mixed_result = jnp.dot(flat_piece, w_mamba_out, preferred_element_type=jnp.float32).reshape(
        row_count, steps, local_width
    )
    second = (first.astype(jnp.float32) + tp_sum(mixed_result)).astype(jnp.bfloat16)
    squares_ff = local_squares(second)
    normed_ff = gained(second, mlp_gain)
    flat_ff = normed_ff.reshape(requests * steps, local_width)
    up_local = jnp.dot(flat_ff, w_up, preferred_element_type=jnp.float32).reshape(
        requests, steps, -1
    )
    up_every, squares_every = (
        lax.psum(up_local.astype(jnp.bfloat16), "attn").astype(jnp.float32),
        lax.psum(squares_ff.astype(jnp.bfloat16), "attn").astype(jnp.float32),
    )
    scale_ff = scale_from(squares_every, layer_width)
    active = squared_relu(up_every * scale_ff[..., None])
    downward = jnp.dot(
        active.reshape(requests * steps, -1), w_down, preferred_element_type=jnp.float32
    ).reshape(requests, steps, local_width)
    return (second.astype(jnp.float32) + tp_sum(downward)).astype(jnp.bfloat16)


def solution(mesh):
    in_specs = (
        P(None, None, "attn"),
        P(),
        P(),
        P("attn", None, None, "tp"),
        P("attn"),
        P("attn", "tp"),
        P("attn", "tp"),
        P("attn", "tp"),
        P("tp", "attn"),
        P("attn"),
        P("attn", "tp", None),
        P("attn", "tp"),
        P("tp", "attn"),
        P(None, "tp", None),
        P("tp", None),
        P("attn", None, "tp", None),
        P("attn", "tp", None, None),
        P("tp"),
        P("tp"),
        P("tp"),
        P("tp", None),
        P("attn"),
        P("attn", "tp"),
        P("tp", "attn"),
    )
    out_specs = P(None, None, "attn")
    return jax.shard_map(
        on_device, mesh=mesh, in_specs=in_specs, out_specs=out_specs, check_vma=False
    )
```

profile of v0, /device:TPU:1, one launch (start us, length us, event | category | flops | bytes accessed | tf_op | source)
XLA Modules:
  0.0 913.2 jit_solution(17144986190916837250)
XLA Ops:
  6.5 1.6 fusion.51
  8.1 1.6 fusion.59
  9.8 1.6 fusion.61
  11.4 2.0 fusion.34
  15.1 135.5 %all-reduce.21.cloned.1.call-done = (f32[32,2,128]{2,0,1:T(8,128)}, f32[32,2,128]{2,0,1:T(8,128)}, f32[32,2]{0,1:T(2,128)}) async-done(((f32[32,2,128]{2,0,1:T(8,128)}, f32[32,2,128]{2,0,1:T(8,128)}, f32[32,2]{0,1:T(2,128)}), (f32[32,2,128]{2,0,1:T(8,128)}, f32[32,2,128]{2,0,1:T(8,128)}, f32[32,2]{0,1:T(2,128)})) %all-reduce.21.cloned.1.call-update) | async-done | bytes 65808 | tf_op jit(solution)/shard_map/psum | solution.py:189
  151.2 145.4 %all-reduce.9.cloned.1.call-done = f32[32,2,1024]{2,0,1:T(8,128)} async-done(((f32[32,2,1024]{2,0,1:T(8,128)}), f32[32,2,1024]{2,0,1:T(8,128)}) %all-reduce.9.cloned.1.call-update) | async-done | bytes 262160 | tf_op jit(solution)/shard_map/psum | solution.py:189
  296.6 1.3 convolution_convert_fusion.2
  298.2 2.4 fusion.112
  301.1 2.1 fusion.24
  303.2 35.1 %all_gather.6 = bf16[64,2,1024]{2,1,0:T(2,128)(2,1)S(1)} all-gather(bf16[2,2,1024]{2,1,0:T(2,128)(2,1)S(1)} %convert_element_type.89), channel_id=1, replica_groups=mesh['attn'=32,'tp'=8] {'attn'}, dimensions={0}, use_global_device_ids=true | all-gather | bytes 270336 | tf_op jit(solution)/shard_map/all_gather | solution.py:200
  339.5 76.8 %all-reduce.11.cloned.1.call-done = f32[32,2,256]{2,0,1:T(8,128)} async-done(((f32[32,2,256]{2,0,1:T(8,128)}), f32[32,2,256]{2,0,1:T(8,128)}) %all-reduce.11.cloned.1.call-update) | async-done | bytes 65552 | tf_op jit(solution)/shard_map/psum | solution.py:40
  418.0 1.0 concatenate.19
  419.2 145.3 %all-reduce.13.cloned.1.call-done = bf16[32,2,4768]{2,0,1:T(8,128)(2,1)} async-done(((bf16[32,2,4768]{2,0,1:T(8,128)(2,1)}), bf16[32,2,4768]{2,0,1:T(8,128)(2,1)}) %all-reduce.13.cloned.1.call-update) | async-done | bytes 610320 | tf_op jit(solution)/shard_map/psum | solution.py:221
  567.9 1.4 reshape.436
  569.2 1.2 compare_select_fusion
  570.5 1.4 reshape.435
  574.1 3.4 multiply_reduce_fusion.1
  582.0 34.9 %all_gather.7 = bf16[32,2,2048]{2,1,0:T(2,128)(2,1)S(1)} all-gather(bf16[1,2,2048]{2,1,0:T(2,128)(2,1)S(1)} %pad_maximum_fusion), channel_id=1, replica_groups=mesh['attn'=32,'tp'=8] {'attn'}, dimensions={0}, use_global_device_ids=true | all-gather | bytes 270336 | tf_op jit(solution)/shard_map/all_gather | solution.py:248
  617.9 76.9 %all-reduce.15.cloned.1.call-done = f32[32,2,256]{2,0,1:T(8,128)} async-done(((f32[32,2,256]{2,0,1:T(8,128)}), f32[32,2,256]{2,0,1:T(8,128)}) %all-reduce.15.cloned.1.call-update) | async-done | bytes 65552 | tf_op jit(solution)/shard_map/psum | solution.py:40
  695.8 2.2 convolution_convert_fusion.1
  698.1 61.2 %psum.78 = bf16[32,2]{0,1:T(2,128)(2,1)S(1)} all-reduce(bf16[32,2]{0,1:T(2,128)(2,1)S(1)} %get-tuple-element.10), channel_id=1, replica_groups=mesh['attn'=32,'tp'=8] {'attn'}, use_global_device_ids=true, to_apply=%region_20.21 | all-reduce | flops 64 | bytes 256 | tf_op jit(solution)/shard_map/psum | solution.py:263
  759.2 80.0 %all-reduce.17.cloned.1.call-done = bf16[32,2,2048]{2,0,1:T(8,128)(2,1)} async-done(((bf16[32,2,2048]{2,0,1:T(8,128)(2,1)}), bf16[32,2,2048]{2,0,1:T(8,128)(2,1)}) %all-reduce.17.cloned.1.call-update) | async-done | bytes 262160 | tf_op jit(solution)/shard_map/psum | solution.py:262
  839.2 2.3 fusion.27
  841.5 63.4 %all-reduce.19.cloned.1.call-done = f32[32,2,256]{2,0,1:T(8,128)} async-done(((f32[32,2,256]{2,0,1:T(8,128)}), f32[32,2,256]{2,0,1:T(8,128)}) %all-reduce.19.cloned.1.call-update) | async-done | bytes 65552 | tf_op jit(solution)/shard_map/psum | solution.py:40
  (76 shorter events, 18.3 us)
Async XLA Ops:
  6.5 410.7 %copy-start = (bf16[256,1,4608]{2,0,1:T(8,128)(2,1)S(1)}, bf16[256,1,4608]{2,0,1:T(8,128)(2,1)}, u32[]{:S(2)}) copy-start(bf16[256,1,4608]{2,0,1:T(8,128)(2,1)} %param.34) | copy-start | bytes 7077892
  6.5 144.0 %all-reduce.21.cloned.1.call-start = ((), (), s32[]{:S(2)}) async-start(), calls=%async_computation.6 | async-start | bytes 133120 | tf_op jit(solution)/shard_map/psum | solution.py:189
  11.4 285.2 %all-reduce.9.cloned.1.call-start = ((), (), s32[]{:S(2)}) async-start(), calls=%async_computation | async-start | bytes 524288 | tf_op jit(solution)/shard_map/psum | solution.py:189
  13.5 402.8 %all-reduce.11.cloned.1.call-start = ((), (), s32[]{:S(2)}) async-start(), calls=%async_computation.1 | async-start | bytes 131072 | tf_op jit(solution)/shard_map/psum | solution.py:40
  300.6 37.7 %copy-start.3 = (bf16[1024,256]{1,0:T(8,128)(2,1)S(1)}, bf16[1024,256]{1,0:T(8,128)(2,1)}, u32[]{:S(2)}) copy-start(bf16[1024,256]{1,0:T(8,128)(2,1)} %param.32) | copy-start | bytes 1572868
  300.7 37.9 %copy-start.6 = (s32[32]{0:T(128)S(1)}, s32[32]{0:T(128)}, u32[]{:S(2)}) copy-start(s32[32]{0:T(128)} %param.26) | copy-start | bytes 388
  300.9 115.4 %copy-start.2 = (bf16[32,2,256]{2,1,0:T(2,128)(2,1)S(1)}, bf16[32,2,256]{2,1,0:T(2,128)(2,1)}, u32[]{:S(2)}) copy-start(bf16[32,2,256]{2,1,0:T(2,128)(2,1)} %param.24) | copy-start | bytes 98308
  301.1 116.1 %copy-start.5 = (f32[256]{0:T(256)S(1)}, f32[256]{0:T(256)}, u32[]{:S(2)}) copy-start(f32[256]{0:T(256)} %param.33) | copy-start | bytes 3076
  338.3 79.5 %copy-start.4 = (bf16[256,32]{0,1:T(8,128)(2,1)S(1)}, bf16[256,32]{0,1:T(8,128)(2,1)}, u32[]{:S(2)}) copy-start(bf16[256,32]{0,1:T(8,128)(2,1)} %param.35) | copy-start | bytes 49156
  339.4 225.1 %all-reduce.13.cloned.1.call-start = ((), (), s32[]{:S(2)}) async-start(), calls=%async_computation.2 | async-start | bytes 1245184 | tf_op jit(solution)/shard_map/psum | solution.py:221
  417.2 1.8 copy-start.8
  419.0 197.9 %copy-start.1 = (bf16[2048,256]{1,0:T(8,128)(2,1)S(1)}, bf16[2048,256]{1,0:T(8,128)(2,1)}, u32[]{:S(2)}) copy-start(bf16[2048,256]{1,0:T(8,128)(2,1)} %param.36) | copy-start | bytes 3145732
  419.0 275.8 %all-reduce.15.cloned.1.call-start = ((), (), s32[]{:S(2)}) async-start(), calls=%async_computation.3 | async-start | bytes 131072 | tf_op jit(solution)/shard_map/psum | solution.py:40
  574.1 121.7 %copy-start.7 = (f32[256]{0:T(256)S(1)}, f32[256]{0:T(256)}, u32[]{:S(2)}) copy-start(f32[256]{0:T(256)} %param.45) | copy-start | bytes 3076
  617.8 221.4 %all-reduce.17.cloned.1.call-start = ((), (), s32[]{:S(2)}) async-start(), calls=%async_computation.4 | async-start | bytes 524288 | tf_op jit(solution)/shard_map/psum | solution.py:262
  698.0 206.9 %all-reduce.19.cloned.1.call-start = ((), (), s32[]{:S(2)}) async-start(), calls=%async_computation.5 | async-start | bytes 131072 | tf_op jit(solution)/shard_map/psum | solution.py:40
Sparse Core Ops, SparseCore 0:
  11.5 138.9 all-reduce.20
  154.0 142.6 all-reduce.8
  339.6 76.6 all-reduce.10
  419.9 144.5 all-reduce.12
  618.0 76.8 all-reduce.14
  698.5 140.6 all-reduce.16
  841.6 63.2 all-reduce.18
where the time goes:
time: 916 us; the launch traced here: 913 us
  waiting for transfers between devices  723 us (79%)
  blocking collectives  131 us (14%)
  matrix products  18.4 us (2%)
  other arithmetic  17.4 us (2%)
  between operations  15.1 us (2%)
    psum x2, waiting for transfers between devices, on_device(): summed = lax.psum((query_part, key_part, value_part, squares_attn), 'attn')  281 us
    psum x3, waiting for transfers between devices, tp_sum(): return lax.psum(values, 'tp')  217 us
    psum x1, waiting for transfers between devices, on_device(): lax.psum(jnp.concatenate([main_term, step_term, block_squares], axis=1).r...  145 us
    psum x1, waiting for transfers between devices, on_device(): lax.psum(up_local.astype(jnp.bfloat16), 'attn').astype(jnp.float32)  80 us
    psum x1, blocking collectives, on_device(): lax.psum(squares_ff.astype(jnp.bfloat16), 'attn').astype(jnp.float32)  61.2 us
    all_gather x1, blocking collectives, on_device(): shard_piece = lax.all_gather(slot_outputs, 'attn', axis=0, tiled=True)  35.1 us
    all_gather x1, blocking collectives, on_device(): shard_piece = lax.all_gather(shortened(mixer), 'attn', axis=0, tiled=True)  34.9 us
  transfers between devices with their start and end apart: 7, of which 7 were waited for; matrix products, arithmetic and copies ran while one was open for 0% of the time, Pallas kernels for 0%

commit v1 on v0

--- a/solution.py
+++ b/solution.py
@@ -11,14 +11,6 @@
 SQUARE_COLUMNS = 128
 
 
-def shortened(x):
-
-    def short(part):
-        return part.astype(jnp.bfloat16) if part.dtype == jnp.float32 else part
-
-    return jax.tree.map(short, x)
-
-
 def local_squares(values):
     widened = values.astype(jnp.float32)
     return jnp.sum(widened * widened, axis=-1)
@@ -28,16 +20,28 @@
     return lax.rsqrt(squares / layer_width + EPS)
 
 
-def square_block(squares):
-    return jnp.broadcast_to(squares[..., None], squares.shape + (SQUARE_COLUMNS,))
-
-
 def gained(values, gain):
     return (values.astype(jnp.float32) * gain).astype(jnp.bfloat16)
 
 
+def hi_lo(squares):
+    high = squares.astype(jnp.bfloat16)
+    low = (squares - high.astype(jnp.float32)).astype(jnp.bfloat16)
+    pair = jnp.stack([high, low], axis=-1)
+    return jnp.pad(pair, [(0, 0)] * (pair.ndim - 1) + [(0, SQUARE_COLUMNS - 2)])
+
+
+def spread(values, axis):
+    copies = jnp.broadcast_to(values[None], (lax.axis_size(axis),) + values.shape)
+    return lax.all_to_all(copies, axis, 0, 0)
+
+
+def gather_sum(values, axis):
+    return jnp.sum(lax.all_to_all(values, axis, 0, 0).astype(jnp.float32), axis=0)
+
+
 def tp_sum(values):
-    return lax.psum(values, "tp")
+    return jnp.sum(spread(values.astype(jnp.bfloat16), "tp").astype(jnp.float32), axis=0)
 
 
 def attend(query, new_keys, new_values, cache, length):
@@ -177,35 +181,35 @@
     squares_attn = local_squares(hidden)
     normed_attn = gained(hidden, attn_gain)
     flat_rows = normed_attn.reshape(requests * steps, local_width)
-    query_part = jnp.dot(flat_rows, w_query, preferred_element_type=jnp.float32).reshape(
-        requests, steps, -1
-    )
-    key_part = jnp.dot(flat_rows, key_matrix, preferred_element_type=jnp.float32).reshape(
-        requests, steps, -1
-    )
-    value_part = jnp.dot(flat_rows, value_matrix, preferred_element_type=jnp.float32).reshape(
-        requests, steps, -1
-    )
-    summed = lax.psum((query_part, key_part, value_part, squares_attn), "attn")
-    scale_attn = scale_from(summed[3], layer_width)
-    joined = jnp.concatenate(summed[:3], axis=2) * scale_attn[..., None]
-    projected = jnp.einsum(
-        "jr,rsc->jsc", own_slots.astype(jnp.float32), joined, precision=lax.Precision.HIGHEST
-    )
-    projected = projected.astype(jnp.bfloat16)
+    by_slot = jnp.einsum(
+        "jr,rsd->jsd", placed.astype(jnp.bfloat16), normed_attn,
+        preferred_element_type=jnp.float32,
+    ).astype(jnp.bfloat16).reshape(total_slots * steps, local_width)
+    squares_by_slot = jnp.einsum(
+        "jr,rs->js", placed.astype(jnp.float32), squares_attn, precision=lax.Precision.HIGHEST
+    ).reshape(total_slots * steps)
+    weights_in = jnp.concatenate([w_query, key_matrix, value_matrix], axis=1)
+    parts = jnp.dot(by_slot, weights_in, preferred_element_type=jnp.float32).astype(jnp.bfloat16)
+    parts = jnp.concatenate([parts, hi_lo(squares_by_slot)], axis=1)
+    summed = gather_sum(parts.reshape(devices, slots * steps, -1), "attn")
+    all_cols = query_cols + 2 * key_cols
+    scale_attn = scale_from(summed[:, all_cols] + summed[:, all_cols + 1], layer_width)
+    projected = (summed[:, :all_cols] * scale_attn[:, None]).astype(jnp.bfloat16)
+    projected = projected.reshape(slots, steps, all_cols)
     query = projected[..., :query_cols]
     new_keys = projected[..., query_cols : query_cols + key_cols]
     new_values = projected[..., query_cols + key_cols :]
     slot_outputs = jax.vmap(attend)(query, new_keys, new_values, kv_cache, slot_length)
-    shard_piece = lax.all_gather(slot_outputs, "attn", axis=0, tiled=True)
-    row_count = shard_piece.shape[0]
-    flat_piece = shard_piece.reshape(row_count * steps, -1)
-    slot_result = jnp.dot(flat_piece, w_attn_out, preferred_element_type=jnp.float32).reshape(
-        row_count, steps, local_width
-    )
-    request_result = jnp.einsum(
-        "jr,jsd->rsd", placed.astype(jnp.float32), slot_result, precision=lax.Precision.HIGHEST
-    )
+    every_slot = spread(slot_outputs.reshape(slots * steps, -1), "attn")
+    by_request = jnp.einsum(
+        "jr,jsd->rsd",
+        placed.astype(jnp.bfloat16),
+        every_slot.reshape(total_slots, steps, -1),
+        preferred_element_type=jnp.float32,
+    ).astype(jnp.bfloat16)
+    request_result = jnp.dot(
+        by_request.reshape(requests * steps, -1), w_attn_out, preferred_element_type=jnp.float32
+    ).reshape(requests, steps, local_width)
     first = (hidden.astype(jnp.float32) + tp_sum(request_result)).astype(jnp.bfloat16)
     squares_mix = local_squares(first)
     normed_mix = gained(first, mamba_gain)
@@ -217,16 +221,15 @@
     block = normed_mix.reshape(requests * steps, local_width)
     main_term = jnp.dot(block, w_main, preferred_element_type=jnp.float32)
     step_term = jnp.dot(block, w_mamba_dt, preferred_element_type=jnp.float32)
-    block_squares = square_block(squares_mix).reshape(requests * steps, SQUARE_COLUMNS)
-    every_terms = lax.psum(
-        jnp.concatenate([main_term, step_term, block_squares], axis=1)
-        .reshape(requests, steps, -1)
-        .astype(jnp.bfloat16),
-        "attn",
-    ).astype(jnp.float32)
-    own_terms = lax.dynamic_slice_in_dim(every_terms, position_here * own_rows, own_rows, 0)
-    own_scale_mix = scale_from(own_terms[..., mix_cols], layer_width)
-    own_terms = own_terms[..., :mix_cols] * own_scale_mix[..., None]
+    terms = jnp.concatenate(
+        [main_term.astype(jnp.bfloat16), step_term.astype(jnp.bfloat16),
+         hi_lo(squares_mix.reshape(requests * steps))[:, : SQUARE_COLUMNS - w_mamba_dt.shape[1]]],
+        axis=1,
+    )
+    own_rows = requests // devices
+    own_terms = gather_sum(terms.reshape(devices, own_rows * steps, -1), "attn")
+    own_scale_mix = scale_from(own_terms[:, mix_cols] + own_terms[:, mix_cols + 1], layer_width)
+    own_terms = (own_terms[:, :mix_cols] * own_scale_mix[:, None]).reshape(own_rows, steps, mix_cols)
     main_part = own_terms[..., :main_cols].reshape(own_rows, steps, groups_local, -1)
     dt_raw = own_terms[..., main_cols:]
 
@@ -245,25 +248,20 @@
         )
 
     mixer = jax.vmap(one_request)(main_part, dt_raw, conv_state, ssm_state)
-    shard_piece = lax.all_gather(shortened(mixer), "attn", axis=0, tiled=True)
-    row_count = shard_piece.shape[0]
-    flat_piece = shard_piece.reshape(row_count * steps, -1)
-    mixed_result = jnp.dot(flat_piece, w_mamba_out, preferred_element_type=jnp.float32).reshape(
-        row_count, steps, local_width
-    )
+    every_mixer = spread(mixer.reshape(own_rows * steps, -1), "attn")
+    mixed_result = jnp.dot(
+        every_mixer.reshape(requests * steps, -1), w_mamba_out, preferred_element_type=jnp.float32
+    ).reshape(requests, steps, local_width)
     second = (first.astype(jnp.float32) + tp_sum(mixed_result)).astype(jnp.bfloat16)
     squares_ff = local_squares(second)
     normed_ff = gained(second, mlp_gain)
     flat_ff = normed_ff.reshape(requests * steps, local_width)
-    up_local = jnp.dot(flat_ff, w_up, preferred_element_type=jnp.float32).reshape(
-        requests, steps, -1
-    )
-    up_every, squares_every = (
-        lax.psum(up_local.astype(jnp.bfloat16), "attn").astype(jnp.float32),
-        lax.psum(squares_ff.astype(jnp.bfloat16), "attn").astype(jnp.float32),
-    )
-    scale_ff = scale_from(squares_every, layer_width)
-    active = squared_relu(up_every * scale_ff[..., None])
+    up_local = jnp.dot(flat_ff, w_up, preferred_element_type=jnp.float32).astype(jnp.bfloat16)
+    up_cols = up_local.shape[1]
+    up_local = jnp.concatenate([up_local, hi_lo(squares_ff.reshape(requests * steps))], axis=1)
+    own_up = gather_sum(up_local.reshape(devices, own_rows * steps, -1), "attn")
+    scale_ff = scale_from(own_up[:, up_cols] + own_up[:, up_cols + 1], layer_width)
+    active = spread(squared_relu(own_up[:, :up_cols] * scale_ff[:, None]), "attn")
     downward = jnp.dot(
         active.reshape(requests * steps, -1), w_down, preferred_element_type=jnp.float32
     ).reshape(requests, steps, local_width)

time: 916 us -> 181 us (0.20)
  waiting for transfers between devices: 723 us -> 29.9 us
  blocking collectives: 131 us -> 99.9 us
  starting transfers between devices: 0.25 us -> 15.9 us
  between operations: 15.1 us -> 1.83 us
    psum x7 -> x0, waiting for transfers between devices: 723 us -> none  [the longest x2 281 us: on_device(): summed = lax.psum((query_part, key_part, value_part, squares_attn), 'attn')]
    all_to_all x0 -> x7, blocking collectives: none -> 99.9 us  [the longest x6 86.1 us: spread(): return lax.all_to_all(copies, axis, 0, 0)]
    all_gather x2 -> x0, blocking collectives: 70 us -> none  [the longest x1 35.1 us: on_device(): shard_piece = lax.all_gather(slot_outputs, 'attn', axis=0, tiled=True)]
    psum x1 -> x0, blocking collectives: 61.2 us -> none  [on_device(): lax.psum(squares_ff.astype(jnp.bfloat16), 'attn').astype(jnp.float32)]
    all_to_all x0 -> x2, waiting for transfers between devices: none -> 29.9 us  [gather_sum(): lax.all_to_all(values, axis, 0, 0).astype(jnp.float32)]
    all_to_all x0 -> x2, starting transfers between devices: none -> 15.9 us  [gather_sum(): lax.all_to_all(values, axis, 0, 0).astype(jnp.float32)]
  transfers between devices with their start and end apart: 7 -> 2, of which waited for: 7 -> 2; matrix products, arithmetic and copies ran while one was open for 0% -> 1% of each run, Pallas kernels for 0% -> 0%
where the time goes in v1:
time: 181 us; the launch traced here: 180 us
  blocking collectives  99.9 us (55%)
  waiting for transfers between devices  29.9 us (17%)
  starting transfers between devices  15.9 us (9%)
  matrix products  12.5 us (7%)
  other arithmetic  10.4 us (6%)
  local copies, waits for them, and re-layouts  9.59 us (5%)
  between operations  1.83 us (1%)
    all_to_all x6, blocking collectives, spread(): return lax.all_to_all(copies, axis, 0, 0)  86.1 us
    all_to_all x2, waiting for transfers between devices, gather_sum(): lax.all_to_all(values, axis, 0, 0).astype(jnp.float32)  29.9 us
    all_to_all x2, starting transfers between devices, gather_sum(): lax.all_to_all(values, axis, 0, 0).astype(jnp.float32)  15.9 us
    all_to_all x1, blocking collectives, gather_sum(): lax.all_to_all(values, axis, 0, 0).astype(jnp.float32)  13.8 us
  transfers between devices with their start and end apart: 2, of which 2 were waited for; matrix products, arithmetic and copies ran while one was open for 1% of the time, Pallas kernels for 0%

profile of v1, /device:TPU:1, one launch (start us, length us, event | category | flops | bytes accessed | tf_op | source)
XLA Modules:
  0.0 180.1 jit_solution(15477404963876223284)
XLA Ops:
  0.0 1.0 fusion.48
  1.0 0.9 fusion.79
  2.2 1.1 convolution_convert_fusion.4
  3.5 1.4 convolution_convert_fusion.1
  4.9 0.8 reshape.514
  5.7 11.9 %all-to-all-start = ((bf16[32,4,1408]{2,1,0:T(4,128)(2,1)}), bf16[32,4,1408]{2,1,0:T(4,128)(2,1)S(1)}, u32[]{:S(2)}, u32[]{:S(2)}) async-start(bf16[32,4,1408]{2,1,0:T(4,128)(2,1)} %reshape.514), calls=%async_computation | async-start | bytes 720896 | tf_op jit(solution)/shard_map/all_to_all | solution.py:40
  17.9 13.1 %all-to-all-done = bf16[32,4,1408]{2,1,0:T(4,128)(2,1)S(1)} async-done(((bf16[32,4,1408]{2,1,0:T(4,128)(2,1)}), bf16[32,4,1408]{2,1,0:T(4,128)(2,1)S(1)}, u32[]{:S(2)}, u32[]{:S(2)}) %all-to-all-start) | async-done | bytes 360480 | tf_op jit(solution)/shard_map/all_to_all | solution.py:40
  31.6 2.4 %fusion.121 = (f32[2,2,8]{2,1,0:T(2,128)S(1)}, f32[2,2,1,8,4096]{4,3,1,0,2:T(8,128)S(1)}) fusion(bf16[2,2,8,128]{3,2,1,0:T(8,128)(2,1)S(1)} %reshape.516, bf16[2,2,4096,128]{3,2,1,0:T(8,128)(2,1)} %param.27, pred[2,4096]{1,0:T(4,128)(4,1)S(1)} %iota_compare_fusion.2), kind=kOutput, calls=%fused_computation.183 | convolution fusion | flops 33947616 | bytes 2637952 | tf_op jit(solution)/shard_map/vmap(sngd,cnd->sngc)/dot_general | solution.py:59
  34.5 2.1 %fusion.23 = bf16[2,1,128,2,8]{2,4,3,0,1:T(8,128)(2,1)S(1)} fusion(f32[2,128,2,8]{1,3,2,0:T(8,128)S(1)} %fusion.95, bf16[2,2,4096,128]{3,2,1,0:T(8,128)(2,1)} %param.27, f32[2,2,1,8,4096]{4,3,1,0,2:T(8,128)S(1)} %get-tuple-element.38, f32[2,2,8]{2,1,0:T(2,128)S(1)} %max.23, f32[2,2,8]{2,1,0:T(2,128)S(1)} %add.169), kind=kOutput, calls=%fused_computation.29 | convolution fusion | flops 33828864 | bytes 2646272 | tf_op jit(solution)/shard_map/vmap(sngc,cnd->sngd)/dot_general | solution.py:73
  36.7 15.0 %all_to_all.45 = bf16[32,4,1024]{2,1,0:T(4,128)(2,1)S(1)} all-to-all(bf16[32,4,1024]{2,1,0:T(4,128)(2,1)S(1)} %broadcast_in_dim.54), channel_id=1, replica_groups=mesh['attn'=32,'tp'=8] {'attn'}, dimensions={0} | all-to-all | bytes 524288 | tf_op jit(solution)/shard_map/all_to_all | solution.py:36
  52.2 14.5 %all_to_all.46 = bf16[8,32,2,256]{3,1,2,0:T(8,128)(2,1)S(1)} all-to-all(bf16[8,32,2,256]{3,1,2,0:T(8,128)(2,1)S(1)} %broadcast_in_dim.55), channel_id=1, replica_groups=mesh['attn'=32,'tp'=8] {'tp'}, dimensions={0} | all-to-all | bytes 524288 | tf_op jit(solution)/shard_map/all_to_all | solution.py:36
  69.3 0.9 concatenate.21
  70.2 1.0 reshape.525
  71.2 4.0 %all-to-all-start.3 = ((bf16[32,2,4736]{2,1,0:T(2,128)(2,1)}), bf16[32,2,4736]{2,1,0:T(2,128)(2,1)S(1)}, u32[]{:S(2)}, u32[]{:S(2)}) async-start(bf16[32,2,4736]{2,1,0:T(2,128)(2,1)} %reshape.525), calls=%async_computation.3 | async-start | bytes 1212416 | tf_op jit(solution)/shard_map/all_to_all | solution.py:40
  76.1 16.9 %all-to-all-done.3 = bf16[32,2,4736]{2,1,0:T(2,128)(2,1)S(1)} async-done(((bf16[32,2,4736]{2,1,0:T(2,128)(2,1)}), bf16[32,2,4736]{2,1,0:T(2,128)(2,1)S(1)}, u32[]{:S(2)}, u32[]{:S(2)}) %all-to-all-start.3) | async-done | bytes 606240 | tf_op jit(solution)/shard_map/all_to_all | solution.py:40
  93.7 0.9 divide_multiply_fusion
  98.2 2.8 %multiply_reduce_fusion.1 = (f32[32,64]{1,0:T(8,128)S(1)}, f32[32,64]{1,0:T(8,128)S(1)}) fusion(f32[1,32,64,256]{3,2,1,0:T(8,128)} %param.40, f32[256]{0:T(256)} %bitcast.233, f32[256]{0:T(256)} %bitcast.234, f32[32,64]{1,0:T(8,128)S(1)} %broadcast_multiply_fusion.1, f32[32]{0:T(128)S(1)} %get-tuple-element.28, f32[256]{0:T(256)} %bitcast.232, ...), kind=kLoop, calls=%fused_computation.12 | loop fusion | flops 5238784 | bytes 2134272 | tf_op jit(solution)/shard_map/vmap()/reduce_sum | solution.py:129
  104.1 15.7 %all_to_all.47 = bf16[32,2,2048]{2,1,0:T(2,128)(2,1)S(1)} all-to-all(bf16[32,2,2048]{2,1,0:T(2,128)(2,1)S(1)} %broadcast_in_dim.58), channel_id=1, replica_groups=mesh['attn'=32,'tp'=8] {'attn'}, dimensions={0} | all-to-all | bytes 524288 | tf_op jit(solution)/shard_map/all_to_all | solution.py:36
  120.1 12.7 %all_to_all.48 = bf16[8,32,2,256]{3,1,2,0:T(8,128)(2,1)S(1)} all-to-all(bf16[8,32,2,256]{3,1,2,0:T(8,128)(2,1)S(1)} %broadcast_in_dim.59), channel_id=1, replica_groups=mesh['attn'=32,'tp'=8] {'tp'}, dimensions={0} | all-to-all | bytes 524288 | tf_op jit(solution)/shard_map/all_to_all | solution.py:36
  133.4 1.5 convolution_convert_fusion.2
  135.0 13.8 %all_to_all.49 = bf16[32,2,2176]{2,1,0:T(2,128)(2,1)S(1)} all-to-all(bf16[32,2,2176]{2,1,0:T(2,128)(2,1)S(1)} %reshape.533), channel_id=1, replica_groups=mesh['attn'=32,'tp'=8] {'attn'}, dimensions={0} | all-to-all | bytes 557056 | tf_op jit(solution)/shard_map/all_to_all | solution.py:40
  149.6 15.6 %all_to_all.50 = bf16[32,2,2048]{2,1,0:T(2,128)(2,1)S(1)} all-to-all(bf16[32,2,2048]{2,1,0:T(2,128)(2,1)S(1)} %broadcast_in_dim.60), channel_id=1, replica_groups=mesh['attn'=32,'tp'=8] {'attn'}, dimensions={0} | all-to-all | bytes 524288 | tf_op jit(solution)/shard_map/all_to_all | solution.py:36
  165.2 1.5 convolution_convert_fusion.5
  166.7 12.7 %all_to_all.51 = bf16[8,32,2,256]{3,1,2,0:T(8,128)(2,1)S(1)} all-to-all(bf16[8,32,2,256]{3,1,2,0:T(8,128)(2,1)S(1)} %broadcast_in_dim.61), channel_id=1, replica_groups=mesh['attn'=32,'tp'=8] {'tp'}, dimensions={0} | all-to-all | bytes 524288 | tf_op jit(solution)/shard_map/all_to_all | solution.py:36
  (109 shorter events, 14.2 us)
Async XLA Ops:
  0.0 67.9 %copy-start = (bf16[256,1,4608]{2,0,1:T(8,128)(2,1)S(1)}, bf16[256,1,4608]{2,0,1:T(8,128)(2,1)}, u32[]{:S(2)}) copy-start(bf16[256,1,4608]{2,0,1:T(8,128)(2,1)} %param.34) | copy-start | bytes 7077892
  3.4 14.2 %copy-start.7 = (s32[32]{0:T(128)S(1)}, s32[32]{0:T(128)}, u32[]{:S(2)}) copy-start(s32[32]{0:T(128)} %param.26) | copy-start | bytes 388
  3.4 14.3 %copy-start.11 = (s32[32]{0:T(128)S(1)}, s32[32]{0:T(128)}, u32[]{:S(2)}) copy-start(s32[32]{0:T(128)} %param.25) | copy-start | bytes 388
  5.7 25.2 %all-to-all-start = ((bf16[32,4,1408]{2,1,0:T(4,128)(2,1)}), bf16[32,4,1408]{2,1,0:T(4,128)(2,1)S(1)}, u32[]{:S(2)}, u32[]{:S(2)}) async-start(bf16[32,4,1408]{2,1,0:T(4,128)(2,1)} %reshape.514), calls=%async_computation | async-start | bytes 720896 | tf_op jit(solution)/shard_map/all_to_all | solution.py:40
  34.3 17.4 %copy-start.2 = (bf16[1024,256]{1,0:T(8,128)(2,1)S(1)}, bf16[1024,256]{1,0:T(8,128)(2,1)}, u32[]{:S(2)}) copy-start(bf16[1024,256]{1,0:T(8,128)(2,1)} %param.32) | copy-start | bytes 1572868
  36.6 30.2 %copy-start.3 = (bf16[32,2,256]{2,1,0:T(2,128)(2,1)S(1)}, bf16[32,2,256]{2,1,0:T(2,128)(2,1)}, u32[]{:S(2)}) copy-start(bf16[32,2,256]{2,1,0:T(2,128)(2,1)} %param.24) | copy-start | bytes 98308
  36.6 31.2 %copy-start.8 = (f32[256]{0:T(256)S(1)}, f32[256]{0:T(256)}, u32[]{:S(2)}) copy-start(f32[256]{0:T(256)} %param.33) | copy-start | bytes 3076
  52.2 16.2 %copy-start.6 = (bf16[256,32]{0,1:T(8,128)(2,1)S(1)}, bf16[256,32]{0,1:T(8,128)(2,1)}, u32[]{:S(2)}) copy-start(bf16[256,32]{0,1:T(8,128)(2,1)} %param.35) | copy-start | bytes 49156
  66.8 1.0 copy-start.4
  71.2 24.7 %copy-start.10 = (f32[32]{0:T(128)S(1)}, f32[32]{0:T(128)}, u32[]{:S(2)}) copy-start(f32[32]{0:T(128)} %param.42) | copy-start | bytes 388
  71.2 21.7 %all-to-all-start.3 = ((bf16[32,2,4736]{2,1,0:T(2,128)(2,1)}), bf16[32,2,4736]{2,1,0:T(2,128)(2,1)S(1)}, u32[]{:S(2)}, u32[]{:S(2)}) async-start(bf16[32,2,4736]{2,1,0:T(2,128)(2,1)} %reshape.525), calls=%async_computation.3 | async-start | bytes 1212416 | tf_op jit(solution)/shard_map/all_to_all | solution.py:40
  93.4 26.3 %copy-start.1 = (bf16[2048,256]{1,0:T(8,128)(2,1)S(1)}, bf16[2048,256]{1,0:T(8,128)(2,1)}, u32[]{:S(2)}) copy-start(bf16[2048,256]{1,0:T(8,128)(2,1)} %param.36) | copy-start | bytes 3145732
  101.0 31.9 %copy-start.5 = (bf16[32,2,256]{2,0,1:T(8,128)(2,1)S(1)}, bf16[32,2,256]{2,0,1:T(8,128)(2,1)}, u32[]{:S(2)}) copy-start(bf16[32,2,256]{2,0,1:T(8,128)(2,1)} %copy-done.4) | copy-start | bytes 98308
  101.0 31.9 %copy-start.9 = (f32[256]{0:T(256)S(1)}, f32[256]{0:T(256)}, u32[]{:S(2)}) copy-start(f32[256]{0:T(256)} %param.45) | copy-start | bytes 3076

commit v2 on v0

v2 whole, which is shorter than its diff:
```python
import jax
import jax.numpy as jnp
from jax import lax
from jax.experimental import pallas as pl
from jax.experimental.pallas import tpu as pltpu
from jax.sharding import PartitionSpec as P

HEAD_SIZE = 128
EPS = 1e-05
MASKED = -1e30
LANES = 128
STEPS = 2
REQ = 32
ROWS = REQ * STEPS
ATTN = 32
TP = 8
WIDTH = 8192
QKV_HALF = 768
UP_QUARTER = 512
MIX_QUARTER = 1280
FF_QUARTER = 640
INNER = 2048
STATES = 256
HEADS = 32
F32 = jnp.float32
BF16 = jnp.bfloat16


def dot(a, b):
    return jnp.dot(a, b, preferred_element_type=F32)


def iota(shape, axis):
    return lax.broadcasted_iota(jnp.int32, shape, axis)


def one_hot(condition):
    return jnp.where(condition, 1.0, 0.0).astype(BF16)


def gain_rows(x, gain):
    squares = jnp.sum(x * x, axis=-1, keepdims=True)
    high = squares.astype(BF16).astype(F32)
    column = iota((x.shape[0], LANES), 1)
    tile = jnp.where(column == 0, high, jnp.where(column == 1, squares - high, 0.0))
    return (x * gain).astype(BF16), tile.astype(BF16)


def scale_of(tile):
    return lax.rsqrt((tile[:, 0:1] + tile[:, 1:2]) / WIDTH + EPS)


def sum_pieces(ref, pieces):
    rows = ref.shape[0] // pieces
    return jnp.sum(ref[...].astype(F32).reshape(pieces, rows, ref.shape[1]), axis=0)


def write_copies(ref, piece, copies):
    piece = piece.astype(ref.dtype)
    for k in range(copies):
        ref[pl.ds(k * piece.shape[0], piece.shape[0]), :] = piece


def slots_by_row(slot_ref, columns):
    request = iota((REQ, columns), 0)
    column = iota((REQ, columns), 1)
    spread = one_hot((column % ROWS) // STEPS == request)
    slots = jnp.broadcast_to(slot_ref[...], (8, REQ)).astype(F32).astype(BF16)
    return dot(slots, spread)[0:1].astype(jnp.int32)


def qkv_kernel(hidden, slot_of, gain, w_query, w_key, w_value, out):
    normed, tile = gain_rows(hidden[...].astype(F32), gain[...])
    key = dot(normed, w_key[...]).astype(BF16)
    value = dot(normed, w_value[...]).astype(BF16)
    query = dot(normed, w_query[...]).astype(BF16)
    spare = jnp.zeros_like(tile)
    second = jnp.concatenate([query[:, QKV_HALF:], key, value, tile, spare], axis=1)
    halves = jnp.concatenate([query[:, :QKV_HALF], second], axis=0)
    column = iota((1, 2 * ROWS), 1)
    code = slots_by_row(slot_of, 2 * ROWS) * 4 + (column // ROWS) * 2 + column % STEPS
    row = iota((ATTN * 8, 2 * ROWS), 0)
    row_code = ((row // 8) * 2 + (row // 2) % 2) * 4 + ((row // 4) % 2) * 2 + row % 2
    out[...] = dot(one_hot(row_code == code), halves).astype(BF16)


def attend_kernel(pieces, lengths, slot_of, cache, out):
    first_slot = lax.axis_index("attn") * 2
    summed = sum_pieces(pieces, ATTN)
    low, high = summed[0:4], summed[4:8]
    scale = scale_of(high[:, 512 : 512 + LANES])
    low = (low * scale).astype(BF16).astype(F32)
    high = (high * scale).astype(BF16).astype(F32)
    whole = jnp.concatenate([low, high], axis=1)
    heads = 8
    factor = HEAD_SIZE ** (-0.5)
    group = heads * STEPS
    step_of_row = iota((group, 1), 0) % STEPS
    outputs = []
    for slot in range(2):
        length = jnp.int32(0)
        for r in range(REQ):
            length = length + jnp.where(slot_of[r] == first_slot + slot, lengths[r], 0)
        rows = whole[slot * 2 : slot * 2 + 2]
        query = jnp.concatenate([rows[:, h * LANES : (h + 1) * LANES] for h in range(heads)], axis=0)
        fresh_key = rows[:, 1024 : 1024 + LANES]
        fresh_value = rows[:, 1024 + LANES : 1024 + 2 * LANES]
        scores = (
            lax.dot_general(
                query.astype(BF16), cache[slot, 0], (((1,), (1,)), ((), ())), preferred_element_type=F32
            )
            * factor
        )
        scores = jnp.where(iota(scores.shape, 1) < length, scores, MASKED)
        fresh = []
        for t in range(STEPS):
            score = jnp.sum(query * fresh_key[t : t + 1], axis=-1, keepdims=True) * factor
            fresh.append(jnp.where(step_of_row >= t, score, MASKED))
        top = jnp.maximum(jnp.max(scores, axis=-1, keepdims=True), jnp.maximum(fresh[0], fresh[1]))
        weights = jnp.exp(scores - top)
        total = jnp.sum(weights, axis=-1, keepdims=True)
        mixed = dot(weights.astype(BF16), cache[slot, 1])
        for t in range(STEPS):
            weight = jnp.exp(fresh[t] - top)
            total = total + weight
            mixed = mixed + weight.astype(BF16).astype(F32) * fresh_value[t : t + 1]
        outputs.append(mixed / total)
    halves = []
    for half in range(2):
        for slot in range(2):
            part = outputs[slot]
            first = half * 4
            halves.append(
                jnp.concatenate([part[(first + h) * 2 : (first + h) * 2 + 2] for h in range(4)], axis=1)
            )
    write_copies(out, jnp.concatenate(halves, axis=0), ATTN)


def attn_out_kernel(pieces, slot_of, weight, out):
    column = iota((1, ROWS), 1)
    slots = slots_by_row(slot_of, ROWS) * 4 + column % STEPS
    row = iota((ATTN * 8, ROWS), 0)
    row_code = ((row // 8) * 2 + (row // 2) % 2) * 4 + ((row // 4) % 2) * 2 + row % 2
    gathered = pieces[...]
    total = None
    for half in range(2):
        chosen = one_hot(row_code == slots + half * 2)
        mine = lax.dot_general(chosen, gathered, (((0,), (0,)), ((), ())), preferred_element_type=F32)
        term = dot(mine.astype(BF16), weight[pl.ds(half * 512, 512), :])
        total = term if total is None else total + term
    write_copies(out, total, TP)


def by_owner(quarters):
    stacked = jnp.concatenate(quarters, axis=0)
    row = iota((ATTN * 8, 4 * ROWS), 0)
    column = iota((ATTN * 8, 4 * ROWS), 1)
    source = ((row // 2) % 4) * ROWS + (row // 8) * 2 + row % 2
    return dot(one_hot(source == column), stacked).astype(BF16)


def mix_in_kernel(pieces, hidden, gain, w_main, w_step, out, first_out):
    first = (sum_pieces(pieces, TP) + hidden[...].astype(F32)).astype(BF16)
    first_out[...] = first
    normed, tile = gain_rows(first.astype(F32), gain[...])
    main = dot(normed, w_main[...]).astype(BF16)
    steps = dot(normed, w_step[...]).astype(BF16)
    spare = jnp.zeros_like(tile)
    steps = jnp.concatenate([steps, spare[:, : LANES - HEADS]], axis=1)
    state = 2 * INNER
    extra = (
        [main[:, state : state + STATES]],
        [main[:, state + STATES : state + 2 * STATES]],
        [steps, tile],
        [spare, spare],
    )
    quarters = []
    for q in range(4):
        cut = slice(q * 512, (q + 1) * 512)
        parts = [main[:, :INNER][:, cut], main[:, INNER : 2 * INNER][:, cut]]
        quarters.append(jnp.concatenate(parts + extra[q], axis=1))
    out[...] = by_owner(quarters)


def silu(x):
    return x / (1.0 + jnp.exp(-x))


def mamba_kernel(
    pieces, conv_weight, conv_bias, conv_state, state, a_log, dt_bias, skip_gain, group_gain, out
):
    summed = sum_pieces(pieces, ATTN)
    scale = scale_of(summed[4:6, 1024 + LANES :])
    summed = summed * jnp.concatenate([scale] * 4, axis=0)

    def conved(now, cut):
        window = jnp.concatenate([conv_state[:, cut], now], axis=0)
        total = conv_bias[:, cut]
        for k in range(4):
            total = total + conv_weight[k : k + 1, cut] * window[k : k + 2]
        return silu(total)

    xs = jnp.concatenate(
        [
            conved(summed[q * 2 : q * 2 + 2, 512:1024], slice(q * 512, (q + 1) * 512))
            for q in range(4)
        ],
        axis=1,
    )
    b_in = conved(summed[0:2, 1024:1280], slice(INNER, INNER + STATES))
    c_out = conved(summed[2:4, 1024:1280], slice(INNER + STATES, INNER + 2 * STATES))
    gate = jnp.concatenate([summed[q * 2 : q * 2 + 2, 0:512] for q in range(4)], axis=1)
    raw = summed[4:6, 1024 : 1024 + HEADS] + dt_bias[...]
    step = jnp.maximum(raw, 0.0) + jnp.log1p(jnp.exp(-jnp.abs(raw)))
    decay = jnp.exp(-step * jnp.exp(a_log[...]))
    d0, d1, s0, s1 = decay[0:1], decay[1:2], step[0:1], step[1:2]
    per_head = jnp.concatenate([d0, d0 * d1, s0, d1 * s0, s1, skip_gain[...], d0, d0], axis=0)
    spread = jnp.where(iota((HEADS, INNER), 1) // 64 == iota((HEADS, INNER), 0), 1.0, 0.0)
    wide = jnp.dot(per_head, spread, precision=lax.Precision.HIGHEST, preferred_element_type=F32)
    c_high = c_out.astype(BF16)
    c_low = (c_out - c_high.astype(F32)).astype(BF16)
    whole = state[...]
    high = whole.astype(BF16)
    low = (whole - high.astype(F32)).astype(BF16)
    last = (((1,), (1,)), ((), ()))
    both = jnp.concatenate([c_high, c_low], axis=0)
    by_high = lax.dot_general(both, high, last, preferred_element_type=F32)
    by_low = lax.dot_general(c_high, low, last, preferred_element_type=F32)
    read_old = by_high[0:2] + by_high[2:4] + by_low
    b0c0 = jnp.sum(b_in[0:1] * c_out[0:1], axis=-1, keepdims=True)
    b0c1 = jnp.sum(b_in[0:1] * c_out[1:2], axis=-1, keepdims=True)
    b1c1 = jnp.sum(b_in[1:2] * c_out[1:2], axis=-1, keepdims=True)
    x0, x1 = xs[0:1], xs[1:2]
    read0 = wide[0:1] * read_old[0:1] + wide[2:3] * x0 * b0c0
    read1 = wide[1:2] * read_old[1:2] + wide[3:4] * x0 * b0c1 + wide[4:5] * x1 * b1c1
    read = jnp.concatenate([read0, read1], axis=0) + wide[5:6] * xs
    gated = read * silu(gate)
    mixer = gated * lax.rsqrt(jnp.mean(gated * gated, axis=-1, keepdims=True) + EPS) * group_gain[...]
    piece = jnp.concatenate([mixer[:, q * 512 : (q + 1) * 512] for q in range(4)], axis=0)
    write_copies(out, piece, ATTN)


def project_out_kernel(pieces, weight, out):
    row = iota((4 * ROWS, ATTN * 8), 0)
    column = iota((4 * ROWS, ATTN * 8), 1)
    source = ((row % ROWS) // 2) * 8 + (row // ROWS) * 2 + row % 2
    ordered = dot(one_hot(source == column), pieces[...]).astype(BF16)
    total = None
    for q in range(4):
        term = dot(ordered[q * ROWS : (q + 1) * ROWS], weight[pl.ds(q * 512, 512), :])
        total = term if total is None else total + term
    write_copies(out, total, TP)


def up_kernel(pieces, first, gain, w_up, out, second_out):
    second = (sum_pieces(pieces, TP) + first[...].astype(F32)).astype(BF16)
    second_out[...] = second
    normed, tile = gain_rows(second.astype(F32), gain[...])
    up = dot(normed, w_up[...]).astype(BF16)
    out[...] = by_owner(
        [
            jnp.concatenate([up[:, q * UP_QUARTER : (q + 1) * UP_QUARTER], tile], axis=1)
            for q in range(4)
        ]
    )


def active_kernel(pieces, out):
    summed = sum_pieces(pieces, ATTN)
    lifted = jnp.maximum(summed[:, :UP_QUARTER] * scale_of(summed[:, UP_QUARTER:]), 0.0)
    write_copies(out, lifted * lifted, ATTN)


def last_kernel(pieces, second, out):
    out[...] = (sum_pieces(pieces, TP) + second[...].astype(F32)).astype(BF16)


def call(kernel, out_shapes, *operands, smem=()):
    vmem = pl.BlockSpec(memory_space=pltpu.VMEM)
    scalar = pl.BlockSpec(memory_space=pltpu.SMEM)
    shapes = [jax.ShapeDtypeStruct(shape, BF16) for shape in out_shapes]
    return pl.pallas_call(
        kernel,
        out_shape=shapes[0] if len(shapes) == 1 else shapes,
        in_specs=[scalar if k in smem else vmem for k in range(len(operands))],
        out_specs=vmem if len(shapes) == 1 else [vmem] * len(shapes),
        compiler_params=pltpu.CompilerParams(vmem_limit_bytes=24 * 1024 * 1024),
    )(*operands)


def exchange(values, axis, pieces):
    rows, columns = values.shape
    cut = values.reshape(pieces, rows // pieces, columns)
    return lax.all_to_all(cut, axis, 0, 0).reshape(rows, columns)


def on_device(
    hidden,
    lengths,
    slot_of,
    kv_cache,
    attn_gain,
    w_query,
    key_matrix,
    value_matrix,
    w_attn_out,
    mamba_gain,
    w_mamba_in,
    w_mamba_dt,
    w_mamba_out,
    conv_weight,
    conv_bias,
    conv_state,
    ssm_state,
    a_log,
    dt_bias,
    skip_gain,
    group_gain,
    mlp_gain,
    w_up,
    w_down,
):
    rows = hidden.reshape(ROWS, -1)
    width = rows.shape[1]
    slot_row = slot_of.reshape(1, REQ)
    owned = ATTN * 8

    def row(x):
        return x.reshape(1, -1)

    pieces = call(
        qkv_kernel, [(owned, QKV_HALF)],
        rows, slot_row, row(attn_gain), w_query, key_matrix, value_matrix,
    )
    pieces = exchange(pieces, "attn", ATTN)
    pieces = call(
        attend_kernel, [(owned, 512)], pieces, lengths, slot_of, kv_cache, smem=(1, 2)
    )
    pieces = exchange(pieces, "attn", ATTN)
    pieces = call(attn_out_kernel, [(TP * ROWS, width)], pieces, slot_row, w_attn_out)
    pieces = exchange(pieces, "tp", TP)
    pieces, first = call(
        mix_in_kernel, [(owned, MIX_QUARTER), (ROWS, width)],
        pieces, rows, row(mamba_gain), w_mamba_in.reshape(width, -1), w_mamba_dt,
    )
    pieces = exchange(pieces, "attn", ATTN)
    pieces = call(
        mamba_kernel, [(owned, 512)],
        pieces, conv_weight.reshape(4, -1), conv_bias, conv_state.reshape(3, -1),
        ssm_state.reshape(INNER, STATES), row(a_log), row(dt_bias), row(skip_gain), group_gain,
    )
    pieces = exchange(pieces, "attn", ATTN)
    pieces = call(project_out_kernel, [(TP * ROWS, width)], pieces, w_mamba_out)
    pieces = exchange(pieces, "tp", TP)
    pieces, second = call(
        up_kernel, [(owned, FF_QUARTER), (ROWS, width)], pieces, first, row(mlp_gain), w_up
    )
    pieces = exchange(pieces, "attn", ATTN)
    pieces = call(active_kernel, [(owned, 512)], pieces)
    pieces = exchange(pieces, "attn", ATTN)
    pieces = call(project_out_kernel, [(TP * ROWS, width)], pieces, w_down)
    pieces = exchange(pieces, "tp", TP)
    return call(last_kernel, [(ROWS, width)], pieces, second).reshape(hidden.shape)


def solution(mesh):
    in_specs = (
        P(None, None, "attn"),
        P(),
        P(),
        P("attn", None, None, "tp"),
        P("attn"),
        P("attn", "tp"),
        P("attn", "tp"),
        P("attn", "tp"),
        P("tp", "attn"),
        P("attn"),
        P("attn", "tp", None),
        P("attn", "tp"),
        P("tp", "attn"),
        P(None, "tp", None),
        P("tp", None),
        P("attn", None, "tp", None),
        P("attn", "tp", None, None),
        P("tp"),
        P("tp"),
        P("tp"),
        P("tp", None),
        P("attn"),
        P("attn", "tp"),
        P("tp", "attn"),
    )
    out_specs = P(None, None, "attn")
    return jax.shard_map(
        on_device, mesh=mesh, in_specs=in_specs, out_specs=out_specs, check_vma=False
    )
```

time: 916 us -> 169 us (0.18)
  waiting for transfers between devices: 723 us -> 25.2 us
  blocking collectives: 131 us -> 112 us
  matrix products: 18.4 us -> 0 us
  other arithmetic: 17.4 us -> 0 us
  between operations: 15.1 us -> 0.18 us
  starting transfers between devices: 0.25 us -> 12.4 us
    psum x7 -> x0, waiting for transfers between devices: 723 us -> none  [the longest x2 281 us: on_device(): summed = lax.psum((query_part, key_part, value_part, squares_attn), 'attn')]
    all_to_all x0 -> x7, blocking collectives: none -> 112 us  [exchange(): return lax.all_to_all(cut, axis, 0, 0).reshape(rows, columns)]
    all_gather x2 -> x0, blocking collectives: 70 us -> none  [the longest x1 35.1 us: on_device(): shard_piece = lax.all_gather(slot_outputs, 'attn', axis=0, tiled=True)]
    psum x1 -> x0, blocking collectives: 61.2 us -> none  [on_device(): lax.psum(squares_ff.astype(jnp.bfloat16), 'attn').astype(jnp.float32)]
    all_to_all x0 -> x2, waiting for transfers between devices: none -> 25.2 us  [exchange(): return lax.all_to_all(cut, axis, 0, 0).reshape(rows, columns)]
    dot_general x15 -> x0, matrix products: 18.4 us -> none  [the longest x1 2.35 us: attend(): jnp.einsum('sngd,cnd->sngc', queries, old_keys, preferred_element_type=jn...]
    all_to_all x0 -> x2, starting transfers between devices: none -> 12.4 us  [exchange(): return lax.all_to_all(cut, axis, 0, 0).reshape(rows, columns)]
  transfers between devices with their start and end apart: 7 -> 2, of which waited for: 7 -> 2; matrix products, arithmetic and copies ran while one was open for 0% -> 0% of each run, Pallas kernels for 0% -> 0%
where the time goes in v2:
time: 169 us; the launch traced here: 168 us
  blocking collectives  112 us (66%)
  waiting for transfers between devices  25.2 us (15%)
  starting transfers between devices  12.4 us (7%)
  local copies, waits for them, and re-layouts  10.1 us (6%)
  Pallas kernels  8.45 us (5%)
    all_to_all x7, blocking collectives, exchange(): return lax.all_to_all(cut, axis, 0, 0).reshape(rows, columns)  112 us
    all_to_all x2, waiting for transfers between devices, exchange(): return lax.all_to_all(cut, axis, 0, 0).reshape(rows, columns)  25.2 us
    all_to_all x2, starting transfers between devices, exchange(): return lax.all_to_all(cut, axis, 0, 0).reshape(rows, columns)  12.4 us
    unnamed x49, local copies, waits for them, and re-layouts  8.68 us
    pallas_call x10, Pallas kernels, call(): pl.pallas_call(kernel, out_shape=shapes[0] if len(shapes) == 1 else shape...  8.45 us
  transfers between devices with their start and end apart: 2, of which 2 were waited for; matrix products, arithmetic and copies ran while one was open for 0% of the time, Pallas kernels for 0%

profile of v2, /device:TPU:1, one launch (start us, length us, event | category | flops | bytes accessed | tf_op | source)
XLA Modules:
  0.0 168.3 jit_solution(6990915763582883870)
XLA Ops:
  0.0 0.8 reshape.93.hidden
  0.8 1.0 copy-done.6
  1.8 0.8 copy-done.8
  2.7 0.8 copy-done.9
  3.5 0.7 copy-done.12
  4.2 0.7 copy-done.14
  5.3 25.5 %all_to_all.45 = bf16[32,8,768]{2,1,0:T(8,128)(2,1)S(1)} all-to-all(bf16[32,8,768]{2,1,0:T(8,128)(2,1)S(1)} %bitcast.36), channel_id=1, replica_groups=mesh['attn'=32,'tp'=8] {'attn'}, dimensions={0} | all-to-all | bytes 786432 | tf_op jit(solution)/shard_map/all_to_all | solution.py:294
  30.8 2.2 %copy-done = bf16[2,2,4096,128]{3,2,1,0:T(8,128)(2,1)S(1)} copy-done((bf16[2,2,4096,128]{3,2,1,0:T(8,128)(2,1)S(1)}, bf16[2,2,4096,128]{3,2,1,0:T(8,128)(2,1)}, u32[]{:S(2)}) %copy-start) | copy-done | bytes 4194328
  33.0 0.7 copy-done.19
  33.7 2.1 %shard_map.227 = bf16[256,512]{1,0:T(8,128)(2,1)S(1)} custom-call(bf16[256,768]{1,0:T(8,128)(2,1)S(1)} %bitcast.37, s32[32]{0:T(128)S(1)} %copy-done.19, s32[32]{0:T(128)S(1)} %copy-done.12, bf16[2,2,4096,128]{3,2,1,0:T(8,128)(2,1)S(1)} %copy-done), custom_call_target="tpu_custom_call" | custom-call | tf_op jit(solution)/shard_map/pallas_call | solution.py:282
  35.7 15.2 %all_to_all.46 = bf16[32,8,512]{2,1,0:T(8,128)(2,1)S(1)} all-to-all(bf16[32,8,512]{2,1,0:T(8,128)(2,1)S(1)} %bitcast.49), channel_id=1, replica_groups=mesh['attn'=32,'tp'=8] {'attn'}, dimensions={0} | all-to-all | bytes 524288 | tf_op jit(solution)/shard_map/all_to_all | solution.py:294
  51.0 1.3 shard_map.228
  52.3 8.4 %all-to-all-start.2 = ((bf16[8,64,256]{2,1,0:T(8,128)(2,1)}), bf16[8,64,256]{2,1,0:T(8,128)(2,1)S(1)}, u32[]{:S(2)}, u32[]{:S(2)}) async-start(bf16[8,64,256]{2,1,0:T(8,128)(2,1)} %bitcast.6), calls=%async_computation.2 | async-start | bytes 524288 | tf_op jit(solution)/shard_map/all_to_all | solution.py:294
  60.8 6.4 %all-to-all-done.2 = bf16[8,64,256]{2,1,0:T(8,128)(2,1)S(1)} async-done(((bf16[8,64,256]{2,1,0:T(8,128)(2,1)}), bf16[8,64,256]{2,1,0:T(8,128)(2,1)S(1)}, u32[]{:S(2)}, u32[]{:S(2)}) %all-to-all-start.2) | async-done | bytes 262176 | tf_op jit(solution)/shard_map/all_to_all | solution.py:294
  67.2 1.6 shard_map.229
  68.8 4.0 %all-to-all-start.3 = ((bf16[32,8,1280]{2,1,0:T(8,128)(2,1)}), bf16[32,8,1280]{2,1,0:T(8,128)(2,1)S(1)}, u32[]{:S(2)}, u32[]{:S(2)}) async-start(bf16[32,8,1280]{2,1,0:T(8,128)(2,1)} %bitcast.10), calls=%async_computation.3 | async-start | bytes 1310720 | tf_op jit(solution)/shard_map/all_to_all | solution.py:294
  72.9 18.8 %all-to-all-done.3 = bf16[32,8,1280]{2,1,0:T(8,128)(2,1)S(1)} async-done(((bf16[32,8,1280]{2,1,0:T(8,128)(2,1)}), bf16[32,8,1280]{2,1,0:T(8,128)(2,1)S(1)}, u32[]{:S(2)}, u32[]{:S(2)}) %all-to-all-start.3) | async-done | bytes 655392 | tf_op jit(solution)/shard_map/all_to_all | solution.py:294
  91.7 1.6 copy-done.2
  93.3 1.2 shard_map.230
  94.5 15.5 %all_to_all.47 = bf16[32,8,512]{2,1,0:T(8,128)(2,1)S(1)} all-to-all(bf16[32,8,512]{2,1,0:T(8,128)(2,1)S(1)} %bitcast.48), channel_id=1, replica_groups=mesh['attn'=32,'tp'=8] {'attn'}, dimensions={0} | all-to-all | bytes 524288 | tf_op jit(solution)/shard_map/all_to_all | solution.py:294
  110.5 12.7 %all_to_all.48 = bf16[8,64,256]{2,1,0:T(8,128)(2,1)S(1)} all-to-all(bf16[8,64,256]{2,1,0:T(8,128)(2,1)S(1)} %bitcast.45), channel_id=1, replica_groups=mesh['attn'=32,'tp'=8] {'tp'}, dimensions={0} | all-to-all | bytes 524288 | tf_op jit(solution)/shard_map/all_to_all | solution.py:294
  123.7 15.1 %all_to_all.49 = bf16[32,8,640]{2,1,0:T(8,128)(2,1)S(1)} all-to-all(bf16[32,8,640]{2,1,0:T(8,128)(2,1)S(1)} %bitcast.50), channel_id=1, replica_groups=mesh['attn'=32,'tp'=8] {'attn'}, dimensions={0} | all-to-all | bytes 655360 | tf_op jit(solution)/shard_map/all_to_all | solution.py:294
  139.1 15.4 %all_to_all.50 = bf16[32,8,512]{2,1,0:T(8,128)(2,1)S(1)} all-to-all(bf16[32,8,512]{2,1,0:T(8,128)(2,1)S(1)} %bitcast.41), channel_id=1, replica_groups=mesh['attn'=32,'tp'=8] {'attn'}, dimensions={0} | all-to-all | bytes 524288 | tf_op jit(solution)/shard_map/all_to_all | solution.py:294
  155.0 12.7 %all_to_all.51 = bf16[8,64,256]{2,1,0:T(8,128)(2,1)S(1)} all-to-all(bf16[8,64,256]{2,1,0:T(8,128)(2,1)S(1)} %bitcast.47), channel_id=1, replica_groups=mesh['attn'=32,'tp'=8] {'tp'}, dimensions={0} | all-to-all | bytes 524288 | tf_op jit(solution)/shard_map/all_to_all | solution.py:294
  (48 shorter events, 3.1 us)
Async XLA Ops:
  0.8 1.0 copy-start.6
  1.8 0.8 copy-start.8
  2.7 0.8 copy-start.9
  4.2 0.7 copy-start.14
  30.8 2.2 %copy-start = (bf16[2,2,4096,128]{3,2,1,0:T(8,128)(2,1)S(1)}, bf16[2,2,4096,128]{3,2,1,0:T(8,128)(2,1)}, u32[]{:S(2)}) copy-start(bf16[2,2,4096,128]{3,2,1,0:T(8,128)(2,1)} %cache.1) | copy-start | bytes 12582916
  33.0 0.7 copy-start.19
  33.6 17.3 %copy-start.7 = (bf16[1024,256]{1,0:T(8,128)(2,1)S(1)}, bf16[1024,256]{1,0:T(8,128)(2,1)}, u32[]{:S(2)}) copy-start(bf16[1024,256]{1,0:T(8,128)(2,1)} %weight.3) | copy-start | bytes 1572868
  33.7 27.1 %copy-start.22 = (bf16[256,32]{0,1:T(8,128)(2,1)S(1)}, bf16[256,32]{0,1:T(8,128)(2,1)}, u32[]{:S(2)}) copy-start(bf16[256,32]{0,1:T(8,128)(2,1)} %param.35) | copy-start | bytes 49156
  33.7 33.6 %copy-start.1 = (bf16[256,1,4608]{2,0,1:T(8,128)(2,1)S(1)}, bf16[256,1,4608]{2,0,1:T(8,128)(2,1)}, u32[]{:S(2)}) copy-start(bf16[256,1,4608]{2,0,1:T(8,128)(2,1)} %param.34) | copy-start | bytes 7077892
  33.7 33.6 %copy-start.13 = (f32[256]{0:T(256)S(1)}, f32[256]{0:T(256)}, u32[]{:S(2)}) copy-start(f32[256]{0:T(256)} %param.33) | copy-start | bytes 3076
  52.3 20.5 %copy-start.21 = (f32[1,3,1,2560]{3,2,1,0:T(1,128)S(1)}, f32[1,3,1,2560]{3,2,1,0:T(1,128)}, u32[]{:S(2)}) copy-start(f32[1,3,1,2560]{3,2,1,0:T(1,128)} %param.39) | copy-start | bytes 92164
  52.3 20.6 %copy-start.20 = (f32[4,1,2560]{2,1,0:T(1,128)S(1)}, f32[4,1,2560]{2,1,0:T(1,128)}, u32[]{:S(2)}) copy-start(f32[4,1,2560]{2,1,0:T(1,128)} %param.37) | copy-start | bytes 122884
  52.3 39.4 %copy-start.10 = (f32[1,2560]{1,0:T(1,128)S(1)}, f32[1,2560]{1,0:T(1,128)}, u32[]{:S(2)}) copy-start(f32[1,2560]{1,0:T(1,128)} %conv_bias.1) | copy-start | bytes 30724
  52.3 39.4 %copy-start.11 = (f32[1,2048]{1,0:T(1,128)S(1)}, f32[1,2048]{1,0:T(1,128)}, u32[]{:S(2)}) copy-start(f32[1,2048]{1,0:T(1,128)} %group_gain.1) | copy-start | bytes 24580
  52.3 39.4 %copy-start.16 = (f32[32]{0:T(128)S(1)}, f32[32]{0:T(128)}, u32[]{:S(2)}) copy-start(f32[32]{0:T(128)} %param.41) | copy-start | bytes 388
  52.3 39.4 %copy-start.17 = (f32[32]{0:T(128)S(1)}, f32[32]{0:T(128)}, u32[]{:S(2)}) copy-start(f32[32]{0:T(128)} %param.42) | copy-start | bytes 388
  52.3 39.4 %copy-start.18 = (f32[32]{0:T(128)S(1)}, f32[32]{0:T(128)}, u32[]{:S(2)}) copy-start(f32[32]{0:T(128)} %param.43) | copy-start | bytes 388
  52.3 14.9 %all-to-all-start.2 = ((bf16[8,64,256]{2,1,0:T(8,128)(2,1)}), bf16[8,64,256]{2,1,0:T(8,128)(2,1)S(1)}, u32[]{:S(2)}, u32[]{:S(2)}) async-start(bf16[8,64,256]{2,1,0:T(8,128)(2,1)} %bitcast.6), calls=%async_computation.2 | async-start | bytes 524288 | tf_op jit(solution)/shard_map/all_to_all | solution.py:294
  68.8 41.2 %copy-start.3 = (bf16[2048,256]{1,0:T(8,128)(2,1)S(1)}, bf16[2048,256]{1,0:T(8,128)(2,1)}, u32[]{:S(2)}) copy-start(bf16[2048,256]{1,0:T(8,128)(2,1)} %weight.4) | copy-start | bytes 3145732
  68.8 22.9 %all-to-all-start.3 = ((bf16[32,8,1280]{2,1,0:T(8,128)(2,1)}), bf16[32,8,1280]{2,1,0:T(8,128)(2,1)S(1)}, u32[]{:S(2)}, u32[]{:S(2)}) async-start(bf16[32,8,1280]{2,1,0:T(8,128)(2,1)} %bitcast.10), calls=%async_computation.3 | async-start | bytes 1310720 | tf_op jit(solution)/shard_map/all_to_all | solution.py:294
  91.7 1.6 copy-start.2
  93.3 29.9 %copy-start.5 = (bf16[256,2048]{1,0:T(8,128)(2,1)S(1)}, bf16[256,2048]{1,0:T(8,128)(2,1)}, u32[]{:S(2)}) copy-start(bf16[256,2048]{1,0:T(8,128)(2,1)} %w_up.1) | copy-start | bytes 3145732
  93.3 29.9 %copy-start.15 = (f32[256]{0:T(256)S(1)}, f32[256]{0:T(256)}, u32[]{:S(2)}) copy-start(f32[256]{0:T(256)} %param.45) | copy-start | bytes 3076
  110.0 44.5 %copy-start.4 = (bf16[2048,256]{1,0:T(8,128)(2,1)S(1)}, bf16[2048,256]{1,0:T(8,128)(2,1)}, u32[]{:S(2)}) copy-start(bf16[2048,256]{1,0:T(8,128)(2,1)} %weight.5) | copy-start | bytes 3145732
  (1 other events, 0.7 us)

commit v3 on v2

--- a/solution.py
+++ b/solution.py
@@ -69,19 +69,35 @@
     return dot(slots, spread)[0:1].astype(jnp.int32)
 
 
-def qkv_kernel(hidden, slot_of, gain, w_query, w_key, w_value, out):
-    normed, tile = gain_rows(hidden[...].astype(F32), gain[...])
-    key = dot(normed, w_key[...]).astype(BF16)
-    value = dot(normed, w_value[...]).astype(BF16)
-    query = dot(normed, w_query[...]).astype(BF16)
+def qkv_kernel(
+    hidden, gain, slot_of, lengths, w_key, w_value, w_query, cache,
+    out, rows_out, slots_out, lengths_out, cache_out, *scratch
+):
+    places = (*scratch[:2], slots_out, lengths_out, *scratch[2:5], cache_out)
+    copies = []
+    for k, source in enumerate((hidden, gain, slot_of, lengths, w_key, w_value, w_query, cache)):
+        copies.append(pltpu.make_async_copy(source, places[k], scratch[5].at[k]))
+        copies[k].start()
+    hidden_here, gain_here, key_here, value_here, query_here = scratch[:5]
+    copies[0].wait()
+    rows = hidden_here[...].astype(F32).reshape(ROWS, -1)
+    rows_out[...] = rows.astype(BF16)
+    copies[1].wait()
+    normed, tile = gain_rows(rows, gain_here[...])
+    for k in range(2, 7):
+        copies[k].wait()
+    key = dot(normed, key_here[...]).astype(BF16)
+    value = dot(normed, value_here[...]).astype(BF16)
+    query = dot(normed, query_here[...]).astype(BF16)
     spare = jnp.zeros_like(tile)
     second = jnp.concatenate([query[:, QKV_HALF:], key, value, tile, spare], axis=1)
     halves = jnp.concatenate([query[:, :QKV_HALF], second], axis=0)
     column = iota((1, 2 * ROWS), 1)
-    code = slots_by_row(slot_of, 2 * ROWS) * 4 + (column // ROWS) * 2 + column % STEPS
+    code = slots_by_row(slots_out, 2 * ROWS) * 4 + (column // ROWS) * 2 + column % STEPS
     row = iota((ATTN * 8, 2 * ROWS), 0)
     row_code = ((row // 8) * 2 + (row // 2) % 2) * 4 + ((row // 4) % 2) * 2 + row % 2
     out[...] = dot(one_hot(row_code == code), halves).astype(BF16)
+    copies[7].wait()
 
 
 def attend_kernel(pieces, lengths, slot_of, cache, out):
@@ -98,9 +114,9 @@
     step_of_row = iota((group, 1), 0) % STEPS
     outputs = []
     for slot in range(2):
-        length = jnp.int32(0)
-        for r in range(REQ):
-            length = length + jnp.where(slot_of[r] == first_slot + slot, lengths[r], 0)
+        mine = slot_of[...] == first_slot + slot
+        length = jnp.sum(jnp.where(mine, lengths[...].astype(F32), 0.0), axis=1, keepdims=True)
+        length = length.astype(jnp.int32)
         rows = whole[slot * 2 : slot * 2 + 2]
         query = jnp.concatenate([rows[:, h * LANES : (h + 1) * LANES] for h in range(heads)], axis=0)
         fresh_key = rows[:, 1024 : 1024 + LANES]
@@ -164,7 +180,9 @@
     first_out[...] = first
     normed, tile = gain_rows(first.astype(F32), gain[...])
     main = dot(normed, w_main[...]).astype(BF16)
-    steps = dot(normed, w_step[...]).astype(BF16)
+    steps = lax.dot_general(
+        normed, w_step[...], (((1,), (1,)), ((), ())), preferred_element_type=F32
+    ).astype(BF16)
     spare = jnp.zeros_like(tile)
     steps = jnp.concatenate([steps, spare[:, : LANES - HEADS]], axis=1)
     state = 2 * INNER
@@ -194,11 +212,14 @@
     summed = summed * jnp.concatenate([scale] * 4, axis=0)
 
     def conved(now, cut):
-        window = jnp.concatenate([conv_state[:, cut], now], axis=0)
-        total = conv_bias[:, cut]
-        for k in range(4):
-            total = total + conv_weight[k : k + 1, cut] * window[k : k + 2]
-        return silu(total)
+        window = [conv_state[k, :, cut] for k in range(3)] + [now[0:1], now[1:2]]
+        totals = []
+        for s in range(STEPS):
+            total = conv_bias[:, cut]
+            for k in range(4):
+                total = total + conv_weight[k, :, cut] * window[s + k]
+            totals.append(total)
+        return silu(jnp.concatenate(totals, axis=0))
 
     xs = jnp.concatenate(
         [
@@ -272,20 +293,31 @@
 
 
 def last_kernel(pieces, second, out):
-    out[...] = (sum_pieces(pieces, TP) + second[...].astype(F32)).astype(BF16)
-
-
-def call(kernel, out_shapes, *operands, smem=()):
-    vmem = pl.BlockSpec(memory_space=pltpu.VMEM)
-    scalar = pl.BlockSpec(memory_space=pltpu.SMEM)
-    shapes = [jax.ShapeDtypeStruct(shape, BF16) for shape in out_shapes]
-    return pl.pallas_call(
+    total = sum_pieces(pieces, TP) + second[...].astype(F32)
+    out[...] = total.reshape(out.shape).astype(BF16)
+
+
+def call(kernel, outs, *operands, near=False, scratch=(), cost=None):
+    space = pltpu.HBM if near else pltpu.VMEM
+    shapes = [
+        jax.ShapeDtypeStruct(out, BF16) if isinstance(out, tuple) else
+        jax.ShapeDtypeStruct(out.shape, out.dtype)
+        for out in outs
+    ]
+    if cost is None:
+        cost = sum(x.size * x.dtype.itemsize for x in operands)
+    if near:
+        operands = [pltpu.with_memory_space_constraint(x, pltpu.HBM) for x in operands]
+    result = pl.pallas_call(
         kernel,
-        out_shape=shapes[0] if len(shapes) == 1 else shapes,
-        in_specs=[scalar if k in smem else vmem for k in range(len(operands))],
-        out_specs=vmem if len(shapes) == 1 else [vmem] * len(shapes),
+        out_shape=shapes,
+        in_specs=[pl.BlockSpec(memory_space=space)] * len(operands),
+        out_specs=[pl.BlockSpec(memory_space=pltpu.VMEM)] * len(shapes),
+        scratch_shapes=scratch,
+        cost_estimate=pl.CostEstimate(flops=0, bytes_accessed=cost, transcendentals=0),
         compiler_params=pltpu.CompilerParams(vmem_limit_bytes=24 * 1024 * 1024),
     )(*operands)
+    return result[0] if len(shapes) == 1 else result
 
 
 def exchange(values, axis, pieces):
@@ -320,33 +352,35 @@
     w_up,
     w_down,
 ):
-    rows = hidden.reshape(ROWS, -1)
-    width = rows.shape[1]
+    width = hidden.shape[2]
     slot_row = slot_of.reshape(1, REQ)
     owned = ATTN * 8
 
     def row(x):
         return x.reshape(1, -1)
 
-    pieces = call(
-        qkv_kernel, [(owned, QKV_HALF)],
-        rows, slot_row, row(attn_gain), w_query, key_matrix, value_matrix,
-    )
-    pieces = exchange(pieces, "attn", ATTN)
-    pieces = call(
-        attend_kernel, [(owned, 512)], pieces, lengths, slot_of, kv_cache, smem=(1, 2)
-    )
+    length_row = lengths.reshape(1, REQ)
+    kept = (hidden, row(attn_gain), key_matrix, value_matrix, w_query)
+    pieces, rows, slot_row, length_row, cache = call(
+        qkv_kernel, [(owned, QKV_HALF), (ROWS, width), slot_row, length_row, kv_cache],
+        hidden, row(attn_gain), slot_row, length_row, key_matrix, value_matrix, w_query, kv_cache,
+        near=True,
+        scratch=[pltpu.VMEM(x.shape, x.dtype) for x in kept] + [pltpu.SemaphoreType.DMA((8,))],
+        cost=16 * 1024 * 1024,
+    )
+    pieces = exchange(pieces, "attn", ATTN)
+    pieces = call(attend_kernel, [(owned, 512)], pieces, length_row, slot_row, cache)
     pieces = exchange(pieces, "attn", ATTN)
     pieces = call(attn_out_kernel, [(TP * ROWS, width)], pieces, slot_row, w_attn_out)
     pieces = exchange(pieces, "tp", TP)
     pieces, first = call(
         mix_in_kernel, [(owned, MIX_QUARTER), (ROWS, width)],
-        pieces, rows, row(mamba_gain), w_mamba_in.reshape(width, -1), w_mamba_dt,
+        pieces, rows, row(mamba_gain), w_mamba_in.reshape(width, -1), w_mamba_dt.T,
     )
     pieces = exchange(pieces, "attn", ATTN)
     pieces = call(
         mamba_kernel, [(owned, 512)],
-        pieces, conv_weight.reshape(4, -1), conv_bias, conv_state.reshape(3, -1),
+        pieces, conv_weight, conv_bias, conv_state.reshape(3, 1, -1),
         ssm_state.reshape(INNER, STATES), row(a_log), row(dt_bias), row(skip_gain), group_gain,
     )
     pieces = exchange(pieces, "attn", ATTN)
@@ -360,7 +394,7 @@
     pieces = exchange(pieces, "attn", ATTN)
     pieces = call(project_out_kernel, [(TP * ROWS, width)], pieces, w_down)
     pieces = exchange(pieces, "tp", TP)
-    return call(last_kernel, [(ROWS, width)], pieces, second).reshape(hidden.shape)
+    return call(last_kernel, [hidden.shape], pieces, second)
 
 
 def solution(mesh):

time: 169 us -> 159 us (0.941)
  blocking collectives: 112 us -> 149 us
  waiting for transfers between devices: 25.2 us -> 0 us
  starting transfers between devices: 12.4 us -> 0 us
  local copies, waits for them, and re-layouts: 10.1 us -> 0.1 us
    all_to_all x7 -> x9, blocking collectives: 112 us -> 149 us  [exchange(): return lax.all_to_all(cut, axis, 0, 0).reshape(rows, columns)]
    all_to_all x2 -> x0, waiting for transfers between devices: 25.2 us -> none  [exchange(): return lax.all_to_all(cut, axis, 0, 0).reshape(rows, columns)]
    all_to_all x2 -> x0, starting transfers between devices: 12.4 us -> none  [exchange(): return lax.all_to_all(cut, axis, 0, 0).reshape(rows, columns)]
    unnamed x49 -> x32, local copies, waits for them, and re-layouts: 8.68 us -> 0.1 us
  transfers between devices with their start and end apart: 2 -> 0, of which waited for: 2 -> 0; matrix products, arithmetic and copies ran while one was open for 0% -> 0% of each run, Pallas kernels for 0% -> 0%
where the time goes in v3:
time: 159 us
  blocking collectives  149 us (94%)
  Pallas kernels  9.03 us (6%)
    all_to_all x9, blocking collectives, exchange(): return lax.all_to_all(cut, axis, 0, 0).reshape(rows, columns)  149 us
    pallas_call x10, Pallas kernels, call(): pl.pallas_call(kernel, out_shape=shapes, in_specs=[pl.BlockSpec(memory_sp...  9.03 us

profile of v3, /device:TPU:1, one launch (start us, length us, event | category | flops | bytes accessed | tf_op | source)
XLA Modules:
  0.0 158.5 jit_solution(2242190925197707241)
XLA Ops:
  0.0 2.6 %shard_map.226 = (bf16[256,768]{1,0:T(8,128)(2,1)S(1)}, bf16[64,256]{1,0:T(8,128)(2,1)S(1)}, s32[1,32]{1,0:T(1,128)S(1)}, s32[1,32]{1,0:T(1,128)S(1)}, bf16[2,2,4096,128]{3,2,1,0:T(8,128)(2,1)S(1)}) custom-call(bf16[32,2,256]{2,1,0:T(2,128)(2,1)} %hidden.1, f32[1,256]{1,0:T(1,128)} %bitcast.57, s32[1,32]{1,0:T(1,128)} %bitcast.58, s32[1,32]{1,0:T(1,128)} %bitcast.59, ...), custom_call_target="tpu_custom_call" | custom-call | bytes 16777216 | tf_op jit(solution)/shard_map/pallas_call | solution.py:311
  2.6 0.0 copy-start.5
  2.6 0.0 copy-start.11
  2.6 25.7 %all_to_all.45 = bf16[32,8,768]{2,1,0:T(8,128)(2,1)S(1)} all-to-all(bf16[32,8,768]{2,1,0:T(8,128)(2,1)S(1)} %bitcast.48), channel_id=1, replica_groups=mesh['attn'=32,'tp'=8] {'attn'}, dimensions={0} | all-to-all | bytes 786432 | tf_op jit(solution)/shard_map/all_to_all | solution.py:326
  28.3 1.5 shard_map.227
  29.9 0.0 copy-start.6
  29.9 0.0 copy-start.7
  29.9 0.0 copy-start.10
  30.0 15.3 %all_to_all.46 = bf16[32,8,512]{2,1,0:T(8,128)(2,1)S(1)} all-to-all(bf16[32,8,512]{2,1,0:T(8,128)(2,1)S(1)} %bitcast.46), channel_id=1, replica_groups=mesh['attn'=32,'tp'=8] {'attn'}, dimensions={0} | all-to-all | bytes 524288 | tf_op jit(solution)/shard_map/all_to_all | solution.py:326
  45.3 0.6 shard_map.228
  45.9 14.7 %all_to_all.47 = bf16[8,64,256]{2,1,0:T(8,128)(2,1)S(1)} all-to-all(bf16[8,64,256]{2,1,0:T(8,128)(2,1)S(1)} %bitcast.41), channel_id=1, replica_groups=mesh['attn'=32,'tp'=8] {'tp'}, dimensions={0} | all-to-all | bytes 524288 | tf_op jit(solution)/shard_map/all_to_all | solution.py:326
  60.6 0.7 shard_map.229
  61.4 21.5 %all_to_all.48 = bf16[32,8,1280]{2,1,0:T(8,128)(2,1)S(1)} all-to-all(bf16[32,8,1280]{2,1,0:T(8,128)(2,1)S(1)} %bitcast.47), channel_id=1, replica_groups=mesh['attn'=32,'tp'=8] {'attn'}, dimensions={0} | all-to-all | bytes 1310720 | tf_op jit(solution)/shard_map/all_to_all | solution.py:326
  83.0 1.2 shard_map.230
  84.2 16.0 %all_to_all.49 = bf16[32,8,512]{2,1,0:T(8,128)(2,1)S(1)} all-to-all(bf16[32,8,512]{2,1,0:T(8,128)(2,1)S(1)} %bitcast.36), channel_id=1, replica_groups=mesh['attn'=32,'tp'=8] {'attn'}, dimensions={0} | all-to-all | bytes 524288 | tf_op jit(solution)/shard_map/all_to_all | solution.py:326
  100.2 0.5 shard_map.231
  100.7 12.7 %all_to_all.50 = bf16[8,64,256]{2,1,0:T(8,128)(2,1)S(1)} all-to-all(bf16[8,64,256]{2,1,0:T(8,128)(2,1)S(1)} %bitcast.43), channel_id=1, replica_groups=mesh['attn'=32,'tp'=8] {'tp'}, dimensions={0} | all-to-all | bytes 524288 | tf_op jit(solution)/shard_map/all_to_all | solution.py:326
  113.4 0.5 shard_map.232
  113.9 15.1 %all_to_all.51 = bf16[32,8,640]{2,1,0:T(8,128)(2,1)S(1)} all-to-all(bf16[32,8,640]{2,1,0:T(8,128)(2,1)S(1)} %bitcast.49), channel_id=1, replica_groups=mesh['attn'=32,'tp'=8] {'attn'}, dimensions={0} | all-to-all | bytes 655360 | tf_op jit(solution)/shard_map/all_to_all | solution.py:326
  129.1 0.2 shard_map.233
  129.3 15.4 %all_to_all.52 = bf16[32,8,512]{2,1,0:T(8,128)(2,1)S(1)} all-to-all(bf16[32,8,512]{2,1,0:T(8,128)(2,1)S(1)} %bitcast.38), channel_id=1, replica_groups=mesh['attn'=32,'tp'=8] {'attn'}, dimensions={0} | all-to-all | bytes 524288 | tf_op jit(solution)/shard_map/all_to_all | solution.py:326
  144.7 0.5 shard_map.234
  145.2 12.7 %all_to_all.53 = bf16[8,64,256]{2,1,0:T(8,128)(2,1)S(1)} all-to-all(bf16[8,64,256]{2,1,0:T(8,128)(2,1)S(1)} %bitcast.45), channel_id=1, replica_groups=mesh['attn'=32,'tp'=8] {'tp'}, dimensions={0} | all-to-all | bytes 524288 | tf_op jit(solution)/shard_map/all_to_all | solution.py:326
  157.9 0.7 shard_map.235
  (27 shorter events, 0.1 us)
Async XLA Ops:
  2.6 42.7 %copy-start.5 = (bf16[1024,256]{1,0:T(8,128)(2,1)S(1)}, bf16[1024,256]{1,0:T(8,128)(2,1)}, u32[]{:S(2)}) copy-start(bf16[1024,256]{1,0:T(8,128)(2,1)} %weight.3) | copy-start | bytes 1572868
  2.6 58.0 %copy-start = (bf16[256,1,4608]{2,0,1:T(8,128)(2,1)S(1)}, bf16[256,1,4608]{2,0,1:T(8,128)(2,1)}, u32[]{:S(2)}) copy-start(bf16[256,1,4608]{2,0,1:T(8,128)(2,1)} %param.34) | copy-start | bytes 7077892
  2.6 58.0 %copy-start.8 = (bf16[256,32]{0,1:T(8,128)(2,1)S(1)}, bf16[256,32]{0,1:T(8,128)(2,1)}, u32[]{:S(2)}) copy-start(bf16[256,32]{0,1:T(8,128)(2,1)} %param.35) | copy-start | bytes 49156
  2.6 58.0 %copy-start.11 = (f32[256]{0:T(256)S(1)}, f32[256]{0:T(256)}, u32[]{:S(2)}) copy-start(f32[256]{0:T(256)} %param.33) | copy-start | bytes 3076
  29.9 53.0 %copy-start.1 = (f32[1,32,64,256]{3,2,1,0:T(8,128)S(1)}, f32[1,32,64,256]{3,2,1,0:T(8,128)}, u32[]{:S(2)}) copy-start(f32[1,32,64,256]{3,2,1,0:T(8,128)} %param.40) | copy-start | bytes 6291460
  29.9 53.0 %copy-start.6 = (f32[4,1,2560]{2,1,0:T(1,128)S(1)}, f32[4,1,2560]{2,1,0:T(1,128)}, u32[]{:S(2)}) copy-start(f32[4,1,2560]{2,1,0:T(1,128)} %conv_weight.1) | copy-start | bytes 122884
  29.9 53.0 %copy-start.7 = (f32[1,3,1,2560]{3,2,1,0:T(1,128)S(1)}, f32[1,3,1,2560]{3,2,1,0:T(1,128)}, u32[]{:S(2)}) copy-start(f32[1,3,1,2560]{3,2,1,0:T(1,128)} %param.39) | copy-start | bytes 92164
  29.9 53.0 %copy-start.9 = (f32[1,2560]{1,0:T(1,128)S(1)}, f32[1,2560]{1,0:T(1,128)}, u32[]{:S(2)}) copy-start(f32[1,2560]{1,0:T(1,128)} %conv_bias.1) | copy-start | bytes 30724
  29.9 53.0 %copy-start.10 = (f32[1,2048]{1,0:T(1,128)S(1)}, f32[1,2048]{1,0:T(1,128)}, u32[]{:S(2)}) copy-start(f32[1,2048]{1,0:T(1,128)} %group_gain.1) | copy-start | bytes 24580
  29.9 53.0 %copy-start.13 = (f32[32]{0:T(128)S(1)}, f32[32]{0:T(128)}, u32[]{:S(2)}) copy-start(f32[32]{0:T(128)} %param.41) | copy-start | bytes 388
  30.0 53.0 %copy-start.14 = (f32[32]{0:T(128)S(1)}, f32[32]{0:T(128)}, u32[]{:S(2)}) copy-start(f32[32]{0:T(128)} %param.42) | copy-start | bytes 388
  30.0 53.0 %copy-start.15 = (f32[32]{0:T(128)S(1)}, f32[32]{0:T(128)}, u32[]{:S(2)}) copy-start(f32[32]{0:T(128)} %param.43) | copy-start | bytes 388
  45.9 54.3 %copy-start.2 = (bf16[2048,256]{1,0:T(8,128)(2,1)S(1)}, bf16[2048,256]{1,0:T(8,128)(2,1)}, u32[]{:S(2)}) copy-start(bf16[2048,256]{1,0:T(8,128)(2,1)} %weight.4) | copy-start | bytes 3145732
  61.4 52.0 %copy-start.4 = (bf16[256,2048]{1,0:T(8,128)(2,1)S(1)}, bf16[256,2048]{1,0:T(8,128)(2,1)}, u32[]{:S(2)}) copy-start(bf16[256,2048]{1,0:T(8,128)(2,1)} %w_up.1) | copy-start | bytes 3145732
  61.4 52.0 %copy-start.12 = (f32[256]{0:T(256)S(1)}, f32[256]{0:T(256)}, u32[]{:S(2)}) copy-start(f32[256]{0:T(256)} %param.45) | copy-start | bytes 3076
  83.0 61.7 %copy-start.3 = (bf16[2048,256]{1,0:T(8,128)(2,1)S(1)}, bf16[2048,256]{1,0:T(8,128)(2,1)}, u32[]{:S(2)}) copy-start(bf16[2048,256]{1,0:T(8,128)(2,1)} %weight.5) | copy-start | bytes 3145732

commit v4 on v3

--- a/solution.py
+++ b/solution.py
@@ -15,10 +15,7 @@
 ATTN = 32
 TP = 8
 WIDTH = 8192
-QKV_HALF = 768
-UP_QUARTER = 512
-MIX_QUARTER = 1280
-FF_QUARTER = 640
+SLOTS = 64
 INNER = 2048
 STATES = 256
 HEADS = 32
@@ -89,25 +86,20 @@
     key = dot(normed, key_here[...]).astype(BF16)
     value = dot(normed, value_here[...]).astype(BF16)
     query = dot(normed, query_here[...]).astype(BF16)
-    spare = jnp.zeros_like(tile)
-    second = jnp.concatenate([query[:, QKV_HALF:], key, value, tile, spare], axis=1)
-    halves = jnp.concatenate([query[:, :QKV_HALF], second], axis=0)
-    column = iota((1, 2 * ROWS), 1)
-    code = slots_by_row(slots_out, 2 * ROWS) * 4 + (column // ROWS) * 2 + column % STEPS
-    row = iota((ATTN * 8, 2 * ROWS), 0)
-    row_code = ((row // 8) * 2 + (row // 2) % 2) * 4 + ((row // 4) % 2) * 2 + row % 2
-    out[...] = dot(one_hot(row_code == code), halves).astype(BF16)
+    whole = jnp.concatenate([query, key, value, tile], axis=1)
+    column = iota((1, ROWS), 1)
+    code = slots_by_row(slots_out, ROWS) * 2 + column % STEPS
+    chosen = one_hot(iota((2 * SLOTS, ROWS), 0) == code)
+    out[...] = dot(chosen, whole).reshape(out.shape).astype(BF16)
     copies[7].wait()
 
 
 def attend_kernel(pieces, lengths, slot_of, cache, out):
     first_slot = lax.axis_index("attn") * 2
-    summed = sum_pieces(pieces, ATTN)
-    low, high = summed[0:4], summed[4:8]
-    scale = scale_of(high[:, 512 : 512 + LANES])
-    low = (low * scale).astype(BF16).astype(F32)
-    high = (high * scale).astype(BF16).astype(F32)
-    whole = jnp.concatenate([low, high], axis=1)
+    summed = jnp.sum(pieces[...].astype(F32), axis=0)
+    keys_at = 8 * HEAD_SIZE
+    columns = keys_at + 2 * HEAD_SIZE
+    whole = (summed[:, :columns] * scale_of(summed[:, columns:])).astype(BF16).astype(F32)
     heads = 8
     factor = HEAD_SIZE ** (-0.5)
     group = heads * STEPS
@@ -119,8 +111,8 @@
         length = length.astype(jnp.int32)
         rows = whole[slot * 2 : slot * 2 + 2]
         query = jnp.concatenate([rows[:, h * LANES : (h + 1) * LANES] for h in range(heads)], axis=0)
-        fresh_key = rows[:, 1024 : 1024 + LANES]
-        fresh_value = rows[:, 1024 + LANES : 1024 + 2 * LANES]
+        fresh_key = rows[:, keys_at : keys_at + HEAD_SIZE]
+        fresh_value = rows[:, keys_at + HEAD_SIZE :]
         scores = (
             lax.dot_general(
                 query.astype(BF16), cache[slot, 0], (((1,), (1,)), ((), ())), preferred_element_type=F32
@@ -167,37 +159,16 @@
     write_copies(out, total, TP)
 
 
-def by_owner(quarters):
-    stacked = jnp.concatenate(quarters, axis=0)
-    row = iota((ATTN * 8, 4 * ROWS), 0)
-    column = iota((ATTN * 8, 4 * ROWS), 1)
-    source = ((row // 2) % 4) * ROWS + (row // 8) * 2 + row % 2
-    return dot(one_hot(source == column), stacked).astype(BF16)
-
-
 def mix_in_kernel(pieces, hidden, gain, w_main, w_step, out, first_out):
     first = (sum_pieces(pieces, TP) + hidden[...].astype(F32)).astype(BF16)
     first_out[...] = first
     normed, tile = gain_rows(first.astype(F32), gain[...])
-    main = dot(normed, w_main[...]).astype(BF16)
+    main = dot(normed, w_main[...])
     steps = lax.dot_general(
         normed, w_step[...], (((1,), (1,)), ((), ())), preferred_element_type=F32
-    ).astype(BF16)
-    spare = jnp.zeros_like(tile)
-    steps = jnp.concatenate([steps, spare[:, : LANES - HEADS]], axis=1)
-    state = 2 * INNER
-    extra = (
-        [main[:, state : state + STATES]],
-        [main[:, state + STATES : state + 2 * STATES]],
-        [steps, tile],
-        [spare, spare],
-    )
-    quarters = []
-    for q in range(4):
-        cut = slice(q * 512, (q + 1) * 512)
-        parts = [main[:, :INNER][:, cut], main[:, INNER : 2 * INNER][:, cut]]
-        quarters.append(jnp.concatenate(parts + extra[q], axis=1))
-    out[...] = by_owner(quarters)
+    )
+    both = jnp.concatenate([main, steps, tile[:, : LANES - HEADS].astype(F32)], axis=1)
+    out[...] = both.reshape(out.shape).astype(BF16)
 
 
 def silu(x):
@@ -207,9 +178,11 @@
 def mamba_kernel(
     pieces, conv_weight, conv_bias, conv_state, state, a_log, dt_bias, skip_gain, group_gain, out
 ):
-    summed = sum_pieces(pieces, ATTN)
-    scale = scale_of(summed[4:6, 1024 + LANES :])
-    summed = summed * jnp.concatenate([scale] * 4, axis=0)
+    summed = jnp.sum(pieces[...].astype(F32), axis=0)
+    state_at = 2 * INNER
+    steps_at = state_at + 2 * STATES
+    last = summed[:, steps_at:]
+    summed = summed * scale_of(last[:, HEADS:])
 
     def conved(now, cut):
         window = [conv_state[k, :, cut] for k in range(3)] + [now[0:1], now[1:2]]
@@ -221,17 +194,11 @@
             totals.append(total)
         return silu(jnp.concatenate(totals, axis=0))
 
-    xs = jnp.concatenate(
-        [
-            conved(summed[q * 2 : q * 2 + 2, 512:1024], slice(q * 512, (q + 1) * 512))
-            for q in range(4)
-        ],
-        axis=1,
-    )
-    b_in = conved(summed[0:2, 1024:1280], slice(INNER, INNER + STATES))
-    c_out = conved(summed[2:4, 1024:1280], slice(INNER + STATES, INNER + 2 * STATES))
-    gate = jnp.concatenate([summed[q * 2 : q * 2 + 2, 0:512] for q in range(4)], axis=1)
-    raw = summed[4:6, 1024 : 1024 + HEADS] + dt_bias[...]
+    xs = conved(summed[:, INNER:state_at], slice(0, INNER))
+    b_in = conved(summed[:, state_at : state_at + STATES], slice(INNER, INNER + STATES))
+    c_out = conved(summed[:, state_at + STATES : steps_at], slice(INNER + STATES, INNER + 2 * STATES))
+    gate = summed[:, :INNER]
+    raw = summed[:, steps_at : steps_at + HEADS] + dt_bias[...]
     step = jnp.maximum(raw, 0.0) + jnp.log1p(jnp.exp(-jnp.abs(raw)))
     decay = jnp.exp(-step * jnp.exp(a_log[...]))
     d0, d1, s0, s1 = decay[0:1], decay[1:2], step[0:1], step[1:2]
@@ -243,10 +210,10 @@
     whole = state[...]
     high = whole.astype(BF16)
     low = (whole - high.astype(F32)).astype(BF16)
-    last = (((1,), (1,)), ((), ()))
+    along = (((1,), (1,)), ((), ()))
     both = jnp.concatenate([c_high, c_low], axis=0)
-    by_high = lax.dot_general(both, high, last, preferred_element_type=F32)
-    by_low = lax.dot_general(c_high, low, last, preferred_element_type=F32)
+    by_high = lax.dot_general(both, high, along, preferred_element_type=F32)
+    by_low = lax.dot_general(c_high, low, along, preferred_element_type=F32)
     read_old = by_high[0:2] + by_high[2:4] + by_low
     b0c0 = jnp.sum(b_in[0:1] * c_out[0:1], axis=-1, keepdims=True)
     b0c1 = jnp.sum(b_in[0:1] * c_out[1:2], axis=-1, keepdims=True)
@@ -277,19 +244,17 @@
     second = (sum_pieces(pieces, TP) + first[...].astype(F32)).astype(BF16)
     second_out[...] = second
     normed, tile = gain_rows(second.astype(F32), gain[...])
-    up = dot(normed, w_up[...]).astype(BF16)
-    out[...] = by_owner(
-        [
-            jnp.concatenate([up[:, q * UP_QUARTER : (q + 1) * UP_QUARTER], tile], axis=1)
-            for q in range(4)
-        ]
-    )
+    up = dot(normed, w_up[...])
+    both = jnp.concatenate([up, tile.astype(F32)], axis=1)
+    out[...] = both.reshape(out.shape).astype(BF16)
 
 
 def active_kernel(pieces, out):
-    summed = sum_pieces(pieces, ATTN)
-    lifted = jnp.maximum(summed[:, :UP_QUARTER] * scale_of(summed[:, UP_QUARTER:]), 0.0)
-    write_copies(out, lifted * lifted, ATTN)
+    summed = jnp.sum(pieces[...].astype(F32), axis=0)
+    lifted = jnp.maximum(summed[:, :INNER] * scale_of(summed[:, INNER:]), 0.0)
+    active = lifted * lifted
+    piece = jnp.concatenate([active[:, q * 512 : (q + 1) * 512] for q in range(4)], axis=0)
+    write_copies(out, piece, ATTN)
 
 
 def last_kernel(pieces, second, out):
@@ -362,22 +327,22 @@
     length_row = lengths.reshape(1, REQ)
     kept = (hidden, row(attn_gain), key_matrix, value_matrix, w_query)
     pieces, rows, slot_row, length_row, cache = call(
-        qkv_kernel, [(owned, QKV_HALF), (ROWS, width), slot_row, length_row, kv_cache],
+        qkv_kernel, [(ATTN, 4, 1408), (ROWS, width), slot_row, length_row, kv_cache],
         hidden, row(attn_gain), slot_row, length_row, key_matrix, value_matrix, w_query, kv_cache,
         near=True,
         scratch=[pltpu.VMEM(x.shape, x.dtype) for x in kept] + [pltpu.SemaphoreType.DMA((8,))],
         cost=16 * 1024 * 1024,
     )
-    pieces = exchange(pieces, "attn", ATTN)
+    pieces = lax.all_to_all(pieces, "attn", 0, 0)
     pieces = call(attend_kernel, [(owned, 512)], pieces, length_row, slot_row, cache)
     pieces = exchange(pieces, "attn", ATTN)
     pieces = call(attn_out_kernel, [(TP * ROWS, width)], pieces, slot_row, w_attn_out)
     pieces = exchange(pieces, "tp", TP)
     pieces, first = call(
-        mix_in_kernel, [(owned, MIX_QUARTER), (ROWS, width)],
+        mix_in_kernel, [(ATTN, STEPS, 2 * INNER + 2 * STATES + LANES), (ROWS, width)],
         pieces, rows, row(mamba_gain), w_mamba_in.reshape(width, -1), w_mamba_dt.T,
     )
-    pieces = exchange(pieces, "attn", ATTN)
+    pieces = lax.all_to_all(pieces, "attn", 0, 0)
     pieces = call(
         mamba_kernel, [(owned, 512)],
         pieces, conv_weight, conv_bias, conv_state.reshape(3, 1, -1),
@@ -387,9 +352,9 @@
     pieces = call(project_out_kernel, [(TP * ROWS, width)], pieces, w_mamba_out)
     pieces = exchange(pieces, "tp", TP)
     pieces, second = call(
-        up_kernel, [(owned, FF_QUARTER), (ROWS, width)], pieces, first, row(mlp_gain), w_up
-    )
-    pieces = exchange(pieces, "attn", ATTN)
+        up_kernel, [(ATTN, STEPS, INNER + LANES), (ROWS, width)], pieces, first, row(mlp_gain), w_up
+    )
+    pieces = lax.all_to_all(pieces, "attn", 0, 0)
     pieces = call(active_kernel, [(owned, 512)], pieces)
     pieces = exchange(pieces, "attn", ATTN)
     pieces = call(project_out_kernel, [(TP * ROWS, width)], pieces, w_down)

time: 159 us -> 157 us (0.987)
  blocking collectives: 149 us -> 146 us
    all_to_all x9 -> x6, blocking collectives: 149 us -> 87 us  [exchange(): return lax.all_to_all(cut, axis, 0, 0).reshape(rows, columns)]
    all_to_all x0 -> x3, blocking collectives: none -> 59.3 us  [on_device(): pieces = lax.all_to_all(pieces, 'attn', 0, 0)]
where the time goes in v4:
time: 157 us; the launch traced here: 156 us
  blocking collectives  146 us (93%)
  Pallas kernels  9.52 us (6%)
    all_to_all x6, blocking collectives, exchange(): return lax.all_to_all(cut, axis, 0, 0).reshape(rows, columns)  87 us
    all_to_all x3, blocking collectives, on_device(): pieces = lax.all_to_all(pieces, 'attn', 0, 0)  59.3 us
    pallas_call x10, Pallas kernels, call(): pl.pallas_call(kernel, out_shape=shapes, in_specs=[pl.BlockSpec(memory_sp...  9.52 us

profile of v4, /device:TPU:1, one launch (start us, length us, event | category | flops | bytes accessed | tf_op | source)
XLA Modules:
  0.0 156.2 jit_solution(844950324890528660)
XLA Ops:
  0.0 2.6 %shard_map.226 = (bf16[32,4,1408]{2,1,0:T(4,128)(2,1)S(1)}, bf16[64,256]{1,0:T(8,128)(2,1)S(1)}, s32[1,32]{1,0:T(1,128)S(1)}, s32[1,32]{1,0:T(1,128)S(1)}, bf16[2,2,4096,128]{3,2,1,0:T(8,128)(2,1)S(1)}) custom-call(bf16[32,2,256]{2,1,0:T(2,128)(2,1)} %hidden.1, f32[1,256]{1,0:T(1,128)} %bitcast.45, s32[1,32]{1,0:T(1,128)} %bitcast.46, s32[1,32]{1,0:T(1,128)} %bitcast.47, ...), custom_call_target="tpu_custom_call" | custom-call | bytes 16777216 | tf_op jit(solution)/shard_map/pallas_call | solution.py:276
  2.6 0.0 copy-start.5
  2.6 0.0 copy-start.11
  2.6 25.3 %all_to_all.45.pieces = bf16[32,4,1408]{2,1,0:T(4,128)(2,1)S(1)} all-to-all(bf16[32,4,1408]{2,1,0:T(4,128)(2,1)S(1)} %get-tuple-element.14), channel_id=1, replica_groups=mesh['attn'=32,'tp'=8] {'attn'}, dimensions={0} | all-to-all | bytes 720896 | tf_op jit(solution)/shard_map/all_to_all | solution.py:336
  27.9 1.5 shard_map.227
  29.5 0.0 copy-start.6
  29.5 0.0 copy-start.7
  29.5 0.0 copy-start.13
  29.6 15.1 %all_to_all.46 = bf16[32,8,512]{2,1,0:T(8,128)(2,1)S(1)} all-to-all(bf16[32,8,512]{2,1,0:T(8,128)(2,1)S(1)} %bitcast.37), channel_id=1, replica_groups=mesh['attn'=32,'tp'=8] {'attn'}, dimensions={0} | all-to-all | bytes 524288 | tf_op jit(solution)/shard_map/all_to_all | solution.py:291
  44.7 0.6 shard_map.228
  45.3 14.6 %all_to_all.47 = bf16[8,64,256]{2,1,0:T(8,128)(2,1)S(1)} all-to-all(bf16[8,64,256]{2,1,0:T(8,128)(2,1)S(1)} %bitcast.32), channel_id=1, replica_groups=mesh['attn'=32,'tp'=8] {'tp'}, dimensions={0} | all-to-all | bytes 524288 | tf_op jit(solution)/shard_map/all_to_all | solution.py:291
  60.0 0.8 shard_map.229
  60.8 20.2 %all_to_all.48.pieces = bf16[32,2,4736]{2,1,0:T(2,128)(2,1)S(1)} all-to-all(bf16[32,2,4736]{2,1,0:T(2,128)(2,1)S(1)} %get-tuple-element.19), channel_id=1, replica_groups=mesh['attn'=32,'tp'=8] {'attn'}, dimensions={0} | all-to-all | bytes 1212416 | tf_op jit(solution)/shard_map/all_to_all | solution.py:345
  81.0 1.5 shard_map.230
  82.5 16.3 %all_to_all.49 = bf16[32,8,512]{2,1,0:T(8,128)(2,1)S(1)} all-to-all(bf16[32,8,512]{2,1,0:T(8,128)(2,1)S(1)} %bitcast.27), channel_id=1, replica_groups=mesh['attn'=32,'tp'=8] {'attn'}, dimensions={0} | all-to-all | bytes 524288 | tf_op jit(solution)/shard_map/all_to_all | solution.py:291
  98.8 0.5 shard_map.231
  99.3 12.7 %all_to_all.50 = bf16[8,64,256]{2,1,0:T(8,128)(2,1)S(1)} all-to-all(bf16[8,64,256]{2,1,0:T(8,128)(2,1)S(1)} %bitcast.34), channel_id=1, replica_groups=mesh['attn'=32,'tp'=8] {'tp'}, dimensions={0} | all-to-all | bytes 524288 | tf_op jit(solution)/shard_map/all_to_all | solution.py:291
  112.0 0.5 shard_map.232
  112.5 13.8 %all_to_all.51.pieces = bf16[32,2,2176]{2,1,0:T(2,128)(2,1)S(1)} all-to-all(bf16[32,2,2176]{2,1,0:T(2,128)(2,1)S(1)} %get-tuple-element.21), channel_id=1, replica_groups=mesh['attn'=32,'tp'=8] {'attn'}, dimensions={0} | all-to-all | bytes 557056 | tf_op jit(solution)/shard_map/all_to_all | solution.py:357
  126.3 0.4 shard_map.233
  126.7 15.6 %all_to_all.52 = bf16[32,8,512]{2,1,0:T(8,128)(2,1)S(1)} all-to-all(bf16[32,8,512]{2,1,0:T(8,128)(2,1)S(1)} %bitcast.29), channel_id=1, replica_groups=mesh['attn'=32,'tp'=8] {'attn'}, dimensions={0} | all-to-all | bytes 524288 | tf_op jit(solution)/shard_map/all_to_all | solution.py:291
  142.3 0.5 shard_map.234
  142.8 12.7 %all_to_all.53 = bf16[8,64,256]{2,1,0:T(8,128)(2,1)S(1)} all-to-all(bf16[8,64,256]{2,1,0:T(8,128)(2,1)S(1)} %bitcast.36), channel_id=1, replica_groups=mesh['attn'=32,'tp'=8] {'tp'}, dimensions={0} | all-to-all | bytes 524288 | tf_op jit(solution)/shard_map/all_to_all | solution.py:291
  155.5 0.7 shard_map.235
  (27 shorter events, 0.1 us)
Async XLA Ops:
  2.6 42.1 %copy-start.5 = (bf16[1024,256]{1,0:T(8,128)(2,1)S(1)}, bf16[1024,256]{1,0:T(8,128)(2,1)}, u32[]{:S(2)}) copy-start(bf16[1024,256]{1,0:T(8,128)(2,1)} %weight.3) | copy-start | bytes 1572868
  2.6 57.4 %copy-start = (bf16[256,1,4608]{2,0,1:T(8,128)(2,1)S(1)}, bf16[256,1,4608]{2,0,1:T(8,128)(2,1)}, u32[]{:S(2)}) copy-start(bf16[256,1,4608]{2,0,1:T(8,128)(2,1)} %param.34) | copy-start | bytes 7077892
  2.6 57.3 %copy-start.8 = (bf16[256,32]{0,1:T(8,128)(2,1)S(1)}, bf16[256,32]{0,1:T(8,128)(2,1)}, u32[]{:S(2)}) copy-start(bf16[256,32]{0,1:T(8,128)(2,1)} %param.35) | copy-start | bytes 49156
  2.6 57.3 %copy-start.11 = (f32[256]{0:T(256)S(1)}, f32[256]{0:T(256)}, u32[]{:S(2)}) copy-start(f32[256]{0:T(256)} %param.33) | copy-start | bytes 3076
  29.5 51.5 %copy-start.1 = (f32[1,32,64,256]{3,2,1,0:T(8,128)S(1)}, f32[1,32,64,256]{3,2,1,0:T(8,128)}, u32[]{:S(2)}) copy-start(f32[1,32,64,256]{3,2,1,0:T(8,128)} %param.40) | copy-start | bytes 6291460
  29.5 51.5 %copy-start.6 = (f32[4,1,2560]{2,1,0:T(1,128)S(1)}, f32[4,1,2560]{2,1,0:T(1,128)}, u32[]{:S(2)}) copy-start(f32[4,1,2560]{2,1,0:T(1,128)} %conv_weight.1) | copy-start | bytes 122884
  29.5 51.5 %copy-start.7 = (f32[1,3,1,2560]{3,2,1,0:T(1,128)S(1)}, f32[1,3,1,2560]{3,2,1,0:T(1,128)}, u32[]{:S(2)}) copy-start(f32[1,3,1,2560]{3,2,1,0:T(1,128)} %param.39) | copy-start | bytes 92164
  29.5 51.5 %copy-start.9 = (f32[1,2560]{1,0:T(1,128)S(1)}, f32[1,2560]{1,0:T(1,128)}, u32[]{:S(2)}) copy-start(f32[1,2560]{1,0:T(1,128)} %conv_bias.1) | copy-start | bytes 30724
  29.5 51.5 %copy-start.10 = (f32[1,2048]{1,0:T(1,128)S(1)}, f32[1,2048]{1,0:T(1,128)}, u32[]{:S(2)}) copy-start(f32[1,2048]{1,0:T(1,128)} %group_gain.1) | copy-start | bytes 24580
  29.5 51.5 %copy-start.13 = (f32[32]{0:T(128)S(1)}, f32[32]{0:T(128)}, u32[]{:S(2)}) copy-start(f32[32]{0:T(128)} %param.41) | copy-start | bytes 388
  29.5 51.5 %copy-start.14 = (f32[32]{0:T(128)S(1)}, f32[32]{0:T(128)}, u32[]{:S(2)}) copy-start(f32[32]{0:T(128)} %param.42) | copy-start | bytes 388
  29.5 51.5 %copy-start.15 = (f32[32]{0:T(128)S(1)}, f32[32]{0:T(128)}, u32[]{:S(2)}) copy-start(f32[32]{0:T(128)} %param.43) | copy-start | bytes 388
  45.3 53.5 %copy-start.2 = (bf16[2048,256]{1,0:T(8,128)(2,1)S(1)}, bf16[2048,256]{1,0:T(8,128)(2,1)}, u32[]{:S(2)}) copy-start(bf16[2048,256]{1,0:T(8,128)(2,1)} %weight.4) | copy-start | bytes 3145732
  59.9 52.0 %copy-start.4 = (bf16[256,2048]{1,0:T(8,128)(2,1)S(1)}, bf16[256,2048]{1,0:T(8,128)(2,1)}, u32[]{:S(2)}) copy-start(bf16[256,2048]{1,0:T(8,128)(2,1)} %w_up.1) | copy-start | bytes 3145732
  60.0 52.0 %copy-start.12 = (f32[256]{0:T(256)S(1)}, f32[256]{0:T(256)}, u32[]{:S(2)}) copy-start(f32[256]{0:T(256)} %param.45) | copy-start | bytes 3076
  81.0 61.3 %copy-start.3 = (bf16[2048,256]{1,0:T(8,128)(2,1)S(1)}, bf16[2048,256]{1,0:T(8,128)(2,1)}, u32[]{:S(2)}) copy-start(bf16[2048,256]{1,0:T(8,128)(2,1)} %weight.5) | copy-start | bytes 3145732

commit v5 on v4

--- a/solution.py
+++ b/solution.py
@@ -144,6 +144,15 @@
     write_copies(out, jnp.concatenate(halves, axis=0), ATTN)
 
 
+def pair_kernel(own, other, out):
+    out[...] = (own[...].astype(F32) + other[...].astype(F32)).astype(BF16)
+
+
+def sum_chips(own, second, before, after):
+    here = own[...].astype(F32) + second[...].astype(F32)
+    return here + (before[...].astype(F32) + after[...].astype(F32))
+
+
 def attn_out_kernel(pieces, slot_of, weight, out):
     column = iota((1, ROWS), 1)
     slots = slots_by_row(slot_of, ROWS) * 4 + column % STEPS
@@ -156,11 +165,11 @@
         mine = lax.dot_general(chosen, gathered, (((0,), (0,)), ((), ())), preferred_element_type=F32)
         term = dot(mine.astype(BF16), weight[pl.ds(half * 512, 512), :])
         total = term if total is None else total + term
-    write_copies(out, total, TP)
-
-
-def mix_in_kernel(pieces, hidden, gain, w_main, w_step, out, first_out):
-    first = (sum_pieces(pieces, TP) + hidden[...].astype(F32)).astype(BF16)
+    out[...] = total.astype(BF16)
+
+
+def mix_in_kernel(own, second, before, after, hidden, gain, w_main, w_step, out, first_out):
+    first = (sum_chips(own, second, before, after) + hidden[...].astype(F32)).astype(BF16)
     first_out[...] = first
     normed, tile = gain_rows(first.astype(F32), gain[...])
     main = dot(normed, w_main[...])
@@ -237,11 +246,11 @@
     for q in range(4):
         term = dot(ordered[q * ROWS : (q + 1) * ROWS], weight[pl.ds(q * 512, 512), :])
         total = term if total is None else total + term
-    write_copies(out, total, TP)
-
-
-def up_kernel(pieces, first, gain, w_up, out, second_out):
-    second = (sum_pieces(pieces, TP) + first[...].astype(F32)).astype(BF16)
+    out[...] = total.astype(BF16)
+
+
+def up_kernel(own, opposite, before, after, first, gain, w_up, out, second_out):
+    second = (sum_chips(own, opposite, before, after) + first[...].astype(F32)).astype(BF16)
     second_out[...] = second
     normed, tile = gain_rows(second.astype(F32), gain[...])
     up = dot(normed, w_up[...])
@@ -257,8 +266,8 @@
     write_copies(out, piece, ATTN)
 
 
-def last_kernel(pieces, second, out):
-    total = sum_pieces(pieces, TP) + second[...].astype(F32)
+def last_kernel(own, opposite, before, after, second, out):
+    total = sum_chips(own, opposite, before, after) + second[...].astype(F32)
     out[...] = total.reshape(out.shape).astype(BF16)
 
 
@@ -289,6 +298,13 @@
     rows, columns = values.shape
     cut = values.reshape(pieces, rows // pieces, columns)
     return lax.all_to_all(cut, axis, 0, 0).reshape(rows, columns)
+
+
+def over_tp(part):
+    other = lax.ppermute(part, "tp", [(k, k ^ 1) for k in range(TP)])
+    pair = call(pair_kernel, [part.shape], part, other)
+    shifted = [lax.ppermute(pair, "tp", [(k, (k + s) % TP) for k in range(TP)]) for s in (4, 2, 6)]
+    return [pair, *shifted]
 
 
 def on_device(
@@ -336,11 +352,11 @@
     pieces = lax.all_to_all(pieces, "attn", 0, 0)
     pieces = call(attend_kernel, [(owned, 512)], pieces, length_row, slot_row, cache)
     pieces = exchange(pieces, "attn", ATTN)
-    pieces = call(attn_out_kernel, [(TP * ROWS, width)], pieces, slot_row, w_attn_out)
-    pieces = exchange(pieces, "tp", TP)
+    pieces = call(attn_out_kernel, [(ROWS, width)], pieces, slot_row, w_attn_out)
+    pieces = over_tp(pieces)
     pieces, first = call(
         mix_in_kernel, [(ATTN, STEPS, 2 * INNER + 2 * STATES + LANES), (ROWS, width)],
-        pieces, rows, row(mamba_gain), w_mamba_in.reshape(width, -1), w_mamba_dt.T,
+        *pieces, rows, row(mamba_gain), w_mamba_in.reshape(width, -1), w_mamba_dt.T,
     )
     pieces = lax.all_to_all(pieces, "attn", 0, 0)
     pieces = call(
@@ -349,17 +365,17 @@
         ssm_state.reshape(INNER, STATES), row(a_log), row(dt_bias), row(skip_gain), group_gain,
     )
     pieces = exchange(pieces, "attn", ATTN)
-    pieces = call(project_out_kernel, [(TP * ROWS, width)], pieces, w_mamba_out)
-    pieces = exchange(pieces, "tp", TP)
+    pieces = call(project_out_kernel, [(ROWS, width)], pieces, w_mamba_out)
+    pieces = over_tp(pieces)
     pieces, second = call(
-        up_kernel, [(ATTN, STEPS, INNER + LANES), (ROWS, width)], pieces, first, row(mlp_gain), w_up
+        up_kernel, [(ATTN, STEPS, INNER + LANES), (ROWS, width)], *pieces, first, row(mlp_gain), w_up
     )
     pieces = lax.all_to_all(pieces, "attn", 0, 0)
     pieces = call(active_kernel, [(owned, 512)], pieces)
     pieces = exchange(pieces, "attn", ATTN)
-    pieces = call(project_out_kernel, [(TP * ROWS, width)], pieces, w_down)
-    pieces = exchange(pieces, "tp", TP)
-    return call(last_kernel, [hidden.shape], pieces, second)
+    pieces = call(project_out_kernel, [(ROWS, width)], pieces, w_down)
+    pieces = over_tp(pieces)
+    return call(last_kernel, [hidden.shape], *pieces, second)
 
 
 def solution(mesh):

time: 157 us -> 151 us (0.962)
  blocking collectives: 146 us -> 105 us
  starting transfers between devices: 0 us -> 24 us
  waiting for transfers between devices: 0 us -> 11.4 us
    all_to_all x6 -> x3, blocking collectives: 87 us -> 45.8 us  [exchange(): return lax.all_to_all(cut, axis, 0, 0).reshape(rows, columns)]
    ppermute x0 -> x12, starting transfers between devices: none -> 24 us  [the longest x3 12.1 us: over_tp(): other = lax.ppermute(part, 'tp', [(k, k ^ 1) for k in range(TP)])]
    ppermute x0 -> x12, waiting for transfers between devices: none -> 11.4 us  [the longest x9 8.84 us: over_tp(): lax.ppermute(pair, 'tp', [(k, (k + s) % TP) for k in range(TP)])]
    pallas_call x10 -> x13, Pallas kernels: 9.52 us -> 9.52 us  [call(): pl.pallas_call(kernel, out_shape=shapes, in_specs=[pl.BlockSpec(memory_sp...]
  transfers between devices with their start and end apart: 0 -> 12, of which waited for: 0 -> 9; matrix products, arithmetic and copies ran while one was open for 0% -> 0% of each run, Pallas kernels for 0% -> 0%
where the time goes in v5:
time: 151 us; the launch traced here: 150 us
  blocking collectives  105 us (70%)
  starting transfers between devices  24 us (16%)
  waiting for transfers between devices  11.4 us (8%)
  Pallas kernels  9.52 us (6%)
    all_to_all x3, blocking collectives, on_device(): pieces = lax.all_to_all(pieces, 'attn', 0, 0)  59 us
    all_to_all x3, blocking collectives, exchange(): return lax.all_to_all(cut, axis, 0, 0).reshape(rows, columns)  45.8 us
    ppermute x3, starting transfers between devices, over_tp(): other = lax.ppermute(part, 'tp', [(k, k ^ 1) for k in range(TP)])  12.1 us
    ppermute x9, starting transfers between devices, over_tp(): lax.ppermute(pair, 'tp', [(k, (k + s) % TP) for k in range(TP)])  11.8 us
    pallas_call x13, Pallas kernels, call(): pl.pallas_call(kernel, out_shape=shapes, in_specs=[pl.BlockSpec(memory_sp...  9.52 us
    ppermute x9, waiting for transfers between devices, over_tp(): lax.ppermute(pair, 'tp', [(k, (k + s) % TP) for k in range(TP)])  8.84 us
  transfers between devices with their start and end apart: 12, of which 9 were waited for; matrix products, arithmetic and copies ran while one was open for 0% of the time, Pallas kernels for 0%

profile of v5, /device:TPU:1, one launch (start us, length us, event | category | flops | bytes accessed | tf_op | source)
XLA Modules:
  0.0 150.0 jit_solution(9936487743486637161)
XLA Ops:
  0.0 2.6 %shard_map.226 = (bf16[32,4,1408]{2,1,0:T(4,128)(2,1)S(1)}, bf16[64,256]{1,0:T(8,128)(2,1)S(1)}, s32[1,32]{1,0:T(1,128)S(1)}, s32[1,32]{1,0:T(1,128)S(1)}, bf16[2,2,4096,128]{3,2,1,0:T(8,128)(2,1)S(1)}) custom-call(bf16[32,2,256]{2,1,0:T(2,128)(2,1)} %hidden.1, f32[1,256]{1,0:T(1,128)} %bitcast.33, s32[1,32]{1,0:T(1,128)} %bitcast.34, s32[1,32]{1,0:T(1,128)} %bitcast.35, ...), custom_call_target="tpu_custom_call" | custom-call | bytes 16777216 | tf_op jit(solution)/shard_map/pallas_call | solution.py:285
  2.6 25.3 %all_to_all.30.pieces = bf16[32,4,1408]{2,1,0:T(4,128)(2,1)S(1)} all-to-all(bf16[32,4,1408]{2,1,0:T(4,128)(2,1)S(1)} %get-tuple-element.14), channel_id=1, replica_groups=mesh['attn'=32,'tp'=8] {'attn'}, dimensions={0} | all-to-all | bytes 720896 | tf_op jit(solution)/shard_map/all_to_all | solution.py:352
  28.0 1.5 %shard_map.227 = bf16[256,512]{1,0:T(8,128)(2,1)S(1)} custom-call(bf16[32,4,1408]{2,1,0:T(4,128)(2,1)S(1)} %all_to_all.30.pieces, s32[1,32]{1,0:T(1,128)S(1)} %get-tuple-element.15.lengths, s32[1,32]{1,0:T(1,128)S(1)} %get-tuple-element.16.slot_of, bf16[2,2,4096,128]{3,2,1,0:T(8,128)(2,1)S(1)} %get-tuple-element.17.cache), custom_call_target="tpu_custom_call" | custom-call | bytes 4555008 | tf_op jit(solution)/shard_map/pallas_call | solution.py:285
  29.5 15.0 %all_to_all.31 = bf16[32,8,512]{2,1,0:T(8,128)(2,1)S(1)} all-to-all(bf16[32,8,512]{2,1,0:T(8,128)(2,1)S(1)} %bitcast.25), channel_id=1, replica_groups=mesh['attn'=32,'tp'=8] {'attn'}, dimensions={0} | all-to-all | bytes 524288 | tf_op jit(solution)/shard_map/all_to_all | solution.py:300
  45.1 3.8 %collective-permute-start = (bf16[64,256]{1,0:T(8,128)(2,1)S(1)}, bf16[64,256]{1,0:T(8,128)(2,1)S(1)}, u32[]{:S(2)}, u32[]{:S(2)}) collective-permute-start(bf16[64,256]{1,0:T(8,128)(2,1)S(1)} %shard_map.228.own), channel_id=1, source_target_pairs={{0,1},{1,0},{2,3},{3,2},{4,5},{5,4},{6,7},{7,6},{8,9},{9,8},{10,11... | collective-permute-start | bytes 98312 | tf_op jit(solution)/shard_map/ppermute | solution.py:304
  48.9 0.9 collective-permute-done.other
  49.8 2.8 %collective-permute-start.3 = (bf16[64,256]{1,0:T(8,128)(2,1)S(1)}, bf16[64,256]{1,0:T(8,128)(2,1)S(1)}, u32[]{:S(2)}, u32[]{:S(2)}) collective-permute-start(bf16[64,256]{1,0:T(8,128)(2,1)S(1)} %shard_map.229.own), channel_id=1, source_target_pairs={{0,6},{1,7},{2,0},{3,1},{4,2},{5,3},{6,4},{7,5},{8,14},{9,15},{10,... | collective-permute-start | bytes 98312 | tf_op jit(solution)/shard_map/ppermute | solution.py:306
  52.6 1.6 %collective-permute-start.1 = (bf16[64,256]{1,0:T(8,128)(2,1)S(1)}, bf16[64,256]{1,0:T(8,128)(2,1)S(1)}, u32[]{:S(2)}, u32[]{:S(2)}) collective-permute-start(bf16[64,256]{1,0:T(8,128)(2,1)S(1)} %shard_map.229.own), channel_id=1, source_target_pairs={{0,4},{1,5},{2,6},{3,7},{4,0},{5,1},{6,2},{7,3},{8,12},{9,13},{10,... | collective-permute-start | bytes 98312 | tf_op jit(solution)/shard_map/ppermute | solution.py:306
  54.3 2.4 %collective-permute-done.2.before = bf16[64,256]{1,0:T(8,128)(2,1)S(1)} collective-permute-done((bf16[64,256]{1,0:T(8,128)(2,1)S(1)}, bf16[64,256]{1,0:T(8,128)(2,1)S(1)}, u32[]{:S(2)}, u32[]{:S(2)}) %collective-permute-start.2) | collective-permute-done | bytes 32800 | tf_op jit(solution)/shard_map/ppermute | solution.py:306
  57.9 20.0 %all_to_all.32.pieces = bf16[32,2,4736]{2,1,0:T(2,128)(2,1)S(1)} all-to-all(bf16[32,2,4736]{2,1,0:T(2,128)(2,1)S(1)} %get-tuple-element.19), channel_id=1, replica_groups=mesh['attn'=32,'tp'=8] {'attn'}, dimensions={0} | all-to-all | bytes 1212416 | tf_op jit(solution)/shard_map/all_to_all | solution.py:361
  77.9 1.5 shard_map.231
  79.4 16.3 %all_to_all.33 = bf16[32,8,512]{2,1,0:T(8,128)(2,1)S(1)} all-to-all(bf16[32,8,512]{2,1,0:T(8,128)(2,1)S(1)} %bitcast.20), channel_id=1, replica_groups=mesh['attn'=32,'tp'=8] {'attn'}, dimensions={0} | all-to-all | bytes 524288 | tf_op jit(solution)/shard_map/all_to_all | solution.py:300
  96.2 3.8 %collective-permute-start.4 = (bf16[64,256]{1,0:T(8,128)(2,1)S(1)}, bf16[64,256]{1,0:T(8,128)(2,1)S(1)}, u32[]{:S(2)}, u32[]{:S(2)}) collective-permute-start(bf16[64,256]{1,0:T(8,128)(2,1)S(1)} %shard_map.232.own), channel_id=1, source_target_pairs={{0,1},{1,0},{2,3},{3,2},{4,5},{5,4},{6,7},{7,6},{8,9},{9,8},{10,11... | collective-permute-start | bytes 98312 | tf_op jit(solution)/shard_map/ppermute | solution.py:304
  100.1 0.9 collective-permute-done.4.other
  100.9 2.2 %collective-permute-start.7 = (bf16[64,256]{1,0:T(8,128)(2,1)S(1)}, bf16[64,256]{1,0:T(8,128)(2,1)S(1)}, u32[]{:S(2)}, u32[]{:S(2)}) collective-permute-start(bf16[64,256]{1,0:T(8,128)(2,1)S(1)} %shard_map.233.own), channel_id=1, source_target_pairs={{0,6},{1,7},{2,0},{3,1},{4,2},{5,3},{6,4},{7,5},{8,14},{9,15},{10,... | collective-permute-start | bytes 98312 | tf_op jit(solution)/shard_map/ppermute | solution.py:306
  103.2 1.3 collective-permute-start.5
  104.5 2.7 %collective-permute-done.6.before = bf16[64,256]{1,0:T(8,128)(2,1)S(1)} collective-permute-done((bf16[64,256]{1,0:T(8,128)(2,1)S(1)}, bf16[64,256]{1,0:T(8,128)(2,1)S(1)}, u32[]{:S(2)}, u32[]{:S(2)}) %collective-permute-start.6) | collective-permute-done | bytes 32800 | tf_op jit(solution)/shard_map/ppermute | solution.py:306
  108.0 13.7 %all_to_all.34.pieces = bf16[32,2,2176]{2,1,0:T(2,128)(2,1)S(1)} all-to-all(bf16[32,2,2176]{2,1,0:T(2,128)(2,1)S(1)} %get-tuple-element.21), channel_id=1, replica_groups=mesh['attn'=32,'tp'=8] {'attn'}, dimensions={0} | all-to-all | bytes 557056 | tf_op jit(solution)/shard_map/all_to_all | solution.py:373
  122.1 14.5 %all_to_all.35 = bf16[32,8,512]{2,1,0:T(8,128)(2,1)S(1)} all-to-all(bf16[32,8,512]{2,1,0:T(8,128)(2,1)S(1)} %bitcast.21), channel_id=1, replica_groups=mesh['attn'=32,'tp'=8] {'attn'}, dimensions={0} | all-to-all | bytes 524288 | tf_op jit(solution)/shard_map/all_to_all | solution.py:300
  137.1 4.5 %collective-permute-start.8 = (bf16[64,256]{1,0:T(8,128)(2,1)S(1)}, bf16[64,256]{1,0:T(8,128)(2,1)S(1)}, u32[]{:S(2)}, u32[]{:S(2)}) collective-permute-start(bf16[64,256]{1,0:T(8,128)(2,1)S(1)} %shard_map.236.own), channel_id=1, source_target_pairs={{0,1},{1,0},{2,3},{3,2},{4,5},{5,4},{6,7},{7,6},{8,9},{9,8},{10,11... | collective-permute-start | bytes 98312 | tf_op jit(solution)/shard_map/ppermute | solution.py:304
  141.5 0.9 collective-permute-done.8.other
  142.4 2.6 %collective-permute-start.11 = (bf16[64,256]{1,0:T(8,128)(2,1)S(1)}, bf16[64,256]{1,0:T(8,128)(2,1)S(1)}, u32[]{:S(2)}, u32[]{:S(2)}) collective-permute-start(bf16[64,256]{1,0:T(8,128)(2,1)S(1)} %shard_map.237.own), channel_id=1, source_target_pairs={{0,6},{1,7},{2,0},{3,1},{4,2},{5,3},{6,4},{7,5},{8,14},{9,15},{10,... | collective-permute-start | bytes 98312 | tf_op jit(solution)/shard_map/ppermute | solution.py:306
  145.0 1.3 collective-permute-start.9
  146.3 2.7 %collective-permute-done.10.before = bf16[64,256]{1,0:T(8,128)(2,1)S(1)} collective-permute-done((bf16[64,256]{1,0:T(8,128)(2,1)S(1)}, bf16[64,256]{1,0:T(8,128)(2,1)S(1)}, u32[]{:S(2)}, u32[]{:S(2)}) %collective-permute-start.10) | collective-permute-done | bytes 32800 | tf_op jit(solution)/shard_map/ppermute | solution.py:306
  (51 shorter events, 5.1 us)
Async XLA Ops:
  2.6 54.4 %copy-start = (bf16[256,1,4608]{2,0,1:T(8,128)(2,1)S(1)}, bf16[256,1,4608]{2,0,1:T(8,128)(2,1)}, u32[]{:S(2)}) copy-start(bf16[256,1,4608]{2,0,1:T(8,128)(2,1)} %param.34) | copy-start | bytes 7077892
  2.6 54.4 %copy-start.8 = (bf16[256,32]{0,1:T(8,128)(2,1)S(1)}, bf16[256,32]{0,1:T(8,128)(2,1)}, u32[]{:S(2)}) copy-start(bf16[256,32]{0,1:T(8,128)(2,1)} %param.35) | copy-start | bytes 49156
  2.6 54.4 %copy-start.11 = (f32[256]{0:T(256)S(1)}, f32[256]{0:T(256)}, u32[]{:S(2)}) copy-start(f32[256]{0:T(256)} %param.33) | copy-start | bytes 3076
  27.9 50.0 %copy-start.9 = (f32[1,2560]{1,0:T(1,128)S(1)}, f32[1,2560]{1,0:T(1,128)}, u32[]{:S(2)}) copy-start(f32[1,2560]{1,0:T(1,128)} %conv_bias.1) | copy-start | bytes 30724
  27.9 50.0 %copy-start.10 = (f32[1,2048]{1,0:T(1,128)S(1)}, f32[1,2048]{1,0:T(1,128)}, u32[]{:S(2)}) copy-start(f32[1,2048]{1,0:T(1,128)} %group_gain.1) | copy-start | bytes 24580
  27.9 50.0 %copy-start.13 = (f32[32]{0:T(128)S(1)}, f32[32]{0:T(128)}, u32[]{:S(2)}) copy-start(f32[32]{0:T(128)} %param.41) | copy-start | bytes 388
  27.9 50.0 %copy-start.14 = (f32[32]{0:T(128)S(1)}, f32[32]{0:T(128)}, u32[]{:S(2)}) copy-start(f32[32]{0:T(128)} %param.42) | copy-start | bytes 388
  28.0 50.0 %copy-start.15 = (f32[32]{0:T(128)S(1)}, f32[32]{0:T(128)}, u32[]{:S(2)}) copy-start(f32[32]{0:T(128)} %param.43) | copy-start | bytes 388
  44.5 51.2 %copy-start.2 = (bf16[2048,256]{1,0:T(8,128)(2,1)S(1)}, bf16[2048,256]{1,0:T(8,128)(2,1)}, u32[]{:S(2)}) copy-start(bf16[2048,256]{1,0:T(8,128)(2,1)} %weight.4) | copy-start | bytes 3145732
  45.1 4.7 %collective-permute-start = (bf16[64,256]{1,0:T(8,128)(2,1)S(1)}, bf16[64,256]{1,0:T(8,128)(2,1)S(1)}, u32[]{:S(2)}, u32[]{:S(2)}) collective-permute-start(bf16[64,256]{1,0:T(8,128)(2,1)S(1)} %shard_map.228.own), channel_id=1, source_target_pairs={{0,1},{1,0},{2,3},{3,2},{4,5},{5,4},{6,7},{7,6},{8,9},{9,8},{10,11... | collective-permute-start | bytes 98312 | tf_op jit(solution)/shard_map/ppermute | solution.py:304
  49.8 4.5 %collective-permute-start.3 = (bf16[64,256]{1,0:T(8,128)(2,1)S(1)}, bf16[64,256]{1,0:T(8,128)(2,1)S(1)}, u32[]{:S(2)}, u32[]{:S(2)}) collective-permute-start(bf16[64,256]{1,0:T(8,128)(2,1)S(1)} %shard_map.229.own), channel_id=1, source_target_pairs={{0,6},{1,7},{2,0},{3,1},{4,2},{5,3},{6,4},{7,5},{8,14},{9,15},{10,... | collective-permute-start | bytes 98312 | tf_op jit(solution)/shard_map/ppermute | solution.py:306
  52.6 4.0 %collective-permute-start.2 = (bf16[64,256]{1,0:T(8,128)(2,1)S(1)}, bf16[64,256]{1,0:T(8,128)(2,1)S(1)}, u32[]{:S(2)}, u32[]{:S(2)}) collective-permute-start(bf16[64,256]{1,0:T(8,128)(2,1)S(1)} %shard_map.229.own), channel_id=1, source_target_pairs={{0,2},{1,3},{2,4},{3,5},{4,6},{5,7},{6,0},{7,1},{8,10},{9,11},{10,... | collective-permute-start | bytes 98312 | tf_op jit(solution)/shard_map/ppermute | solution.py:306
  52.6 4.4 %collective-permute-start.1 = (bf16[64,256]{1,0:T(8,128)(2,1)S(1)}, bf16[64,256]{1,0:T(8,128)(2,1)S(1)}, u32[]{:S(2)}, u32[]{:S(2)}) collective-permute-start(bf16[64,256]{1,0:T(8,128)(2,1)S(1)} %shard_map.229.own), channel_id=1, source_target_pairs={{0,4},{1,5},{2,6},{3,7},{4,0},{5,1},{6,2},{7,3},{8,12},{9,13},{10,... | collective-permute-start | bytes 98312 | tf_op jit(solution)/shard_map/ppermute | solution.py:306
  57.0 50.5 %copy-start.3 = (bf16[256,2048]{1,0:T(8,128)(2,1)S(1)}, bf16[256,2048]{1,0:T(8,128)(2,1)}, u32[]{:S(2)}) copy-start(bf16[256,2048]{1,0:T(8,128)(2,1)} %w_up.1) | copy-start | bytes 3145732
  57.0 50.5 %copy-start.12 = (f32[256]{0:T(256)S(1)}, f32[256]{0:T(256)}, u32[]{:S(2)}) copy-start(f32[256]{0:T(256)} %param.45) | copy-start | bytes 3076
  77.9 58.7 %copy-start.4 = (bf16[2048,256]{1,0:T(8,128)(2,1)S(1)}, bf16[2048,256]{1,0:T(8,128)(2,1)}, u32[]{:S(2)}) copy-start(bf16[2048,256]{1,0:T(8,128)(2,1)} %weight.5) | copy-start | bytes 3145732
  96.2 4.7 %collective-permute-start.4 = (bf16[64,256]{1,0:T(8,128)(2,1)S(1)}, bf16[64,256]{1,0:T(8,128)(2,1)S(1)}, u32[]{:S(2)}, u32[]{:S(2)}) collective-permute-start(bf16[64,256]{1,0:T(8,128)(2,1)S(1)} %shard_map.232.own), channel_id=1, source_target_pairs={{0,1},{1,0},{2,3},{3,2},{4,5},{5,4},{6,7},{7,6},{8,9},{9,8},{10,11... | collective-permute-start | bytes 98312 | tf_op jit(solution)/shard_map/ppermute | solution.py:304
  100.9 3.5 %collective-permute-start.7 = (bf16[64,256]{1,0:T(8,128)(2,1)S(1)}, bf16[64,256]{1,0:T(8,128)(2,1)S(1)}, u32[]{:S(2)}, u32[]{:S(2)}) collective-permute-start(bf16[64,256]{1,0:T(8,128)(2,1)S(1)} %shard_map.233.own), channel_id=1, source_target_pairs={{0,6},{1,7},{2,0},{3,1},{4,2},{5,3},{6,4},{7,5},{8,14},{9,15},{10,... | collective-permute-start | bytes 98312 | tf_op jit(solution)/shard_map/ppermute | solution.py:306
  103.2 4.0 %collective-permute-start.6 = (bf16[64,256]{1,0:T(8,128)(2,1)S(1)}, bf16[64,256]{1,0:T(8,128)(2,1)S(1)}, u32[]{:S(2)}, u32[]{:S(2)}) collective-permute-start(bf16[64,256]{1,0:T(8,128)(2,1)S(1)} %shard_map.233.own), channel_id=1, source_target_pairs={{0,2},{1,3},{2,4},{3,5},{4,6},{5,7},{6,0},{7,1},{8,10},{9,11},{10,... | collective-permute-start | bytes 98312 | tf_op jit(solution)/shard_map/ppermute | solution.py:306
  103.2 4.3 %collective-permute-start.5 = (bf16[64,256]{1,0:T(8,128)(2,1)S(1)}, bf16[64,256]{1,0:T(8,128)(2,1)S(1)}, u32[]{:S(2)}, u32[]{:S(2)}) collective-permute-start(bf16[64,256]{1,0:T(8,128)(2,1)S(1)} %shard_map.233.own), channel_id=1, source_target_pairs={{0,4},{1,5},{2,6},{3,7},{4,0},{5,1},{6,2},{7,3},{8,12},{9,13},{10,... | collective-permute-start | bytes 98312 | tf_op jit(solution)/shard_map/ppermute | solution.py:306
  137.1 5.3 %collective-permute-start.8 = (bf16[64,256]{1,0:T(8,128)(2,1)S(1)}, bf16[64,256]{1,0:T(8,128)(2,1)S(1)}, u32[]{:S(2)}, u32[]{:S(2)}) collective-permute-start(bf16[64,256]{1,0:T(8,128)(2,1)S(1)} %shard_map.236.own), channel_id=1, source_target_pairs={{0,1},{1,0},{2,3},{3,2},{4,5},{5,4},{6,7},{7,6},{8,9},{9,8},{10,11... | collective-permute-start | bytes 98312 | tf_op jit(solution)/shard_map/ppermute | solution.py:304
  142.4 3.9 %collective-permute-start.11 = (bf16[64,256]{1,0:T(8,128)(2,1)S(1)}, bf16[64,256]{1,0:T(8,128)(2,1)S(1)}, u32[]{:S(2)}, u32[]{:S(2)}) collective-permute-start(bf16[64,256]{1,0:T(8,128)(2,1)S(1)} %shard_map.237.own), channel_id=1, source_target_pairs={{0,6},{1,7},{2,0},{3,1},{4,2},{5,3},{6,4},{7,5},{8,14},{9,15},{10,... | collective-permute-start | bytes 98312 | tf_op jit(solution)/shard_map/ppermute | solution.py:306
  145.0 4.0 %collective-permute-start.10 = (bf16[64,256]{1,0:T(8,128)(2,1)S(1)}, bf16[64,256]{1,0:T(8,128)(2,1)S(1)}, u32[]{:S(2)}, u32[]{:S(2)}) collective-permute-start(bf16[64,256]{1,0:T(8,128)(2,1)S(1)} %shard_map.237.own), channel_id=1, source_target_pairs={{0,2},{1,3},{2,4},{3,5},{4,6},{5,7},{6,0},{7,1},{8,10},{9,11},{10,... | collective-permute-start | bytes 98312 | tf_op jit(solution)/shard_map/ppermute | solution.py:306
  145.0 4.3 %collective-permute-start.9 = (bf16[64,256]{1,0:T(8,128)(2,1)S(1)}, bf16[64,256]{1,0:T(8,128)(2,1)S(1)}, u32[]{:S(2)}, u32[]{:S(2)}) collective-permute-start(bf16[64,256]{1,0:T(8,128)(2,1)S(1)} %shard_map.237.own), channel_id=1, source_target_pairs={{0,4},{1,5},{2,6},{3,7},{4,0},{5,1},{6,2},{7,3},{8,12},{9,13},{10,... | collective-permute-start | bytes 98312 | tf_op jit(solution)/shard_map/ppermute | solution.py:306
  (4 other events, 191.8 us)

commit v6 on v5

--- a/solution.py
+++ b/solution.py
@@ -168,7 +168,7 @@
     out[...] = total.astype(BF16)
 
 
-def mix_in_kernel(own, second, before, after, hidden, gain, w_main, w_step, out, first_out):
+def mix_in_kernel(own, before, after, second, hidden, gain, w_main, w_step, out, first_out):
     first = (sum_chips(own, second, before, after) + hidden[...].astype(F32)).astype(BF16)
     first_out[...] = first
     normed, tile = gain_rows(first.astype(F32), gain[...])
@@ -249,7 +249,7 @@
     out[...] = total.astype(BF16)
 
 
-def up_kernel(own, opposite, before, after, first, gain, w_up, out, second_out):
+def up_kernel(own, before, after, opposite, first, gain, w_up, out, second_out):
     second = (sum_chips(own, opposite, before, after) + first[...].astype(F32)).astype(BF16)
     second_out[...] = second
     normed, tile = gain_rows(second.astype(F32), gain[...])
@@ -266,7 +266,7 @@
     write_copies(out, piece, ATTN)
 
 
-def last_kernel(own, opposite, before, after, second, out):
+def last_kernel(own, before, after, opposite, second, out):
     total = sum_chips(own, opposite, before, after) + second[...].astype(F32)
     out[...] = total.reshape(out.shape).astype(BF16)
 
@@ -304,7 +304,7 @@
     other = lax.ppermute(part, "tp", [(k, k ^ 1) for k in range(TP)])
     pair = call(pair_kernel, [part.shape], part, other)
     shifted = [lax.ppermute(pair, "tp", [(k, (k + s) % TP) for k in range(TP)]) for s in (4, 2, 6)]
-    return [pair, *shifted]
+    return [pair, shifted[1], shifted[2], shifted[0]]
 
 
 def on_device(

time: 151 us -> 149 us (0.987)
  starting transfers between devices: 24 us -> 21.8 us
  waiting for transfers between devices: 11.4 us -> 13.4 us
    ppermute x9, starting transfers between devices: 11.8 us -> 8.99 us  [over_tp(): lax.ppermute(pair, 'tp', [(k, (k + s) % TP) for k in range(TP)])]
    ppermute x9, waiting for transfers between devices: 8.84 us -> 10.8 us  [over_tp(): lax.ppermute(pair, 'tp', [(k, (k + s) % TP) for k in range(TP)])]
  transfers between devices with their start and end apart: 12 -> 12, of which waited for: 9 -> 10; matrix products, arithmetic and copies ran while one was open for 0% -> 0% of each run, Pallas kernels for 0% -> 0%
where the time goes in v6:
time: 149 us
  blocking collectives  104 us (70%)
  starting transfers between devices  21.8 us (15%)
  waiting for transfers between devices  13.4 us (9%)
  Pallas kernels  9.51 us (6%)
    all_to_all x3, blocking collectives, on_device(): pieces = lax.all_to_all(pieces, 'attn', 0, 0)  58.4 us
    all_to_all x3, blocking collectives, exchange(): return lax.all_to_all(cut, axis, 0, 0).reshape(rows, columns)  45.6 us
    ppermute x3, starting transfers between devices, over_tp(): other = lax.ppermute(part, 'tp', [(k, k ^ 1) for k in range(TP)])  12.8 us
    ppermute x9, waiting for transfers between devices, over_tp(): lax.ppermute(pair, 'tp', [(k, (k + s) % TP) for k in range(TP)])  10.8 us
    pallas_call x13, Pallas kernels, call(): pl.pallas_call(kernel, out_shape=shapes, in_specs=[pl.BlockSpec(memory_sp...  9.51 us
    ppermute x9, starting transfers between devices, over_tp(): lax.ppermute(pair, 'tp', [(k, (k + s) % TP) for k in range(TP)])  8.99 us
  transfers between devices with their start and end apart: 12, of which 10 were waited for; matrix products, arithmetic and copies ran while one was open for 0% of the time, Pallas kernels for 0%

profile of v6, /device:TPU:1, one launch (start us, length us, event | category | flops | bytes accessed | tf_op | source)
XLA Modules:
  0.0 149.0 jit_solution(12782741269813717361)
XLA Ops:
  0.0 2.6 %shard_map.226 = (bf16[32,4,1408]{2,1,0:T(4,128)(2,1)S(1)}, bf16[64,256]{1,0:T(8,128)(2,1)S(1)}, s32[1,32]{1,0:T(1,128)S(1)}, s32[1,32]{1,0:T(1,128)S(1)}, bf16[2,2,4096,128]{3,2,1,0:T(8,128)(2,1)S(1)}) custom-call(bf16[32,2,256]{2,1,0:T(2,128)(2,1)} %hidden.1, f32[1,256]{1,0:T(1,128)} %bitcast.33, s32[1,32]{1,0:T(1,128)} %bitcast.34, s32[1,32]{1,0:T(1,128)} %bitcast.35, ...), custom_call_target="tpu_custom_call" | custom-call | bytes 16777216 | tf_op jit(solution)/shard_map/pallas_call | solution.py:285
  2.6 25.3 %all_to_all.30.pieces = bf16[32,4,1408]{2,1,0:T(4,128)(2,1)S(1)} all-to-all(bf16[32,4,1408]{2,1,0:T(4,128)(2,1)S(1)} %get-tuple-element.14), channel_id=1, replica_groups=mesh['attn'=32,'tp'=8] {'attn'}, dimensions={0} | all-to-all | bytes 720896 | tf_op jit(solution)/shard_map/all_to_all | solution.py:352
  28.0 1.5 %shard_map.227 = bf16[256,512]{1,0:T(8,128)(2,1)S(1)} custom-call(bf16[32,4,1408]{2,1,0:T(4,128)(2,1)S(1)} %all_to_all.30.pieces, s32[1,32]{1,0:T(1,128)S(1)} %get-tuple-element.15.lengths, s32[1,32]{1,0:T(1,128)S(1)} %get-tuple-element.16.slot_of, bf16[2,2,4096,128]{3,2,1,0:T(8,128)(2,1)S(1)} %get-tuple-element.17.cache), custom_call_target="tpu_custom_call" | custom-call | bytes 4555008 | tf_op jit(solution)/shard_map/pallas_call | solution.py:285
  29.5 15.0 %all_to_all.31 = bf16[32,8,512]{2,1,0:T(8,128)(2,1)S(1)} all-to-all(bf16[32,8,512]{2,1,0:T(8,128)(2,1)S(1)} %bitcast.25), channel_id=1, replica_groups=mesh['attn'=32,'tp'=8] {'attn'}, dimensions={0} | all-to-all | bytes 524288 | tf_op jit(solution)/shard_map/all_to_all | solution.py:300
  45.1 3.8 %collective-permute-start = (bf16[64,256]{1,0:T(8,128)(2,1)S(1)}, bf16[64,256]{1,0:T(8,128)(2,1)S(1)}, u32[]{:S(2)}, u32[]{:S(2)}) collective-permute-start(bf16[64,256]{1,0:T(8,128)(2,1)S(1)} %shard_map.228.own), channel_id=1, source_target_pairs={{0,1},{1,0},{2,3},{3,2},{4,5},{5,4},{6,7},{7,6},{8,9},{9,8},{10,11... | collective-permute-start | bytes 98312 | tf_op jit(solution)/shard_map/ppermute | solution.py:304
  48.9 0.9 collective-permute-done.other
  49.8 3.0 %collective-permute-start.3 = (bf16[64,256]{1,0:T(8,128)(2,1)S(1)}, bf16[64,256]{1,0:T(8,128)(2,1)S(1)}, u32[]{:S(2)}, u32[]{:S(2)}) collective-permute-start(bf16[64,256]{1,0:T(8,128)(2,1)S(1)} %shard_map.229.own), channel_id=1, source_target_pairs={{0,4},{1,5},{2,6},{3,7},{4,0},{5,1},{6,2},{7,3},{8,12},{9,13},{10,... | collective-permute-start | bytes 98312 | tf_op jit(solution)/shard_map/ppermute | solution.py:306
  54.3 1.4 collective-permute-done.2.after
  55.7 1.9 %collective-permute-done.1.before = bf16[64,256]{1,0:T(8,128)(2,1)S(1)} collective-permute-done((bf16[64,256]{1,0:T(8,128)(2,1)S(1)}, bf16[64,256]{1,0:T(8,128)(2,1)S(1)}, u32[]{:S(2)}, u32[]{:S(2)}) %collective-permute-start.1) | collective-permute-done | bytes 32800 | tf_op jit(solution)/shard_map/ppermute | solution.py:306
  58.4 19.2 %all_to_all.32.pieces = bf16[32,2,4736]{2,1,0:T(2,128)(2,1)S(1)} all-to-all(bf16[32,2,4736]{2,1,0:T(2,128)(2,1)S(1)} %get-tuple-element.19), channel_id=1, replica_groups=mesh['attn'=32,'tp'=8] {'attn'}, dimensions={0} | all-to-all | bytes 1212416 | tf_op jit(solution)/shard_map/all_to_all | solution.py:361
  77.7 1.5 shard_map.231
  79.2 16.6 %all_to_all.33 = bf16[32,8,512]{2,1,0:T(8,128)(2,1)S(1)} all-to-all(bf16[32,8,512]{2,1,0:T(8,128)(2,1)S(1)} %bitcast.20), channel_id=1, replica_groups=mesh['attn'=32,'tp'=8] {'attn'}, dimensions={0} | all-to-all | bytes 524288 | tf_op jit(solution)/shard_map/all_to_all | solution.py:300
  96.3 3.9 %collective-permute-start.4 = (bf16[64,256]{1,0:T(8,128)(2,1)S(1)}, bf16[64,256]{1,0:T(8,128)(2,1)S(1)}, u32[]{:S(2)}, u32[]{:S(2)}) collective-permute-start(bf16[64,256]{1,0:T(8,128)(2,1)S(1)} %shard_map.232.own), channel_id=1, source_target_pairs={{0,1},{1,0},{2,3},{3,2},{4,5},{5,4},{6,7},{7,6},{8,9},{9,8},{10,11... | collective-permute-start | bytes 98312 | tf_op jit(solution)/shard_map/ppermute | solution.py:304
  100.2 0.9 collective-permute-done.4.other
  101.1 1.2 collective-permute-start.7
  102.3 1.4 collective-permute-start.6
  103.7 1.7 %collective-permute-done.7.opposite = bf16[64,256]{1,0:T(8,128)(2,1)S(1)} collective-permute-done((bf16[64,256]{1,0:T(8,128)(2,1)S(1)}, bf16[64,256]{1,0:T(8,128)(2,1)S(1)}, u32[]{:S(2)}, u32[]{:S(2)}) %collective-permute-start.7) | collective-permute-done | bytes 32800 | tf_op jit(solution)/shard_map/ppermute | solution.py:306
  105.6 2.1 %collective-permute-done.5.before = bf16[64,256]{1,0:T(8,128)(2,1)S(1)} collective-permute-done((bf16[64,256]{1,0:T(8,128)(2,1)S(1)}, bf16[64,256]{1,0:T(8,128)(2,1)S(1)}, u32[]{:S(2)}, u32[]{:S(2)}) %collective-permute-start.5) | collective-permute-done | bytes 32800 | tf_op jit(solution)/shard_map/ppermute | solution.py:306
  108.2 13.9 %all_to_all.34.pieces = bf16[32,2,2176]{2,1,0:T(2,128)(2,1)S(1)} all-to-all(bf16[32,2,2176]{2,1,0:T(2,128)(2,1)S(1)} %get-tuple-element.21), channel_id=1, replica_groups=mesh['attn'=32,'tp'=8] {'attn'}, dimensions={0} | all-to-all | bytes 557056 | tf_op jit(solution)/shard_map/all_to_all | solution.py:373
  122.4 14.0 %all_to_all.35 = bf16[32,8,512]{2,1,0:T(8,128)(2,1)S(1)} all-to-all(bf16[32,8,512]{2,1,0:T(8,128)(2,1)S(1)} %bitcast.21), channel_id=1, replica_groups=mesh['attn'=32,'tp'=8] {'attn'}, dimensions={0} | all-to-all | bytes 524288 | tf_op jit(solution)/shard_map/all_to_all | solution.py:300
  136.9 5.1 %collective-permute-start.8 = (bf16[64,256]{1,0:T(8,128)(2,1)S(1)}, bf16[64,256]{1,0:T(8,128)(2,1)S(1)}, u32[]{:S(2)}, u32[]{:S(2)}) collective-permute-start(bf16[64,256]{1,0:T(8,128)(2,1)S(1)} %shard_map.236.own), channel_id=1, source_target_pairs={{0,1},{1,0},{2,3},{3,2},{4,5},{5,4},{6,7},{7,6},{8,9},{9,8},{10,11... | collective-permute-start | bytes 98312 | tf_op jit(solution)/shard_map/ppermute | solution.py:304
  143.3 0.9 collective-permute-start.10
  144.7 2.5 %collective-permute-done.11.opposite = bf16[64,256]{1,0:T(8,128)(2,1)S(1)} collective-permute-done((bf16[64,256]{1,0:T(8,128)(2,1)S(1)}, bf16[64,256]{1,0:T(8,128)(2,1)S(1)}, u32[]{:S(2)}, u32[]{:S(2)}) %collective-permute-start.11) | collective-permute-done | bytes 32800 | tf_op jit(solution)/shard_map/ppermute | solution.py:306
  147.2 1.2 collective-permute-done.9.before
  (51 shorter events, 7.6 us)
Async XLA Ops:
  2.6 55.0 %copy-start = (bf16[256,1,4608]{2,0,1:T(8,128)(2,1)S(1)}, bf16[256,1,4608]{2,0,1:T(8,128)(2,1)}, u32[]{:S(2)}) copy-start(bf16[256,1,4608]{2,0,1:T(8,128)(2,1)} %param.34) | copy-start | bytes 7077892
  2.6 55.0 %copy-start.8 = (bf16[256,32]{0,1:T(8,128)(2,1)S(1)}, bf16[256,32]{0,1:T(8,128)(2,1)}, u32[]{:S(2)}) copy-start(bf16[256,32]{0,1:T(8,128)(2,1)} %param.35) | copy-start | bytes 49156
  2.6 55.0 %copy-start.11 = (f32[256]{0:T(256)S(1)}, f32[256]{0:T(256)}, u32[]{:S(2)}) copy-start(f32[256]{0:T(256)} %param.33) | copy-start | bytes 3076
  27.9 49.8 %copy-start.9 = (f32[1,2560]{1,0:T(1,128)S(1)}, f32[1,2560]{1,0:T(1,128)}, u32[]{:S(2)}) copy-start(f32[1,2560]{1,0:T(1,128)} %conv_bias.1) | copy-start | bytes 30724
  27.9 49.8 %copy-start.10 = (f32[1,2048]{1,0:T(1,128)S(1)}, f32[1,2048]{1,0:T(1,128)}, u32[]{:S(2)}) copy-start(f32[1,2048]{1,0:T(1,128)} %group_gain.1) | copy-start | bytes 24580
  27.9 49.8 %copy-start.13 = (f32[32]{0:T(128)S(1)}, f32[32]{0:T(128)}, u32[]{:S(2)}) copy-start(f32[32]{0:T(128)} %param.41) | copy-start | bytes 388
  27.9 49.8 %copy-start.14 = (f32[32]{0:T(128)S(1)}, f32[32]{0:T(128)}, u32[]{:S(2)}) copy-start(f32[32]{0:T(128)} %param.42) | copy-start | bytes 388
  28.0 49.8 %copy-start.15 = (f32[32]{0:T(128)S(1)}, f32[32]{0:T(128)}, u32[]{:S(2)}) copy-start(f32[32]{0:T(128)} %param.43) | copy-start | bytes 388
  44.5 51.3 %copy-start.2 = (bf16[2048,256]{1,0:T(8,128)(2,1)S(1)}, bf16[2048,256]{1,0:T(8,128)(2,1)}, u32[]{:S(2)}) copy-start(bf16[2048,256]{1,0:T(8,128)(2,1)} %weight.4) | copy-start | bytes 3145732
  45.1 4.7 %collective-permute-start = (bf16[64,256]{1,0:T(8,128)(2,1)S(1)}, bf16[64,256]{1,0:T(8,128)(2,1)S(1)}, u32[]{:S(2)}, u32[]{:S(2)}) collective-permute-start(bf16[64,256]{1,0:T(8,128)(2,1)S(1)} %shard_map.228.own), channel_id=1, source_target_pairs={{0,1},{1,0},{2,3},{3,2},{4,5},{5,4},{6,7},{7,6},{8,9},{9,8},{10,11... | collective-permute-start | bytes 98312 | tf_op jit(solution)/shard_map/ppermute | solution.py:304
  49.8 4.5 %collective-permute-start.3 = (bf16[64,256]{1,0:T(8,128)(2,1)S(1)}, bf16[64,256]{1,0:T(8,128)(2,1)S(1)}, u32[]{:S(2)}, u32[]{:S(2)}) collective-permute-start(bf16[64,256]{1,0:T(8,128)(2,1)S(1)} %shard_map.229.own), channel_id=1, source_target_pairs={{0,4},{1,5},{2,6},{3,7},{4,0},{5,1},{6,2},{7,3},{8,12},{9,13},{10,... | collective-permute-start | bytes 98312 | tf_op jit(solution)/shard_map/ppermute | solution.py:306
  52.8 2.9 %collective-permute-start.2 = (bf16[64,256]{1,0:T(8,128)(2,1)S(1)}, bf16[64,256]{1,0:T(8,128)(2,1)S(1)}, u32[]{:S(2)}, u32[]{:S(2)}) collective-permute-start(bf16[64,256]{1,0:T(8,128)(2,1)S(1)} %shard_map.229.own), channel_id=1, source_target_pairs={{0,6},{1,7},{2,0},{3,1},{4,2},{5,3},{6,4},{7,5},{8,14},{9,15},{10,... | collective-permute-start | bytes 98312 | tf_op jit(solution)/shard_map/ppermute | solution.py:306
  53.6 4.0 %collective-permute-start.1 = (bf16[64,256]{1,0:T(8,128)(2,1)S(1)}, bf16[64,256]{1,0:T(8,128)(2,1)S(1)}, u32[]{:S(2)}, u32[]{:S(2)}) collective-permute-start(bf16[64,256]{1,0:T(8,128)(2,1)S(1)} %shard_map.229.own), channel_id=1, source_target_pairs={{0,2},{1,3},{2,4},{3,5},{4,6},{5,7},{6,0},{7,1},{8,10},{9,11},{10,... | collective-permute-start | bytes 98312 | tf_op jit(solution)/shard_map/ppermute | solution.py:306
  57.6 50.1 %copy-start.3 = (bf16[256,2048]{1,0:T(8,128)(2,1)S(1)}, bf16[256,2048]{1,0:T(8,128)(2,1)}, u32[]{:S(2)}) copy-start(bf16[256,2048]{1,0:T(8,128)(2,1)} %w_up.1) | copy-start | bytes 3145732
  57.6 50.1 %copy-start.12 = (f32[256]{0:T(256)S(1)}, f32[256]{0:T(256)}, u32[]{:S(2)}) copy-start(f32[256]{0:T(256)} %param.45) | copy-start | bytes 3076
  77.7 58.7 %copy-start.4 = (bf16[2048,256]{1,0:T(8,128)(2,1)S(1)}, bf16[2048,256]{1,0:T(8,128)(2,1)}, u32[]{:S(2)}) copy-start(bf16[2048,256]{1,0:T(8,128)(2,1)} %weight.5) | copy-start | bytes 3145732
  96.3 4.8 %collective-permute-start.4 = (bf16[64,256]{1,0:T(8,128)(2,1)S(1)}, bf16[64,256]{1,0:T(8,128)(2,1)S(1)}, u32[]{:S(2)}, u32[]{:S(2)}) collective-permute-start(bf16[64,256]{1,0:T(8,128)(2,1)S(1)} %shard_map.232.own), channel_id=1, source_target_pairs={{0,1},{1,0},{2,3},{3,2},{4,5},{5,4},{6,7},{7,6},{8,9},{9,8},{10,11... | collective-permute-start | bytes 98312 | tf_op jit(solution)/shard_map/ppermute | solution.py:304
  101.1 4.4 %collective-permute-start.7 = (bf16[64,256]{1,0:T(8,128)(2,1)S(1)}, bf16[64,256]{1,0:T(8,128)(2,1)S(1)}, u32[]{:S(2)}, u32[]{:S(2)}) collective-permute-start(bf16[64,256]{1,0:T(8,128)(2,1)S(1)} %shard_map.233.own), channel_id=1, source_target_pairs={{0,4},{1,5},{2,6},{3,7},{4,0},{5,1},{6,2},{7,3},{8,12},{9,13},{10,... | collective-permute-start | bytes 98312 | tf_op jit(solution)/shard_map/ppermute | solution.py:306
  102.3 3.3 %collective-permute-start.6 = (bf16[64,256]{1,0:T(8,128)(2,1)S(1)}, bf16[64,256]{1,0:T(8,128)(2,1)S(1)}, u32[]{:S(2)}, u32[]{:S(2)}) collective-permute-start(bf16[64,256]{1,0:T(8,128)(2,1)S(1)} %shard_map.233.own), channel_id=1, source_target_pairs={{0,6},{1,7},{2,0},{3,1},{4,2},{5,3},{6,4},{7,5},{8,14},{9,15},{10,... | collective-permute-start | bytes 98312 | tf_op jit(solution)/shard_map/ppermute | solution.py:306
  103.7 4.0 %collective-permute-start.5 = (bf16[64,256]{1,0:T(8,128)(2,1)S(1)}, bf16[64,256]{1,0:T(8,128)(2,1)S(1)}, u32[]{:S(2)}, u32[]{:S(2)}) collective-permute-start(bf16[64,256]{1,0:T(8,128)(2,1)S(1)} %shard_map.233.own), channel_id=1, source_target_pairs={{0,2},{1,3},{2,4},{3,5},{4,6},{5,7},{6,0},{7,1},{8,10},{9,11},{10,... | collective-permute-start | bytes 98312 | tf_op jit(solution)/shard_map/ppermute | solution.py:306
  136.9 5.9 %collective-permute-start.8 = (bf16[64,256]{1,0:T(8,128)(2,1)S(1)}, bf16[64,256]{1,0:T(8,128)(2,1)S(1)}, u32[]{:S(2)}, u32[]{:S(2)}) collective-permute-start(bf16[64,256]{1,0:T(8,128)(2,1)S(1)} %shard_map.236.own), channel_id=1, source_target_pairs={{0,1},{1,0},{2,3},{3,2},{4,5},{5,4},{6,7},{7,6},{8,9},{9,8},{10,11... | collective-permute-start | bytes 98312 | tf_op jit(solution)/shard_map/ppermute | solution.py:304
  142.8 4.4 %collective-permute-start.11 = (bf16[64,256]{1,0:T(8,128)(2,1)S(1)}, bf16[64,256]{1,0:T(8,128)(2,1)S(1)}, u32[]{:S(2)}, u32[]{:S(2)}) collective-permute-start(bf16[64,256]{1,0:T(8,128)(2,1)S(1)} %shard_map.237.own), channel_id=1, source_target_pairs={{0,4},{1,5},{2,6},{3,7},{4,0},{5,1},{6,2},{7,3},{8,12},{9,13},{10,... | collective-permute-start | bytes 98312 | tf_op jit(solution)/shard_map/ppermute | solution.py:306
  143.3 3.9 %collective-permute-start.10 = (bf16[64,256]{1,0:T(8,128)(2,1)S(1)}, bf16[64,256]{1,0:T(8,128)(2,1)S(1)}, u32[]{:S(2)}, u32[]{:S(2)}) collective-permute-start(bf16[64,256]{1,0:T(8,128)(2,1)S(1)} %shard_map.237.own), channel_id=1, source_target_pairs={{0,6},{1,7},{2,0},{3,1},{4,2},{5,3},{6,4},{7,5},{8,14},{9,15},{10,... | collective-permute-start | bytes 98312 | tf_op jit(solution)/shard_map/ppermute | solution.py:306
  144.2 4.2 %collective-permute-start.9 = (bf16[64,256]{1,0:T(8,128)(2,1)S(1)}, bf16[64,256]{1,0:T(8,128)(2,1)S(1)}, u32[]{:S(2)}, u32[]{:S(2)}) collective-permute-start(bf16[64,256]{1,0:T(8,128)(2,1)S(1)} %shard_map.237.own), channel_id=1, source_target_pairs={{0,2},{1,3},{2,4},{3,5},{4,6},{5,7},{6,0},{7,1},{8,10},{9,11},{10,... | collective-permute-start | bytes 98312 | tf_op jit(solution)/shard_map/ppermute | solution.py:306
  (4 other events, 191.2 us)

commit v7 on v6

--- a/solution.py
+++ b/solution.py
@@ -15,7 +15,6 @@
 ATTN = 32
 TP = 8
 WIDTH = 8192
-SLOTS = 64
 INNER = 2048
 STATES = 256
 HEADS = 32
@@ -89,8 +88,17 @@
     whole = jnp.concatenate([query, key, value, tile], axis=1)
     column = iota((1, ROWS), 1)
     code = slots_by_row(slots_out, ROWS) * 2 + column % STEPS
-    chosen = one_hot(iota((2 * SLOTS, ROWS), 0) == code)
-    out[...] = dot(chosen, whole).reshape(out.shape).astype(BF16)
+    row = iota((ROWS, ROWS), 0)
+    parts = []
+    for slot in range(2):
+        chosen = one_hot((row // STEPS) * 4 + slot * 2 + row % STEPS == code)
+        parts.append(dot(chosen, whole))
+    columns = whole.shape[1] - LANES
+    tiles = parts[0][:, columns:] + jnp.concatenate(
+        [jnp.zeros((ROWS, 2), F32), parts[1][:, columns : columns + LANES - 2]], axis=1
+    )
+    both = jnp.concatenate([parts[0][:, :columns], parts[1][:, :columns], tiles], axis=1)
+    out[...] = both.reshape(out.shape).astype(BF16)
     copies[7].wait()
 
 
@@ -99,39 +107,50 @@
     summed = jnp.sum(pieces[...].astype(F32), axis=0)
     keys_at = 8 * HEAD_SIZE
     columns = keys_at + 2 * HEAD_SIZE
-    whole = (summed[:, :columns] * scale_of(summed[:, columns:])).astype(BF16).astype(F32)
+    both_rows = []
+    for slot in range(2):
+        scale = scale_of(summed[:, 2 * columns + 2 * slot :])
+        rows = summed[:, slot * columns : (slot + 1) * columns] * scale
+        both_rows.append(rows.astype(BF16).astype(F32))
     heads = 8
     factor = HEAD_SIZE ** (-0.5)
     group = heads * STEPS
     step_of_row = iota((group, 1), 0) % STEPS
-    outputs = []
+    queries, kept_rows, all_scores, outputs = [], [], [], []
     for slot in range(2):
-        mine = slot_of[...] == first_slot + slot
-        length = jnp.sum(jnp.where(mine, lengths[...].astype(F32), 0.0), axis=1, keepdims=True)
-        length = length.astype(jnp.int32)
-        rows = whole[slot * 2 : slot * 2 + 2]
+        rows = both_rows[slot]
         query = jnp.concatenate([rows[:, h * LANES : (h + 1) * LANES] for h in range(heads)], axis=0)
-        fresh_key = rows[:, keys_at : keys_at + HEAD_SIZE]
-        fresh_value = rows[:, keys_at + HEAD_SIZE :]
-        scores = (
+        queries.append(query)
+        kept_rows.append(rows)
+        all_scores.append(
             lax.dot_general(
                 query.astype(BF16), cache[slot, 0], (((1,), (1,)), ((), ())), preferred_element_type=F32
             )
             * factor
         )
+    soft = []
+    for slot in range(2):
+        mine = slot_of[...] == first_slot + slot
+        length = jnp.sum(jnp.where(mine, lengths[...].astype(F32), 0.0), axis=1, keepdims=True)
+        length = length.astype(jnp.int32)
+        fresh_key = kept_rows[slot][:, keys_at : keys_at + HEAD_SIZE]
+        scores = all_scores[slot]
         scores = jnp.where(iota(scores.shape, 1) < length, scores, MASKED)
         fresh = []
         for t in range(STEPS):
-            score = jnp.sum(query * fresh_key[t : t + 1], axis=-1, keepdims=True) * factor
+            score = jnp.sum(queries[slot] * fresh_key[t : t + 1], axis=-1, keepdims=True) * factor
             fresh.append(jnp.where(step_of_row >= t, score, MASKED))
         top = jnp.maximum(jnp.max(scores, axis=-1, keepdims=True), jnp.maximum(fresh[0], fresh[1]))
         weights = jnp.exp(scores - top)
         total = jnp.sum(weights, axis=-1, keepdims=True)
-        mixed = dot(weights.astype(BF16), cache[slot, 1])
+        soft.append((weights.astype(BF16), total, [jnp.exp(x - top) for x in fresh]))
+    for slot in range(2):
+        weights, total, fresh = soft[slot]
+        fresh_value = kept_rows[slot][:, keys_at + HEAD_SIZE :]
+        mixed = dot(weights, cache[slot, 1])
         for t in range(STEPS):
-            weight = jnp.exp(fresh[t] - top)
-            total = total + weight
-            mixed = mixed + weight.astype(BF16).astype(F32) * fresh_value[t : t + 1]
+            total = total + fresh[t]
+            mixed = mixed + fresh[t].astype(BF16).astype(F32) * fresh_value[t : t + 1]
         outputs.append(mixed / total)
     halves = []
     for half in range(2):
@@ -212,8 +231,13 @@
     decay = jnp.exp(-step * jnp.exp(a_log[...]))
     d0, d1, s0, s1 = decay[0:1], decay[1:2], step[0:1], step[1:2]
     per_head = jnp.concatenate([d0, d0 * d1, s0, d1 * s0, s1, skip_gain[...], d0, d0], axis=0)
-    spread = jnp.where(iota((HEADS, INNER), 1) // 64 == iota((HEADS, INNER), 0), 1.0, 0.0)
-    wide = jnp.dot(per_head, spread, precision=lax.Precision.HIGHEST, preferred_element_type=F32)
+    spread = one_hot(iota((HEADS, INNER), 1) // 64 == iota((HEADS, INNER), 0))
+    wide, rest = None, per_head
+    for _ in range(3):
+        part = rest.astype(BF16)
+        rest = rest - part.astype(F32)
+        term = dot(part, spread)
+        wide = term if wide is None else wide + term
     c_high = c_out.astype(BF16)
     c_low = (c_out - c_high.astype(F32)).astype(BF16)
     whole = state[...]
@@ -343,7 +367,7 @@
     length_row = lengths.reshape(1, REQ)
     kept = (hidden, row(attn_gain), key_matrix, value_matrix, w_query)
     pieces, rows, slot_row, length_row, cache = call(
-        qkv_kernel, [(ATTN, 4, 1408), (ROWS, width), slot_row, length_row, kv_cache],
+        qkv_kernel, [(ATTN, STEPS, 2 * 1280 + LANES), (ROWS, width), slot_row, length_row, kv_cache],
         hidden, row(attn_gain), slot_row, length_row, key_matrix, value_matrix, w_query, kv_cache,
         near=True,
         scratch=[pltpu.VMEM(x.shape, x.dtype) for x in kept] + [pltpu.SemaphoreType.DMA((8,))],

time: 149 us -> 149 us (level)
  no operation moved by 1% of the time
where the time goes in v7:
time: 149 us; the launch traced here: 148 us
  blocking collectives  104 us (70%)
  starting transfers between devices  21.4 us (14%)
  waiting for transfers between devices  13.6 us (9%)
  Pallas kernels  9.27 us (6%)
    all_to_all x3, blocking collectives, on_device(): pieces = lax.all_to_all(pieces, 'attn', 0, 0)  58 us
    all_to_all x3, blocking collectives, exchange(): return lax.all_to_all(cut, axis, 0, 0).reshape(rows, columns)  45.8 us
    ppermute x3, starting transfers between devices, over_tp(): other = lax.ppermute(part, 'tp', [(k, k ^ 1) for k in range(TP)])  12.4 us
    ppermute x9, waiting for transfers between devices, over_tp(): lax.ppermute(pair, 'tp', [(k, (k + s) % TP) for k in range(TP)])  11 us
    pallas_call x13, Pallas kernels, call(): pl.pallas_call(kernel, out_shape=shapes, in_specs=[pl.BlockSpec(memory_sp...  9.27 us
    ppermute x9, starting transfers between devices, over_tp(): lax.ppermute(pair, 'tp', [(k, (k + s) % TP) for k in range(TP)])  9 us
  transfers between devices with their start and end apart: 12, of which 10 were waited for; matrix products, arithmetic and copies ran while one was open for 0% of the time, Pallas kernels for 0%

profile of v7, /device:TPU:1, one launch (start us, length us, event | category | flops | bytes accessed | tf_op | source)
XLA Modules:
  0.0 148.2 jit_solution(1219870925441475096)
XLA Ops:
  0.0 2.6 %shard_map.226 = (bf16[32,2,2688]{2,1,0:T(2,128)(2,1)S(1)}, bf16[64,256]{1,0:T(8,128)(2,1)S(1)}, s32[1,32]{1,0:T(1,128)S(1)}, s32[1,32]{1,0:T(1,128)S(1)}, bf16[2,2,4096,128]{3,2,1,0:T(8,128)(2,1)S(1)}) custom-call(bf16[32,2,256]{2,1,0:T(2,128)(2,1)} %hidden.1, f32[1,256]{1,0:T(1,128)} %bitcast.33, s32[1,32]{1,0:T(1,128)} %bitcast.34, s32[1,32]{1,0:T(1,128)} %bitcast.35, ...), custom_call_target="tpu_custom_call" | custom-call | bytes 16777216 | tf_op jit(solution)/shard_map/pallas_call | solution.py:309
  2.6 24.9 %all_to_all.30.pieces = bf16[32,2,2688]{2,1,0:T(2,128)(2,1)S(1)} all-to-all(bf16[32,2,2688]{2,1,0:T(2,128)(2,1)S(1)} %get-tuple-element.14), channel_id=1, replica_groups=mesh['attn'=32,'tp'=8] {'attn'}, dimensions={0} | all-to-all | bytes 688128 | tf_op jit(solution)/shard_map/all_to_all | solution.py:376
  27.6 1.4 shard_map.227
  29.0 15.1 %all_to_all.31 = bf16[32,8,512]{2,1,0:T(8,128)(2,1)S(1)} all-to-all(bf16[32,8,512]{2,1,0:T(8,128)(2,1)S(1)} %bitcast.25), channel_id=1, replica_groups=mesh['attn'=32,'tp'=8] {'attn'}, dimensions={0} | all-to-all | bytes 524288 | tf_op jit(solution)/shard_map/all_to_all | solution.py:324
  44.7 3.7 %collective-permute-start = (bf16[64,256]{1,0:T(8,128)(2,1)S(1)}, bf16[64,256]{1,0:T(8,128)(2,1)S(1)}, u32[]{:S(2)}, u32[]{:S(2)}) collective-permute-start(bf16[64,256]{1,0:T(8,128)(2,1)S(1)} %shard_map.228.own), channel_id=1, source_target_pairs={{0,1},{1,0},{2,3},{3,2},{4,5},{5,4},{6,7},{7,6},{8,9},{9,8},{10,11... | collective-permute-start | bytes 98312 | tf_op jit(solution)/shard_map/ppermute | solution.py:328
  48.3 0.9 collective-permute-done.other
  49.2 3.0 %collective-permute-start.3 = (bf16[64,256]{1,0:T(8,128)(2,1)S(1)}, bf16[64,256]{1,0:T(8,128)(2,1)S(1)}, u32[]{:S(2)}, u32[]{:S(2)}) collective-permute-start(bf16[64,256]{1,0:T(8,128)(2,1)S(1)} %shard_map.229.own), channel_id=1, source_target_pairs={{0,4},{1,5},{2,6},{3,7},{4,0},{5,1},{6,2},{7,3},{8,12},{9,13},{10,... | collective-permute-start | bytes 98312 | tf_op jit(solution)/shard_map/ppermute | solution.py:330
  53.7 1.4 collective-permute-done.2.after
  55.1 1.9 %collective-permute-done.1.before = bf16[64,256]{1,0:T(8,128)(2,1)S(1)} collective-permute-done((bf16[64,256]{1,0:T(8,128)(2,1)S(1)}, bf16[64,256]{1,0:T(8,128)(2,1)S(1)}, u32[]{:S(2)}, u32[]{:S(2)}) %collective-permute-start.1) | collective-permute-done | bytes 32800 | tf_op jit(solution)/shard_map/ppermute | solution.py:330
  57.8 19.4 %all_to_all.32.pieces = bf16[32,2,4736]{2,1,0:T(2,128)(2,1)S(1)} all-to-all(bf16[32,2,4736]{2,1,0:T(2,128)(2,1)S(1)} %get-tuple-element.19), channel_id=1, replica_groups=mesh['attn'=32,'tp'=8] {'attn'}, dimensions={0} | all-to-all | bytes 1212416 | tf_op jit(solution)/shard_map/all_to_all | solution.py:385
  77.3 1.4 shard_map.231
  78.7 16.6 %all_to_all.33 = bf16[32,8,512]{2,1,0:T(8,128)(2,1)S(1)} all-to-all(bf16[32,8,512]{2,1,0:T(8,128)(2,1)S(1)} %bitcast.20), channel_id=1, replica_groups=mesh['attn'=32,'tp'=8] {'attn'}, dimensions={0} | all-to-all | bytes 524288 | tf_op jit(solution)/shard_map/all_to_all | solution.py:324
  95.8 3.9 %collective-permute-start.4 = (bf16[64,256]{1,0:T(8,128)(2,1)S(1)}, bf16[64,256]{1,0:T(8,128)(2,1)S(1)}, u32[]{:S(2)}, u32[]{:S(2)}) collective-permute-start(bf16[64,256]{1,0:T(8,128)(2,1)S(1)} %shard_map.232.own), channel_id=1, source_target_pairs={{0,1},{1,0},{2,3},{3,2},{4,5},{5,4},{6,7},{7,6},{8,9},{9,8},{10,11... | collective-permute-start | bytes 98312 | tf_op jit(solution)/shard_map/ppermute | solution.py:328
  99.7 0.9 collective-permute-done.4.other
  100.6 1.2 collective-permute-start.7
  101.8 1.4 collective-permute-start.6
  103.2 1.7 %collective-permute-done.7.opposite = bf16[64,256]{1,0:T(8,128)(2,1)S(1)} collective-permute-done((bf16[64,256]{1,0:T(8,128)(2,1)S(1)}, bf16[64,256]{1,0:T(8,128)(2,1)S(1)}, u32[]{:S(2)}, u32[]{:S(2)}) %collective-permute-start.7) | collective-permute-done | bytes 32800 | tf_op jit(solution)/shard_map/ppermute | solution.py:330
  105.1 2.1 %collective-permute-done.5.before = bf16[64,256]{1,0:T(8,128)(2,1)S(1)} collective-permute-done((bf16[64,256]{1,0:T(8,128)(2,1)S(1)}, bf16[64,256]{1,0:T(8,128)(2,1)S(1)}, u32[]{:S(2)}, u32[]{:S(2)}) %collective-permute-start.5) | collective-permute-done | bytes 32800 | tf_op jit(solution)/shard_map/ppermute | solution.py:330
  107.7 13.6 %all_to_all.34.pieces = bf16[32,2,2176]{2,1,0:T(2,128)(2,1)S(1)} all-to-all(bf16[32,2,2176]{2,1,0:T(2,128)(2,1)S(1)} %get-tuple-element.21), channel_id=1, replica_groups=mesh['attn'=32,'tp'=8] {'attn'}, dimensions={0} | all-to-all | bytes 557056 | tf_op jit(solution)/shard_map/all_to_all | solution.py:397
  121.7 14.1 %all_to_all.35 = bf16[32,8,512]{2,1,0:T(8,128)(2,1)S(1)} all-to-all(bf16[32,8,512]{2,1,0:T(8,128)(2,1)S(1)} %bitcast.21), channel_id=1, replica_groups=mesh['attn'=32,'tp'=8] {'attn'}, dimensions={0} | all-to-all | bytes 524288 | tf_op jit(solution)/shard_map/all_to_all | solution.py:324
  136.3 4.8 %collective-permute-start.8 = (bf16[64,256]{1,0:T(8,128)(2,1)S(1)}, bf16[64,256]{1,0:T(8,128)(2,1)S(1)}, u32[]{:S(2)}, u32[]{:S(2)}) collective-permute-start(bf16[64,256]{1,0:T(8,128)(2,1)S(1)} %shard_map.236.own), channel_id=1, source_target_pairs={{0,1},{1,0},{2,3},{3,2},{4,5},{5,4},{6,7},{7,6},{8,9},{9,8},{10,11... | collective-permute-start | bytes 98312 | tf_op jit(solution)/shard_map/ppermute | solution.py:328
  142.4 1.2 collective-permute-start.10
  143.8 2.4 %collective-permute-done.11.opposite = bf16[64,256]{1,0:T(8,128)(2,1)S(1)} collective-permute-done((bf16[64,256]{1,0:T(8,128)(2,1)S(1)}, bf16[64,256]{1,0:T(8,128)(2,1)S(1)}, u32[]{:S(2)}, u32[]{:S(2)}) %collective-permute-start.11) | collective-permute-done | bytes 32800 | tf_op jit(solution)/shard_map/ppermute | solution.py:330
  146.3 1.3 collective-permute-done.9.before
  (51 shorter events, 7.2 us)
Async XLA Ops:
  2.6 54.4 %copy-start = (bf16[256,1,4608]{2,0,1:T(8,128)(2,1)S(1)}, bf16[256,1,4608]{2,0,1:T(8,128)(2,1)}, u32[]{:S(2)}) copy-start(bf16[256,1,4608]{2,0,1:T(8,128)(2,1)} %param.34) | copy-start | bytes 7077892
  2.6 54.4 %copy-start.8 = (bf16[256,32]{0,1:T(8,128)(2,1)S(1)}, bf16[256,32]{0,1:T(8,128)(2,1)}, u32[]{:S(2)}) copy-start(bf16[256,32]{0,1:T(8,128)(2,1)} %param.35) | copy-start | bytes 49156
  2.6 54.4 %copy-start.11 = (f32[256]{0:T(256)S(1)}, f32[256]{0:T(256)}, u32[]{:S(2)}) copy-start(f32[256]{0:T(256)} %param.33) | copy-start | bytes 3076
  27.6 49.7 %copy-start.9 = (f32[1,2560]{1,0:T(1,128)S(1)}, f32[1,2560]{1,0:T(1,128)}, u32[]{:S(2)}) copy-start(f32[1,2560]{1,0:T(1,128)} %conv_bias.1) | copy-start | bytes 30724
  27.6 49.7 %copy-start.10 = (f32[1,2048]{1,0:T(1,128)S(1)}, f32[1,2048]{1,0:T(1,128)}, u32[]{:S(2)}) copy-start(f32[1,2048]{1,0:T(1,128)} %group_gain.1) | copy-start | bytes 24580
  27.6 49.7 %copy-start.13 = (f32[32]{0:T(128)S(1)}, f32[32]{0:T(128)}, u32[]{:S(2)}) copy-start(f32[32]{0:T(128)} %param.41) | copy-start | bytes 388
  27.6 49.7 %copy-start.14 = (f32[32]{0:T(128)S(1)}, f32[32]{0:T(128)}, u32[]{:S(2)}) copy-start(f32[32]{0:T(128)} %param.42) | copy-start | bytes 388
  27.6 49.7 %copy-start.15 = (f32[32]{0:T(128)S(1)}, f32[32]{0:T(128)}, u32[]{:S(2)}) copy-start(f32[32]{0:T(128)} %param.43) | copy-start | bytes 388
  44.1 51.3 %copy-start.2 = (bf16[2048,256]{1,0:T(8,128)(2,1)S(1)}, bf16[2048,256]{1,0:T(8,128)(2,1)}, u32[]{:S(2)}) copy-start(bf16[2048,256]{1,0:T(8,128)(2,1)} %weight.4) | copy-start | bytes 3145732
  44.7 4.5 %collective-permute-start = (bf16[64,256]{1,0:T(8,128)(2,1)S(1)}, bf16[64,256]{1,0:T(8,128)(2,1)S(1)}, u32[]{:S(2)}, u32[]{:S(2)}) collective-permute-start(bf16[64,256]{1,0:T(8,128)(2,1)S(1)} %shard_map.228.own), channel_id=1, source_target_pairs={{0,1},{1,0},{2,3},{3,2},{4,5},{5,4},{6,7},{7,6},{8,9},{9,8},{10,11... | collective-permute-start | bytes 98312 | tf_op jit(solution)/shard_map/ppermute | solution.py:328
  49.2 4.5 %collective-permute-start.3 = (bf16[64,256]{1,0:T(8,128)(2,1)S(1)}, bf16[64,256]{1,0:T(8,128)(2,1)S(1)}, u32[]{:S(2)}, u32[]{:S(2)}) collective-permute-start(bf16[64,256]{1,0:T(8,128)(2,1)S(1)} %shard_map.229.own), channel_id=1, source_target_pairs={{0,4},{1,5},{2,6},{3,7},{4,0},{5,1},{6,2},{7,3},{8,12},{9,13},{10,... | collective-permute-start | bytes 98312 | tf_op jit(solution)/shard_map/ppermute | solution.py:330
  52.2 2.9 %collective-permute-start.2 = (bf16[64,256]{1,0:T(8,128)(2,1)S(1)}, bf16[64,256]{1,0:T(8,128)(2,1)S(1)}, u32[]{:S(2)}, u32[]{:S(2)}) collective-permute-start(bf16[64,256]{1,0:T(8,128)(2,1)S(1)} %shard_map.229.own), channel_id=1, source_target_pairs={{0,6},{1,7},{2,0},{3,1},{4,2},{5,3},{6,4},{7,5},{8,14},{9,15},{10,... | collective-permute-start | bytes 98312 | tf_op jit(solution)/shard_map/ppermute | solution.py:330
  53.0 4.0 %collective-permute-start.1 = (bf16[64,256]{1,0:T(8,128)(2,1)S(1)}, bf16[64,256]{1,0:T(8,128)(2,1)S(1)}, u32[]{:S(2)}, u32[]{:S(2)}) collective-permute-start(bf16[64,256]{1,0:T(8,128)(2,1)S(1)} %shard_map.229.own), channel_id=1, source_target_pairs={{0,2},{1,3},{2,4},{3,5},{4,6},{5,7},{6,0},{7,1},{8,10},{9,11},{10,... | collective-permute-start | bytes 98312 | tf_op jit(solution)/shard_map/ppermute | solution.py:330
  57.0 50.2 %copy-start.3 = (bf16[256,2048]{1,0:T(8,128)(2,1)S(1)}, bf16[256,2048]{1,0:T(8,128)(2,1)}, u32[]{:S(2)}) copy-start(bf16[256,2048]{1,0:T(8,128)(2,1)} %w_up.1) | copy-start | bytes 3145732
  57.0 50.2 %copy-start.12 = (f32[256]{0:T(256)S(1)}, f32[256]{0:T(256)}, u32[]{:S(2)}) copy-start(f32[256]{0:T(256)} %param.45) | copy-start | bytes 3076
  77.2 58.5 %copy-start.4 = (bf16[2048,256]{1,0:T(8,128)(2,1)S(1)}, bf16[2048,256]{1,0:T(8,128)(2,1)}, u32[]{:S(2)}) copy-start(bf16[2048,256]{1,0:T(8,128)(2,1)} %weight.5) | copy-start | bytes 3145732
  95.8 4.8 %collective-permute-start.4 = (bf16[64,256]{1,0:T(8,128)(2,1)S(1)}, bf16[64,256]{1,0:T(8,128)(2,1)S(1)}, u32[]{:S(2)}, u32[]{:S(2)}) collective-permute-start(bf16[64,256]{1,0:T(8,128)(2,1)S(1)} %shard_map.232.own), channel_id=1, source_target_pairs={{0,1},{1,0},{2,3},{3,2},{4,5},{5,4},{6,7},{7,6},{8,9},{9,8},{10,11... | collective-permute-start | bytes 98312 | tf_op jit(solution)/shard_map/ppermute | solution.py:328
  100.6 4.4 %collective-permute-start.7 = (bf16[64,256]{1,0:T(8,128)(2,1)S(1)}, bf16[64,256]{1,0:T(8,128)(2,1)S(1)}, u32[]{:S(2)}, u32[]{:S(2)}) collective-permute-start(bf16[64,256]{1,0:T(8,128)(2,1)S(1)} %shard_map.233.own), channel_id=1, source_target_pairs={{0,4},{1,5},{2,6},{3,7},{4,0},{5,1},{6,2},{7,3},{8,12},{9,13},{10,... | collective-permute-start | bytes 98312 | tf_op jit(solution)/shard_map/ppermute | solution.py:330
  101.8 3.3 %collective-permute-start.6 = (bf16[64,256]{1,0:T(8,128)(2,1)S(1)}, bf16[64,256]{1,0:T(8,128)(2,1)S(1)}, u32[]{:S(2)}, u32[]{:S(2)}) collective-permute-start(bf16[64,256]{1,0:T(8,128)(2,1)S(1)} %shard_map.233.own), channel_id=1, source_target_pairs={{0,6},{1,7},{2,0},{3,1},{4,2},{5,3},{6,4},{7,5},{8,14},{9,15},{10,... | collective-permute-start | bytes 98312 | tf_op jit(solution)/shard_map/ppermute | solution.py:330
  103.2 4.0 %collective-permute-start.5 = (bf16[64,256]{1,0:T(8,128)(2,1)S(1)}, bf16[64,256]{1,0:T(8,128)(2,1)S(1)}, u32[]{:S(2)}, u32[]{:S(2)}) collective-permute-start(bf16[64,256]{1,0:T(8,128)(2,1)S(1)} %shard_map.233.own), channel_id=1, source_target_pairs={{0,2},{1,3},{2,4},{3,5},{4,6},{5,7},{6,0},{7,1},{8,10},{9,11},{10,... | collective-permute-start | bytes 98312 | tf_op jit(solution)/shard_map/ppermute | solution.py:330
  136.3 5.7 %collective-permute-start.8 = (bf16[64,256]{1,0:T(8,128)(2,1)S(1)}, bf16[64,256]{1,0:T(8,128)(2,1)S(1)}, u32[]{:S(2)}, u32[]{:S(2)}) collective-permute-start(bf16[64,256]{1,0:T(8,128)(2,1)S(1)} %shard_map.236.own), channel_id=1, source_target_pairs={{0,1},{1,0},{2,3},{3,2},{4,5},{5,4},{6,7},{7,6},{8,9},{9,8},{10,11... | collective-permute-start | bytes 98312 | tf_op jit(solution)/shard_map/ppermute | solution.py:328
  141.9 4.4 %collective-permute-start.11 = (bf16[64,256]{1,0:T(8,128)(2,1)S(1)}, bf16[64,256]{1,0:T(8,128)(2,1)S(1)}, u32[]{:S(2)}, u32[]{:S(2)}) collective-permute-start(bf16[64,256]{1,0:T(8,128)(2,1)S(1)} %shard_map.237.own), channel_id=1, source_target_pairs={{0,4},{1,5},{2,6},{3,7},{4,0},{5,1},{6,2},{7,3},{8,12},{9,13},{10,... | collective-permute-start | bytes 98312 | tf_op jit(solution)/shard_map/ppermute | solution.py:330
  142.4 3.9 %collective-permute-start.10 = (bf16[64,256]{1,0:T(8,128)(2,1)S(1)}, bf16[64,256]{1,0:T(8,128)(2,1)S(1)}, u32[]{:S(2)}, u32[]{:S(2)}) collective-permute-start(bf16[64,256]{1,0:T(8,128)(2,1)S(1)} %shard_map.237.own), channel_id=1, source_target_pairs={{0,6},{1,7},{2,0},{3,1},{4,2},{5,3},{6,4},{7,5},{8,14},{9,15},{10,... | collective-permute-start | bytes 98312 | tf_op jit(solution)/shard_map/ppermute | solution.py:330
  143.6 4.0 %collective-permute-start.9 = (bf16[64,256]{1,0:T(8,128)(2,1)S(1)}, bf16[64,256]{1,0:T(8,128)(2,1)S(1)}, u32[]{:S(2)}, u32[]{:S(2)}) collective-permute-start(bf16[64,256]{1,0:T(8,128)(2,1)S(1)} %shard_map.237.own), channel_id=1, source_target_pairs={{0,2},{1,3},{2,4},{3,5},{4,6},{5,7},{6,0},{7,1},{8,10},{9,11},{10,... | collective-permute-start | bytes 98312 | tf_op jit(solution)/shard_map/ppermute | solution.py:330
  (4 other events, 190.5 us)

commit v8 on v7

--- a/solution.py
+++ b/solution.py
@@ -327,7 +327,7 @@
 def over_tp(part):
     other = lax.ppermute(part, "tp", [(k, k ^ 1) for k in range(TP)])
     pair = call(pair_kernel, [part.shape], part, other)
-    shifted = [lax.ppermute(pair, "tp", [(k, (k + s) % TP) for k in range(TP)]) for s in (4, 2, 6)]
+    shifted = [lax.ppermute(pair, "tp", [(k, k ^ s) for k in range(TP)]) for s in (4, 2, 6)]
     return [pair, shifted[1], shifted[2], shifted[0]]
 
 

time: 149 us -> 148 us (level)
  waiting for transfers between devices: 13.6 us -> 11.6 us
    ppermute x9, waiting for transfers between devices: 11 us -> 9.05 us  [over_tp(): lax.ppermute(pair, 'tp', [(k, k ^ s) for k in range(TP)])]
  transfers between devices with their start and end apart: 12 -> 12, of which waited for: 10 -> 9; matrix products, arithmetic and copies ran while one was open for 0% -> 0% of each run, Pallas kernels for 0% -> 0%
where the time goes in v8:
time: 148 us; the launch traced here: 147 us
  blocking collectives  105 us (71%)
  starting transfers between devices  21.2 us (14%)
  waiting for transfers between devices  11.6 us (8%)
  Pallas kernels  9.27 us (6%)
    all_to_all x3, blocking collectives, on_device(): pieces = lax.all_to_all(pieces, 'attn', 0, 0)  58.6 us
    all_to_all x3, blocking collectives, exchange(): return lax.all_to_all(cut, axis, 0, 0).reshape(rows, columns)  46.2 us
    ppermute x3, starting transfers between devices, over_tp(): other = lax.ppermute(part, 'tp', [(k, k ^ 1) for k in range(TP)])  12 us
    pallas_call x13, Pallas kernels, call(): pl.pallas_call(kernel, out_shape=shapes, in_specs=[pl.BlockSpec(memory_sp...  9.27 us
    ppermute x9, starting transfers between devices, over_tp(): lax.ppermute(pair, 'tp', [(k, k ^ s) for k in range(TP)])  9.25 us
    ppermute x9, waiting for transfers between devices, over_tp(): lax.ppermute(pair, 'tp', [(k, k ^ s) for k in range(TP)])  9.05 us
  transfers between devices with their start and end apart: 12, of which 9 were waited for; matrix products, arithmetic and copies ran while one was open for 0% of the time, Pallas kernels for 0%

profile of v8, /device:TPU:1, one launch (start us, length us, event | category | flops | bytes accessed | tf_op | source)
XLA Modules:
  0.0 147.2 jit_solution(6000518894213122753)
XLA Ops:
  0.0 2.6 %shard_map.226 = (bf16[32,2,2688]{2,1,0:T(2,128)(2,1)S(1)}, bf16[64,256]{1,0:T(8,128)(2,1)S(1)}, s32[1,32]{1,0:T(1,128)S(1)}, s32[1,32]{1,0:T(1,128)S(1)}, bf16[2,2,4096,128]{3,2,1,0:T(8,128)(2,1)S(1)}) custom-call(bf16[32,2,256]{2,1,0:T(2,128)(2,1)} %hidden.1, f32[1,256]{1,0:T(1,128)} %bitcast.33, s32[1,32]{1,0:T(1,128)} %bitcast.34, s32[1,32]{1,0:T(1,128)} %bitcast.35, ...), custom_call_target="tpu_custom_call" | custom-call | bytes 16777216 | tf_op jit(solution)/shard_map/pallas_call | solution.py:309
  2.6 24.9 %all_to_all.30.pieces = bf16[32,2,2688]{2,1,0:T(2,128)(2,1)S(1)} all-to-all(bf16[32,2,2688]{2,1,0:T(2,128)(2,1)S(1)} %get-tuple-element.14), channel_id=1, replica_groups=mesh['attn'=32,'tp'=8] {'attn'}, dimensions={0} | all-to-all | bytes 688128 | tf_op jit(solution)/shard_map/all_to_all | solution.py:376
  27.6 1.4 shard_map.227
  29.0 15.1 %all_to_all.31 = bf16[32,8,512]{2,1,0:T(8,128)(2,1)S(1)} all-to-all(bf16[32,8,512]{2,1,0:T(8,128)(2,1)S(1)} %bitcast.25), channel_id=1, replica_groups=mesh['attn'=32,'tp'=8] {'attn'}, dimensions={0} | all-to-all | bytes 524288 | tf_op jit(solution)/shard_map/all_to_all | solution.py:324
  44.7 3.7 %collective-permute-start = (bf16[64,256]{1,0:T(8,128)(2,1)S(1)}, bf16[64,256]{1,0:T(8,128)(2,1)S(1)}, u32[]{:S(2)}, u32[]{:S(2)}) collective-permute-start(bf16[64,256]{1,0:T(8,128)(2,1)S(1)} %shard_map.228.own), channel_id=1, source_target_pairs={{0,1},{1,0},{2,3},{3,2},{4,5},{5,4},{6,7},{7,6},{8,9},{9,8},{10,11... | collective-permute-start | bytes 98312 | tf_op jit(solution)/shard_map/ppermute | solution.py:328
  48.3 0.9 collective-permute-done.other
  49.2 3.0 %collective-permute-start.3 = (bf16[64,256]{1,0:T(8,128)(2,1)S(1)}, bf16[64,256]{1,0:T(8,128)(2,1)S(1)}, u32[]{:S(2)}, u32[]{:S(2)}) collective-permute-start(bf16[64,256]{1,0:T(8,128)(2,1)S(1)} %shard_map.229.own), channel_id=1, source_target_pairs={{0,4},{1,5},{2,6},{3,7},{4,0},{5,1},{6,2},{7,3},{8,12},{9,13},{10,... | collective-permute-start | bytes 98312 | tf_op jit(solution)/shard_map/ppermute | solution.py:330
  53.6 2.6 %collective-permute-done.2.after = bf16[64,256]{1,0:T(8,128)(2,1)S(1)} collective-permute-done((bf16[64,256]{1,0:T(8,128)(2,1)S(1)}, bf16[64,256]{1,0:T(8,128)(2,1)S(1)}, u32[]{:S(2)}, u32[]{:S(2)}) %collective-permute-start.2) | collective-permute-done | bytes 32800 | tf_op jit(solution)/shard_map/ppermute | solution.py:330
  57.1 20.0 %all_to_all.32.pieces = bf16[32,2,4736]{2,1,0:T(2,128)(2,1)S(1)} all-to-all(bf16[32,2,4736]{2,1,0:T(2,128)(2,1)S(1)} %get-tuple-element.19), channel_id=1, replica_groups=mesh['attn'=32,'tp'=8] {'attn'}, dimensions={0} | all-to-all | bytes 1212416 | tf_op jit(solution)/shard_map/all_to_all | solution.py:385
  77.1 1.4 shard_map.231
  78.5 16.4 %all_to_all.33 = bf16[32,8,512]{2,1,0:T(8,128)(2,1)S(1)} all-to-all(bf16[32,8,512]{2,1,0:T(8,128)(2,1)S(1)} %bitcast.20), channel_id=1, replica_groups=mesh['attn'=32,'tp'=8] {'attn'}, dimensions={0} | all-to-all | bytes 524288 | tf_op jit(solution)/shard_map/all_to_all | solution.py:324
  95.5 3.8 %collective-permute-start.4 = (bf16[64,256]{1,0:T(8,128)(2,1)S(1)}, bf16[64,256]{1,0:T(8,128)(2,1)S(1)}, u32[]{:S(2)}, u32[]{:S(2)}) collective-permute-start(bf16[64,256]{1,0:T(8,128)(2,1)S(1)} %shard_map.232.own), channel_id=1, source_target_pairs={{0,1},{1,0},{2,3},{3,2},{4,5},{5,4},{6,7},{7,6},{8,9},{9,8},{10,11... | collective-permute-start | bytes 98312 | tf_op jit(solution)/shard_map/ppermute | solution.py:328
  99.3 0.9 collective-permute-done.4.other
  100.2 1.7 %collective-permute-start.7 = (bf16[64,256]{1,0:T(8,128)(2,1)S(1)}, bf16[64,256]{1,0:T(8,128)(2,1)S(1)}, u32[]{:S(2)}, u32[]{:S(2)}) collective-permute-start(bf16[64,256]{1,0:T(8,128)(2,1)S(1)} %shard_map.233.own), channel_id=1, source_target_pairs={{0,4},{1,5},{2,6},{3,7},{4,0},{5,1},{6,2},{7,3},{8,12},{9,13},{10,... | collective-permute-start | bytes 98312 | tf_op jit(solution)/shard_map/ppermute | solution.py:330
  102.9 1.6 %collective-permute-done.7.opposite = bf16[64,256]{1,0:T(8,128)(2,1)S(1)} collective-permute-done((bf16[64,256]{1,0:T(8,128)(2,1)S(1)}, bf16[64,256]{1,0:T(8,128)(2,1)S(1)}, u32[]{:S(2)}, u32[]{:S(2)}) %collective-permute-start.7) | collective-permute-done | bytes 32800 | tf_op jit(solution)/shard_map/ppermute | solution.py:330
  104.5 1.4 collective-permute-done.6.after
  106.4 13.6 %all_to_all.34.pieces = bf16[32,2,2176]{2,1,0:T(2,128)(2,1)S(1)} all-to-all(bf16[32,2,2176]{2,1,0:T(2,128)(2,1)S(1)} %get-tuple-element.21), channel_id=1, replica_groups=mesh['attn'=32,'tp'=8] {'attn'}, dimensions={0} | all-to-all | bytes 557056 | tf_op jit(solution)/shard_map/all_to_all | solution.py:397
  120.4 14.7 %all_to_all.35 = bf16[32,8,512]{2,1,0:T(8,128)(2,1)S(1)} all-to-all(bf16[32,8,512]{2,1,0:T(8,128)(2,1)S(1)} %bitcast.21), channel_id=1, replica_groups=mesh['attn'=32,'tp'=8] {'attn'}, dimensions={0} | all-to-all | bytes 524288 | tf_op jit(solution)/shard_map/all_to_all | solution.py:324
  135.6 4.5 %collective-permute-start.8 = (bf16[64,256]{1,0:T(8,128)(2,1)S(1)}, bf16[64,256]{1,0:T(8,128)(2,1)S(1)}, u32[]{:S(2)}, u32[]{:S(2)}) collective-permute-start(bf16[64,256]{1,0:T(8,128)(2,1)S(1)} %shard_map.236.own), channel_id=1, source_target_pairs={{0,1},{1,0},{2,3},{3,2},{4,5},{5,4},{6,7},{7,6},{8,9},{9,8},{10,11... | collective-permute-start | bytes 98312 | tf_op jit(solution)/shard_map/ppermute | solution.py:328
  140.0 0.9 collective-permute-done.8.other
  140.9 1.6 %collective-permute-start.11 = (bf16[64,256]{1,0:T(8,128)(2,1)S(1)}, bf16[64,256]{1,0:T(8,128)(2,1)S(1)}, u32[]{:S(2)}, u32[]{:S(2)}) collective-permute-start(bf16[64,256]{1,0:T(8,128)(2,1)S(1)} %shard_map.237.own), channel_id=1, source_target_pairs={{0,4},{1,5},{2,6},{3,7},{4,0},{5,1},{6,2},{7,3},{8,12},{9,13},{10,... | collective-permute-start | bytes 98312 | tf_op jit(solution)/shard_map/ppermute | solution.py:330
  142.5 1.1 collective-permute-start.10
  143.6 1.6 %collective-permute-done.11.opposite = bf16[64,256]{1,0:T(8,128)(2,1)S(1)} collective-permute-done((bf16[64,256]{1,0:T(8,128)(2,1)S(1)}, bf16[64,256]{1,0:T(8,128)(2,1)S(1)}, u32[]{:S(2)}, u32[]{:S(2)}) %collective-permute-start.11) | collective-permute-done | bytes 32800 | tf_op jit(solution)/shard_map/ppermute | solution.py:330
  145.3 1.2 collective-permute-done.10.after
  (51 shorter events, 6.4 us)
Async XLA Ops:
  2.6 53.6 %copy-start = (bf16[256,1,4608]{2,0,1:T(8,128)(2,1)S(1)}, bf16[256,1,4608]{2,0,1:T(8,128)(2,1)}, u32[]{:S(2)}) copy-start(bf16[256,1,4608]{2,0,1:T(8,128)(2,1)} %param.34) | copy-start | bytes 7077892
  2.6 53.6 %copy-start.8 = (bf16[256,32]{0,1:T(8,128)(2,1)S(1)}, bf16[256,32]{0,1:T(8,128)(2,1)}, u32[]{:S(2)}) copy-start(bf16[256,32]{0,1:T(8,128)(2,1)} %param.35) | copy-start | bytes 49156
  2.6 53.6 %copy-start.11 = (f32[256]{0:T(256)S(1)}, f32[256]{0:T(256)}, u32[]{:S(2)}) copy-start(f32[256]{0:T(256)} %param.33) | copy-start | bytes 3076
  27.6 49.5 %copy-start.9 = (f32[1,2560]{1,0:T(1,128)S(1)}, f32[1,2560]{1,0:T(1,128)}, u32[]{:S(2)}) copy-start(f32[1,2560]{1,0:T(1,128)} %conv_bias.1) | copy-start | bytes 30724
  27.6 49.5 %copy-start.10 = (f32[1,2048]{1,0:T(1,128)S(1)}, f32[1,2048]{1,0:T(1,128)}, u32[]{:S(2)}) copy-start(f32[1,2048]{1,0:T(1,128)} %group_gain.1) | copy-start | bytes 24580
  27.6 49.5 %copy-start.13 = (f32[32]{0:T(128)S(1)}, f32[32]{0:T(128)}, u32[]{:S(2)}) copy-start(f32[32]{0:T(128)} %param.41) | copy-start | bytes 388
  27.6 49.5 %copy-start.14 = (f32[32]{0:T(128)S(1)}, f32[32]{0:T(128)}, u32[]{:S(2)}) copy-start(f32[32]{0:T(128)} %param.42) | copy-start | bytes 388
  27.6 49.5 %copy-start.15 = (f32[32]{0:T(128)S(1)}, f32[32]{0:T(128)}, u32[]{:S(2)}) copy-start(f32[32]{0:T(128)} %param.43) | copy-start | bytes 388
  44.1 50.9 %copy-start.2 = (bf16[2048,256]{1,0:T(8,128)(2,1)S(1)}, bf16[2048,256]{1,0:T(8,128)(2,1)}, u32[]{:S(2)}) copy-start(bf16[2048,256]{1,0:T(8,128)(2,1)} %weight.4) | copy-start | bytes 3145732
  44.7 4.5 %collective-permute-start = (bf16[64,256]{1,0:T(8,128)(2,1)S(1)}, bf16[64,256]{1,0:T(8,128)(2,1)S(1)}, u32[]{:S(2)}, u32[]{:S(2)}) collective-permute-start(bf16[64,256]{1,0:T(8,128)(2,1)S(1)} %shard_map.228.own), channel_id=1, source_target_pairs={{0,1},{1,0},{2,3},{3,2},{4,5},{5,4},{6,7},{7,6},{8,9},{9,8},{10,11... | collective-permute-start | bytes 98312 | tf_op jit(solution)/shard_map/ppermute | solution.py:328
  49.2 4.4 %collective-permute-start.3 = (bf16[64,256]{1,0:T(8,128)(2,1)S(1)}, bf16[64,256]{1,0:T(8,128)(2,1)S(1)}, u32[]{:S(2)}, u32[]{:S(2)}) collective-permute-start(bf16[64,256]{1,0:T(8,128)(2,1)S(1)} %shard_map.229.own), channel_id=1, source_target_pairs={{0,4},{1,5},{2,6},{3,7},{4,0},{5,1},{6,2},{7,3},{8,12},{9,13},{10,... | collective-permute-start | bytes 98312 | tf_op jit(solution)/shard_map/ppermute | solution.py:330
  52.2 4.0 %collective-permute-start.2 = (bf16[64,256]{1,0:T(8,128)(2,1)S(1)}, bf16[64,256]{1,0:T(8,128)(2,1)S(1)}, u32[]{:S(2)}, u32[]{:S(2)}) collective-permute-start(bf16[64,256]{1,0:T(8,128)(2,1)S(1)} %shard_map.229.own), channel_id=1, source_target_pairs={{0,6},{1,7},{2,4},{3,5},{4,2},{5,3},{6,0},{7,1},{8,14},{9,15},{10,... | collective-permute-start | bytes 98312 | tf_op jit(solution)/shard_map/ppermute | solution.py:330
  53.0 3.2 %collective-permute-start.1 = (bf16[64,256]{1,0:T(8,128)(2,1)S(1)}, bf16[64,256]{1,0:T(8,128)(2,1)S(1)}, u32[]{:S(2)}, u32[]{:S(2)}) collective-permute-start(bf16[64,256]{1,0:T(8,128)(2,1)S(1)} %shard_map.229.own), channel_id=1, source_target_pairs={{0,2},{1,3},{2,0},{3,1},{4,6},{5,7},{6,4},{7,5},{8,10},{9,11},{10,... | collective-permute-start | bytes 98312 | tf_op jit(solution)/shard_map/ppermute | solution.py:330
  56.2 49.7 %copy-start.3 = (bf16[256,2048]{1,0:T(8,128)(2,1)S(1)}, bf16[256,2048]{1,0:T(8,128)(2,1)}, u32[]{:S(2)}) copy-start(bf16[256,2048]{1,0:T(8,128)(2,1)} %w_up.1) | copy-start | bytes 3145732
  56.2 49.7 %copy-start.12 = (f32[256]{0:T(256)S(1)}, f32[256]{0:T(256)}, u32[]{:S(2)}) copy-start(f32[256]{0:T(256)} %param.45) | copy-start | bytes 3076
  77.1 58.0 %copy-start.4 = (bf16[2048,256]{1,0:T(8,128)(2,1)S(1)}, bf16[2048,256]{1,0:T(8,128)(2,1)}, u32[]{:S(2)}) copy-start(bf16[2048,256]{1,0:T(8,128)(2,1)} %weight.5) | copy-start | bytes 3145732
  95.5 4.7 %collective-permute-start.4 = (bf16[64,256]{1,0:T(8,128)(2,1)S(1)}, bf16[64,256]{1,0:T(8,128)(2,1)S(1)}, u32[]{:S(2)}, u32[]{:S(2)}) collective-permute-start(bf16[64,256]{1,0:T(8,128)(2,1)S(1)} %shard_map.232.own), channel_id=1, source_target_pairs={{0,1},{1,0},{2,3},{3,2},{4,5},{5,4},{6,7},{7,6},{8,9},{9,8},{10,11... | collective-permute-start | bytes 98312 | tf_op jit(solution)/shard_map/ppermute | solution.py:328
  100.2 4.4 %collective-permute-start.7 = (bf16[64,256]{1,0:T(8,128)(2,1)S(1)}, bf16[64,256]{1,0:T(8,128)(2,1)S(1)}, u32[]{:S(2)}, u32[]{:S(2)}) collective-permute-start(bf16[64,256]{1,0:T(8,128)(2,1)S(1)} %shard_map.233.own), channel_id=1, source_target_pairs={{0,4},{1,5},{2,6},{3,7},{4,0},{5,1},{6,2},{7,3},{8,12},{9,13},{10,... | collective-permute-start | bytes 98312 | tf_op jit(solution)/shard_map/ppermute | solution.py:330
  101.9 4.0 %collective-permute-start.6 = (bf16[64,256]{1,0:T(8,128)(2,1)S(1)}, bf16[64,256]{1,0:T(8,128)(2,1)S(1)}, u32[]{:S(2)}, u32[]{:S(2)}) collective-permute-start(bf16[64,256]{1,0:T(8,128)(2,1)S(1)} %shard_map.233.own), channel_id=1, source_target_pairs={{0,6},{1,7},{2,4},{3,5},{4,2},{5,3},{6,0},{7,1},{8,14},{9,15},{10,... | collective-permute-start | bytes 98312 | tf_op jit(solution)/shard_map/ppermute | solution.py:330
  102.7 3.2 %collective-permute-start.5 = (bf16[64,256]{1,0:T(8,128)(2,1)S(1)}, bf16[64,256]{1,0:T(8,128)(2,1)S(1)}, u32[]{:S(2)}, u32[]{:S(2)}) collective-permute-start(bf16[64,256]{1,0:T(8,128)(2,1)S(1)} %shard_map.233.own), channel_id=1, source_target_pairs={{0,2},{1,3},{2,0},{3,1},{4,6},{5,7},{6,4},{7,5},{8,10},{9,11},{10,... | collective-permute-start | bytes 98312 | tf_op jit(solution)/shard_map/ppermute | solution.py:330
  135.6 5.3 %collective-permute-start.8 = (bf16[64,256]{1,0:T(8,128)(2,1)S(1)}, bf16[64,256]{1,0:T(8,128)(2,1)S(1)}, u32[]{:S(2)}, u32[]{:S(2)}) collective-permute-start(bf16[64,256]{1,0:T(8,128)(2,1)S(1)} %shard_map.236.own), channel_id=1, source_target_pairs={{0,1},{1,0},{2,3},{3,2},{4,5},{5,4},{6,7},{7,6},{8,9},{9,8},{10,11... | collective-permute-start | bytes 98312 | tf_op jit(solution)/shard_map/ppermute | solution.py:328
  140.9 4.4 %collective-permute-start.11 = (bf16[64,256]{1,0:T(8,128)(2,1)S(1)}, bf16[64,256]{1,0:T(8,128)(2,1)S(1)}, u32[]{:S(2)}, u32[]{:S(2)}) collective-permute-start(bf16[64,256]{1,0:T(8,128)(2,1)S(1)} %shard_map.237.own), channel_id=1, source_target_pairs={{0,4},{1,5},{2,6},{3,7},{4,0},{5,1},{6,2},{7,3},{8,12},{9,13},{10,... | collective-permute-start | bytes 98312 | tf_op jit(solution)/shard_map/ppermute | solution.py:330
  142.5 4.0 %collective-permute-start.10 = (bf16[64,256]{1,0:T(8,128)(2,1)S(1)}, bf16[64,256]{1,0:T(8,128)(2,1)S(1)}, u32[]{:S(2)}, u32[]{:S(2)}) collective-permute-start(bf16[64,256]{1,0:T(8,128)(2,1)S(1)} %shard_map.237.own), channel_id=1, source_target_pairs={{0,6},{1,7},{2,4},{3,5},{4,2},{5,3},{6,0},{7,1},{8,14},{9,15},{10,... | collective-permute-start | bytes 98312 | tf_op jit(solution)/shard_map/ppermute | solution.py:330
  143.6 2.9 %collective-permute-start.9 = (bf16[64,256]{1,0:T(8,128)(2,1)S(1)}, bf16[64,256]{1,0:T(8,128)(2,1)S(1)}, u32[]{:S(2)}, u32[]{:S(2)}) collective-permute-start(bf16[64,256]{1,0:T(8,128)(2,1)S(1)} %shard_map.237.own), channel_id=1, source_target_pairs={{0,2},{1,3},{2,0},{3,1},{4,6},{5,7},{6,4},{7,5},{8,10},{9,11},{10,... | collective-permute-start | bytes 98312 | tf_op jit(solution)/shard_map/ppermute | solution.py:330
  (4 other events, 190.1 us)

commit v9 on v8

--- a/solution.py
+++ b/solution.py
@@ -49,6 +49,13 @@
 def sum_pieces(ref, pieces):
     rows = ref.shape[0] // pieces
     return jnp.sum(ref[...].astype(F32).reshape(pieces, rows, ref.shape[1]), axis=0)
+
+
+def sum_by_step(ref):
+    devices, steps, columns = ref.shape
+    rows = ref[...].reshape(devices * steps, columns)
+    row, source = iota((8, devices * steps), 0), iota((8, devices * steps), 1)
+    return dot(one_hot(source % steps == row), rows)[:steps]
 
 
 def write_copies(ref, piece, copies):
@@ -104,7 +111,7 @@
 
 def attend_kernel(pieces, lengths, slot_of, cache, out):
     first_slot = lax.axis_index("attn") * 2
-    summed = jnp.sum(pieces[...].astype(F32), axis=0)
+    summed = sum_by_step(pieces)
     keys_at = 8 * HEAD_SIZE
     columns = keys_at + 2 * HEAD_SIZE
     both_rows = []
@@ -206,7 +213,7 @@
 def mamba_kernel(
     pieces, conv_weight, conv_bias, conv_state, state, a_log, dt_bias, skip_gain, group_gain, out
 ):
-    summed = jnp.sum(pieces[...].astype(F32), axis=0)
+    summed = sum_by_step(pieces)
     state_at = 2 * INNER
     steps_at = state_at + 2 * STATES
     last = summed[:, steps_at:]
@@ -283,7 +290,7 @@
 
 
 def active_kernel(pieces, out):
-    summed = jnp.sum(pieces[...].astype(F32), axis=0)
+    summed = sum_by_step(pieces)
     lifted = jnp.maximum(summed[:, :INNER] * scale_of(summed[:, INNER:]), 0.0)
     active = lifted * lifted
     piece = jnp.concatenate([active[:, q * 512 : (q + 1) * 512] for q in range(4)], axis=0)

time: 148 us -> 147 us (level)
  no operation moved by 1% of the time
where the time goes in v9:
time: 147 us
  blocking collectives  105 us (71%)
  starting transfers between devices  21.2 us (14%)
  waiting for transfers between devices  11.6 us (8%)
  Pallas kernels  9.13 us (6%)
    all_to_all x3, blocking collectives, on_device(): pieces = lax.all_to_all(pieces, 'attn', 0, 0)  58.6 us
    all_to_all x3, blocking collectives, exchange(): return lax.all_to_all(cut, axis, 0, 0).reshape(rows, columns)  46 us
    ppermute x3, starting transfers between devices, over_tp(): other = lax.ppermute(part, 'tp', [(k, k ^ 1) for k in range(TP)])  12 us
    ppermute x9, starting transfers between devices, over_tp(): lax.ppermute(pair, 'tp', [(k, k ^ s) for k in range(TP)])  9.25 us
    pallas_call x13, Pallas kernels, call(): pl.pallas_call(kernel, out_shape=shapes, in_specs=[pl.BlockSpec(memory_sp...  9.13 us
    ppermute x9, waiting for transfers between devices, over_tp(): lax.ppermute(pair, 'tp', [(k, k ^ s) for k in range(TP)])  9.05 us
  transfers between devices with their start and end apart: 12, of which 9 were waited for; matrix products, arithmetic and copies ran while one was open for 0% of the time, Pallas kernels for 0%

profile of v9, /device:TPU:1, one launch (start us, length us, event | category | flops | bytes accessed | tf_op | source)
XLA Modules:
  0.0 146.8 jit_solution(15018602054606653582)
XLA Ops:
  0.0 2.6 %shard_map.226 = (bf16[32,2,2688]{2,1,0:T(2,128)(2,1)S(1)}, bf16[64,256]{1,0:T(8,128)(2,1)S(1)}, s32[1,32]{1,0:T(1,128)S(1)}, s32[1,32]{1,0:T(1,128)S(1)}, bf16[2,2,4096,128]{3,2,1,0:T(8,128)(2,1)S(1)}) custom-call(bf16[32,2,256]{2,1,0:T(2,128)(2,1)} %hidden.1, f32[1,256]{1,0:T(1,128)} %bitcast.33, s32[1,32]{1,0:T(1,128)} %bitcast.34, s32[1,32]{1,0:T(1,128)} %bitcast.35, ...), custom_call_target="tpu_custom_call" | custom-call | bytes 16777216 | tf_op jit(solution)/shard_map/pallas_call | solution.py:316
  2.6 24.9 %all_to_all.30.pieces = bf16[32,2,2688]{2,1,0:T(2,128)(2,1)S(1)} all-to-all(bf16[32,2,2688]{2,1,0:T(2,128)(2,1)S(1)} %get-tuple-element.14), channel_id=1, replica_groups=mesh['attn'=32,'tp'=8] {'attn'}, dimensions={0} | all-to-all | bytes 688128 | tf_op jit(solution)/shard_map/all_to_all | solution.py:383
  27.6 1.3 shard_map.227
  29.0 15.1 %all_to_all.31 = bf16[32,8,512]{2,1,0:T(8,128)(2,1)S(1)} all-to-all(bf16[32,8,512]{2,1,0:T(8,128)(2,1)S(1)} %bitcast.25), channel_id=1, replica_groups=mesh['attn'=32,'tp'=8] {'attn'}, dimensions={0} | all-to-all | bytes 524288 | tf_op jit(solution)/shard_map/all_to_all | solution.py:331
  44.6 3.7 %collective-permute-start = (bf16[64,256]{1,0:T(8,128)(2,1)S(1)}, bf16[64,256]{1,0:T(8,128)(2,1)S(1)}, u32[]{:S(2)}, u32[]{:S(2)}) collective-permute-start(bf16[64,256]{1,0:T(8,128)(2,1)S(1)} %shard_map.228.own), channel_id=1, source_target_pairs={{0,1},{1,0},{2,3},{3,2},{4,5},{5,4},{6,7},{7,6},{8,9},{9,8},{10,11... | collective-permute-start | bytes 98312 | tf_op jit(solution)/shard_map/ppermute | solution.py:335
  48.3 0.9 collective-permute-done.other
  49.2 3.0 %collective-permute-start.3 = (bf16[64,256]{1,0:T(8,128)(2,1)S(1)}, bf16[64,256]{1,0:T(8,128)(2,1)S(1)}, u32[]{:S(2)}, u32[]{:S(2)}) collective-permute-start(bf16[64,256]{1,0:T(8,128)(2,1)S(1)} %shard_map.229.own), channel_id=1, source_target_pairs={{0,4},{1,5},{2,6},{3,7},{4,0},{5,1},{6,2},{7,3},{8,12},{9,13},{10,... | collective-permute-start | bytes 98312 | tf_op jit(solution)/shard_map/ppermute | solution.py:337
  53.5 2.6 %collective-permute-done.2.after = bf16[64,256]{1,0:T(8,128)(2,1)S(1)} collective-permute-done((bf16[64,256]{1,0:T(8,128)(2,1)S(1)}, bf16[64,256]{1,0:T(8,128)(2,1)S(1)}, u32[]{:S(2)}, u32[]{:S(2)}) %collective-permute-start.2) | collective-permute-done | bytes 32800 | tf_op jit(solution)/shard_map/ppermute | solution.py:337
  57.0 20.0 %all_to_all.32.pieces = bf16[32,2,4736]{2,1,0:T(2,128)(2,1)S(1)} all-to-all(bf16[32,2,4736]{2,1,0:T(2,128)(2,1)S(1)} %get-tuple-element.19), channel_id=1, replica_groups=mesh['attn'=32,'tp'=8] {'attn'}, dimensions={0} | all-to-all | bytes 1212416 | tf_op jit(solution)/shard_map/all_to_all | solution.py:392
  77.1 1.3 shard_map.231
  78.4 16.4 %all_to_all.33 = bf16[32,8,512]{2,1,0:T(8,128)(2,1)S(1)} all-to-all(bf16[32,8,512]{2,1,0:T(8,128)(2,1)S(1)} %bitcast.20), channel_id=1, replica_groups=mesh['attn'=32,'tp'=8] {'attn'}, dimensions={0} | all-to-all | bytes 524288 | tf_op jit(solution)/shard_map/all_to_all | solution.py:331
  95.3 3.8 %collective-permute-start.4 = (bf16[64,256]{1,0:T(8,128)(2,1)S(1)}, bf16[64,256]{1,0:T(8,128)(2,1)S(1)}, u32[]{:S(2)}, u32[]{:S(2)}) collective-permute-start(bf16[64,256]{1,0:T(8,128)(2,1)S(1)} %shard_map.232.own), channel_id=1, source_target_pairs={{0,1},{1,0},{2,3},{3,2},{4,5},{5,4},{6,7},{7,6},{8,9},{9,8},{10,11... | collective-permute-start | bytes 98312 | tf_op jit(solution)/shard_map/ppermute | solution.py:335
  99.2 0.9 collective-permute-done.4.other
  100.0 1.7 %collective-permute-start.7 = (bf16[64,256]{1,0:T(8,128)(2,1)S(1)}, bf16[64,256]{1,0:T(8,128)(2,1)S(1)}, u32[]{:S(2)}, u32[]{:S(2)}) collective-permute-start(bf16[64,256]{1,0:T(8,128)(2,1)S(1)} %shard_map.233.own), channel_id=1, source_target_pairs={{0,4},{1,5},{2,6},{3,7},{4,0},{5,1},{6,2},{7,3},{8,12},{9,13},{10,... | collective-permute-start | bytes 98312 | tf_op jit(solution)/shard_map/ppermute | solution.py:337
  102.8 1.6 %collective-permute-done.7.opposite = bf16[64,256]{1,0:T(8,128)(2,1)S(1)} collective-permute-done((bf16[64,256]{1,0:T(8,128)(2,1)S(1)}, bf16[64,256]{1,0:T(8,128)(2,1)S(1)}, u32[]{:S(2)}, u32[]{:S(2)}) %collective-permute-start.7) | collective-permute-done | bytes 32800 | tf_op jit(solution)/shard_map/ppermute | solution.py:337
  104.4 1.4 collective-permute-done.6.after
  106.3 13.6 %all_to_all.34.pieces = bf16[32,2,2176]{2,1,0:T(2,128)(2,1)S(1)} all-to-all(bf16[32,2,2176]{2,1,0:T(2,128)(2,1)S(1)} %get-tuple-element.21), channel_id=1, replica_groups=mesh['attn'=32,'tp'=8] {'attn'}, dimensions={0} | all-to-all | bytes 557056 | tf_op jit(solution)/shard_map/all_to_all | solution.py:404
  120.2 14.5 %all_to_all.35 = bf16[32,8,512]{2,1,0:T(8,128)(2,1)S(1)} all-to-all(bf16[32,8,512]{2,1,0:T(8,128)(2,1)S(1)} %bitcast.21), channel_id=1, replica_groups=mesh['attn'=32,'tp'=8] {'attn'}, dimensions={0} | all-to-all | bytes 524288 | tf_op jit(solution)/shard_map/all_to_all | solution.py:331
  135.2 4.5 %collective-permute-start.8 = (bf16[64,256]{1,0:T(8,128)(2,1)S(1)}, bf16[64,256]{1,0:T(8,128)(2,1)S(1)}, u32[]{:S(2)}, u32[]{:S(2)}) collective-permute-start(bf16[64,256]{1,0:T(8,128)(2,1)S(1)} %shard_map.236.own), channel_id=1, source_target_pairs={{0,1},{1,0},{2,3},{3,2},{4,5},{5,4},{6,7},{7,6},{8,9},{9,8},{10,11... | collective-permute-start | bytes 98312 | tf_op jit(solution)/shard_map/ppermute | solution.py:335
  139.7 0.9 collective-permute-done.8.other
  140.6 1.6 %collective-permute-start.11 = (bf16[64,256]{1,0:T(8,128)(2,1)S(1)}, bf16[64,256]{1,0:T(8,128)(2,1)S(1)}, u32[]{:S(2)}, u32[]{:S(2)}) collective-permute-start(bf16[64,256]{1,0:T(8,128)(2,1)S(1)} %shard_map.237.own), channel_id=1, source_target_pairs={{0,4},{1,5},{2,6},{3,7},{4,0},{5,1},{6,2},{7,3},{8,12},{9,13},{10,... | collective-permute-start | bytes 98312 | tf_op jit(solution)/shard_map/ppermute | solution.py:337
  142.2 1.1 collective-permute-start.10
  143.3 1.6 %collective-permute-done.11.opposite = bf16[64,256]{1,0:T(8,128)(2,1)S(1)} collective-permute-done((bf16[64,256]{1,0:T(8,128)(2,1)S(1)}, bf16[64,256]{1,0:T(8,128)(2,1)S(1)}, u32[]{:S(2)}, u32[]{:S(2)}) %collective-permute-start.11) | collective-permute-done | bytes 32800 | tf_op jit(solution)/shard_map/ppermute | solution.py:337
  144.9 1.2 collective-permute-done.10.after
  (51 shorter events, 6.4 us)
Async XLA Ops:
  2.6 53.6 %copy-start = (bf16[256,1,4608]{2,0,1:T(8,128)(2,1)S(1)}, bf16[256,1,4608]{2,0,1:T(8,128)(2,1)}, u32[]{:S(2)}) copy-start(bf16[256,1,4608]{2,0,1:T(8,128)(2,1)} %param.34) | copy-start | bytes 7077892
  2.6 53.6 %copy-start.8 = (bf16[256,32]{0,1:T(8,128)(2,1)S(1)}, bf16[256,32]{0,1:T(8,128)(2,1)}, u32[]{:S(2)}) copy-start(bf16[256,32]{0,1:T(8,128)(2,1)} %param.35) | copy-start | bytes 49156
  2.6 53.6 %copy-start.11 = (f32[256]{0:T(256)S(1)}, f32[256]{0:T(256)}, u32[]{:S(2)}) copy-start(f32[256]{0:T(256)} %param.33) | copy-start | bytes 3076
  27.6 49.5 %copy-start.9 = (f32[1,2560]{1,0:T(1,128)S(1)}, f32[1,2560]{1,0:T(1,128)}, u32[]{:S(2)}) copy-start(f32[1,2560]{1,0:T(1,128)} %conv_bias.1) | copy-start | bytes 30724
  27.6 49.5 %copy-start.10 = (f32[1,2048]{1,0:T(1,128)S(1)}, f32[1,2048]{1,0:T(1,128)}, u32[]{:S(2)}) copy-start(f32[1,2048]{1,0:T(1,128)} %group_gain.1) | copy-start | bytes 24580
  27.6 49.5 %copy-start.13 = (f32[32]{0:T(128)S(1)}, f32[32]{0:T(128)}, u32[]{:S(2)}) copy-start(f32[32]{0:T(128)} %param.41) | copy-start | bytes 388
  27.6 49.5 %copy-start.14 = (f32[32]{0:T(128)S(1)}, f32[32]{0:T(128)}, u32[]{:S(2)}) copy-start(f32[32]{0:T(128)} %param.42) | copy-start | bytes 388
  27.6 49.5 %copy-start.15 = (f32[32]{0:T(128)S(1)}, f32[32]{0:T(128)}, u32[]{:S(2)}) copy-start(f32[32]{0:T(128)} %param.43) | copy-start | bytes 388
  44.0 50.8 %copy-start.2 = (bf16[2048,256]{1,0:T(8,128)(2,1)S(1)}, bf16[2048,256]{1,0:T(8,128)(2,1)}, u32[]{:S(2)}) copy-start(bf16[2048,256]{1,0:T(8,128)(2,1)} %weight.4) | copy-start | bytes 3145732
  44.6 4.5 %collective-permute-start = (bf16[64,256]{1,0:T(8,128)(2,1)S(1)}, bf16[64,256]{1,0:T(8,128)(2,1)S(1)}, u32[]{:S(2)}, u32[]{:S(2)}) collective-permute-start(bf16[64,256]{1,0:T(8,128)(2,1)S(1)} %shard_map.228.own), channel_id=1, source_target_pairs={{0,1},{1,0},{2,3},{3,2},{4,5},{5,4},{6,7},{7,6},{8,9},{9,8},{10,11... | collective-permute-start | bytes 98312 | tf_op jit(solution)/shard_map/ppermute | solution.py:335
  49.2 4.4 %collective-permute-start.3 = (bf16[64,256]{1,0:T(8,128)(2,1)S(1)}, bf16[64,256]{1,0:T(8,128)(2,1)S(1)}, u32[]{:S(2)}, u32[]{:S(2)}) collective-permute-start(bf16[64,256]{1,0:T(8,128)(2,1)S(1)} %shard_map.229.own), channel_id=1, source_target_pairs={{0,4},{1,5},{2,6},{3,7},{4,0},{5,1},{6,2},{7,3},{8,12},{9,13},{10,... | collective-permute-start | bytes 98312 | tf_op jit(solution)/shard_map/ppermute | solution.py:337
  52.2 4.0 %collective-permute-start.2 = (bf16[64,256]{1,0:T(8,128)(2,1)S(1)}, bf16[64,256]{1,0:T(8,128)(2,1)S(1)}, u32[]{:S(2)}, u32[]{:S(2)}) collective-permute-start(bf16[64,256]{1,0:T(8,128)(2,1)S(1)} %shard_map.229.own), channel_id=1, source_target_pairs={{0,6},{1,7},{2,4},{3,5},{4,2},{5,3},{6,0},{7,1},{8,14},{9,15},{10,... | collective-permute-start | bytes 98312 | tf_op jit(solution)/shard_map/ppermute | solution.py:337
  52.9 3.2 %collective-permute-start.1 = (bf16[64,256]{1,0:T(8,128)(2,1)S(1)}, bf16[64,256]{1,0:T(8,128)(2,1)S(1)}, u32[]{:S(2)}, u32[]{:S(2)}) collective-permute-start(bf16[64,256]{1,0:T(8,128)(2,1)S(1)} %shard_map.229.own), channel_id=1, source_target_pairs={{0,2},{1,3},{2,0},{3,1},{4,6},{5,7},{6,4},{7,5},{8,10},{9,11},{10,... | collective-permute-start | bytes 98312 | tf_op jit(solution)/shard_map/ppermute | solution.py:337
  56.2 49.6 %copy-start.3 = (bf16[256,2048]{1,0:T(8,128)(2,1)S(1)}, bf16[256,2048]{1,0:T(8,128)(2,1)}, u32[]{:S(2)}) copy-start(bf16[256,2048]{1,0:T(8,128)(2,1)} %w_up.1) | copy-start | bytes 3145732
  56.2 49.6 %copy-start.12 = (f32[256]{0:T(256)S(1)}, f32[256]{0:T(256)}, u32[]{:S(2)}) copy-start(f32[256]{0:T(256)} %param.45) | copy-start | bytes 3076
  77.1 57.7 %copy-start.4 = (bf16[2048,256]{1,0:T(8,128)(2,1)S(1)}, bf16[2048,256]{1,0:T(8,128)(2,1)}, u32[]{:S(2)}) copy-start(bf16[2048,256]{1,0:T(8,128)(2,1)} %weight.5) | copy-start | bytes 3145732
  95.3 4.7 %collective-permute-start.4 = (bf16[64,256]{1,0:T(8,128)(2,1)S(1)}, bf16[64,256]{1,0:T(8,128)(2,1)S(1)}, u32[]{:S(2)}, u32[]{:S(2)}) collective-permute-start(bf16[64,256]{1,0:T(8,128)(2,1)S(1)} %shard_map.232.own), channel_id=1, source_target_pairs={{0,1},{1,0},{2,3},{3,2},{4,5},{5,4},{6,7},{7,6},{8,9},{9,8},{10,11... | collective-permute-start | bytes 98312 | tf_op jit(solution)/shard_map/ppermute | solution.py:335
  100.0 4.4 %collective-permute-start.7 = (bf16[64,256]{1,0:T(8,128)(2,1)S(1)}, bf16[64,256]{1,0:T(8,128)(2,1)S(1)}, u32[]{:S(2)}, u32[]{:S(2)}) collective-permute-start(bf16[64,256]{1,0:T(8,128)(2,1)S(1)} %shard_map.233.own), channel_id=1, source_target_pairs={{0,4},{1,5},{2,6},{3,7},{4,0},{5,1},{6,2},{7,3},{8,12},{9,13},{10,... | collective-permute-start | bytes 98312 | tf_op jit(solution)/shard_map/ppermute | solution.py:337
  101.8 4.0 %collective-permute-start.6 = (bf16[64,256]{1,0:T(8,128)(2,1)S(1)}, bf16[64,256]{1,0:T(8,128)(2,1)S(1)}, u32[]{:S(2)}, u32[]{:S(2)}) collective-permute-start(bf16[64,256]{1,0:T(8,128)(2,1)S(1)} %shard_map.233.own), channel_id=1, source_target_pairs={{0,6},{1,7},{2,4},{3,5},{4,2},{5,3},{6,0},{7,1},{8,14},{9,15},{10,... | collective-permute-start | bytes 98312 | tf_op jit(solution)/shard_map/ppermute | solution.py:337
  102.6 3.2 %collective-permute-start.5 = (bf16[64,256]{1,0:T(8,128)(2,1)S(1)}, bf16[64,256]{1,0:T(8,128)(2,1)S(1)}, u32[]{:S(2)}, u32[]{:S(2)}) collective-permute-start(bf16[64,256]{1,0:T(8,128)(2,1)S(1)} %shard_map.233.own), channel_id=1, source_target_pairs={{0,2},{1,3},{2,0},{3,1},{4,6},{5,7},{6,4},{7,5},{8,10},{9,11},{10,... | collective-permute-start | bytes 98312 | tf_op jit(solution)/shard_map/ppermute | solution.py:337
  135.2 5.3 %collective-permute-start.8 = (bf16[64,256]{1,0:T(8,128)(2,1)S(1)}, bf16[64,256]{1,0:T(8,128)(2,1)S(1)}, u32[]{:S(2)}, u32[]{:S(2)}) collective-permute-start(bf16[64,256]{1,0:T(8,128)(2,1)S(1)} %shard_map.236.own), channel_id=1, source_target_pairs={{0,1},{1,0},{2,3},{3,2},{4,5},{5,4},{6,7},{7,6},{8,9},{9,8},{10,11... | collective-permute-start | bytes 98312 | tf_op jit(solution)/shard_map/ppermute | solution.py:335
  140.6 4.4 %collective-permute-start.11 = (bf16[64,256]{1,0:T(8,128)(2,1)S(1)}, bf16[64,256]{1,0:T(8,128)(2,1)S(1)}, u32[]{:S(2)}, u32[]{:S(2)}) collective-permute-start(bf16[64,256]{1,0:T(8,128)(2,1)S(1)} %shard_map.237.own), channel_id=1, source_target_pairs={{0,4},{1,5},{2,6},{3,7},{4,0},{5,1},{6,2},{7,3},{8,12},{9,13},{10,... | collective-permute-start | bytes 98312 | tf_op jit(solution)/shard_map/ppermute | solution.py:337
  142.2 4.0 %collective-permute-start.10 = (bf16[64,256]{1,0:T(8,128)(2,1)S(1)}, bf16[64,256]{1,0:T(8,128)(2,1)S(1)}, u32[]{:S(2)}, u32[]{:S(2)}) collective-permute-start(bf16[64,256]{1,0:T(8,128)(2,1)S(1)} %shard_map.237.own), channel_id=1, source_target_pairs={{0,6},{1,7},{2,4},{3,5},{4,2},{5,3},{6,0},{7,1},{8,14},{9,15},{10,... | collective-permute-start | bytes 98312 | tf_op jit(solution)/shard_map/ppermute | solution.py:337
  143.3 2.9 %collective-permute-start.9 = (bf16[64,256]{1,0:T(8,128)(2,1)S(1)}, bf16[64,256]{1,0:T(8,128)(2,1)S(1)}, u32[]{:S(2)}, u32[]{:S(2)}) collective-permute-start(bf16[64,256]{1,0:T(8,128)(2,1)S(1)} %shard_map.237.own), channel_id=1, source_target_pairs={{0,2},{1,3},{2,0},{3,1},{4,6},{5,7},{6,4},{7,5},{8,10},{9,11},{10,... | collective-permute-start | bytes 98312 | tf_op jit(solution)/shard_map/ppermute | solution.py:337
  (4 other events, 190.0 us)
